TPU v7x, 128 devices: a whole 4x4x4 slice. The times are simulated.
128 devices in a mesh: clip: 16 (over y, z), band: 8 (over x, core).
Axes of the slice: x: 4, y: 4, z: 4, core: 2. Of those that a mesh axis runs over, the one named last changes fastest.
Arguments:
- encoded: bfloat16 [4, 4864, 768], P(None, ('clip', 'band')), may hold values from -6 to 6
- visible_pos: int32 [4, 4864], P(None, ('clip', 'band')), may hold values from 0 to 24575, as said below
- clip_len: int32 [4, 16, 3], P(None, 'clip'), may hold values from 0 to 192, as said below
- cotangent: bfloat16 [4, 16, 192, 8, 512], P(None, 'clip', 'band'), may hold values from -6 to 6
- embed_weight: bfloat16 [768, 512], replicated, may hold values from -0.21875 to 0.21875
- embed_bias: bfloat16 [512], replicated, may hold values from -1.75 to 1.75
- mask_token: bfloat16 [512], replicated, may hold values from -3 to 3
- attn_gain: bfloat16 [512], replicated, may hold values from 0.5 to 1.5
- attn_shift: bfloat16 [512], replicated, may hold values from -1.25 to 1.25
- qkv_weight: bfloat16 [512, 1536], replicated, may hold values from -0.25 to 0.25
- query_bias: bfloat16 [512], replicated, may hold values from -1.75 to 1.75
- value_bias: bfloat16 [512], replicated, may hold values from -1.75 to 1.75
- out_weight: bfloat16 [512, 512], replicated, may hold values from -1 to 1
- out_bias: bfloat16 [512], replicated, may hold values from -1.75 to 1.75
- mlp_gain: bfloat16 [512], replicated, may hold values from 0.5 to 1.5
- mlp_shift: bfloat16 [512], replicated, may hold values from -1.25 to 1.25
- up_weight: bfloat16 [512, 2048], replicated, may hold values from -0.25 to 0.25
- up_bias: bfloat16 [2048], replicated, may hold values from -1.75 to 1.75
- down_weight: bfloat16 [2048, 512], replicated, may hold values from -0.125 to 0.125
- down_bias: bfloat16 [512], replicated, may hold values from -1.75 to 1.75
Outputs:
- output: bfloat16 [4, 16, 192, 8, 512], P(None, 'clip', 'band')
- grad_encoded: bfloat16 [4, 4864, 768], P(None, ('clip', 'band'))
- grad_embed_weight: float32 [768, 512], replicated
- grad_embed_bias: float32 [512], replicated
- grad_mask_token: float32 [512], replicated
- grad_attn_gain: float32 [512], replicated
- grad_attn_shift: float32 [512], replicated
- grad_qkv_weight: float32 [512, 1536], replicated
- grad_query_bias: float32 [512], replicated
- grad_value_bias: float32 [512], replicated
- grad_out_weight: float32 [512, 512], replicated
- grad_out_bias: float32 [512], replicated
- grad_mlp_gain: float32 [512], replicated
- grad_mlp_shift: float32 [512], replicated
- grad_up_weight: float32 [512, 2048], replicated
- grad_up_bias: float32 [2048], replicated
- grad_down_weight: float32 [2048, 512], replicated
- grad_down_bias: float32 [512], replicated
Inputs may be any that keep to these rules, and one draw needn't show every extreme that they name: `visible_pos`: cells are distinct within a micro-batch. The patches on a device of band index b lie in time rows b * 24 to (b + 1) * 24 - 1 of their slots. Every device receives exactly 38 cells of its own rows; each device holds at most 9 patches for the slots of any one index of clip, and exactly 9 for one of them. `clip_len`: each slot holds one clip of 192 rows, given as (192, 0, 0), or three clips of 64 rows.
All inputs are finite; a program needn't handle non-finite values.
Results may differ from a plain program's by a relative error of at most 0.014.
Values may be sent and summed in bfloat16 or wider, within the bound.
No kernel may reach another device: no remote copies, remote signals or barrier semaphores. Data moves between devices by JAX's collectives and lax.ppermute only.
A program may use at most 192 MiB of HBM per device.

v0:
```python
import jax
import jax.numpy as jnp
from jax import lax
from jax.sharding import PartitionSpec as P

HEADS = 16
FREQ = 8
LONG = 192


epsilon = 1e-06


def extended(block, sides, width):
    for axis, dim in sides:
        count = lax.axis_size(axis)
        forward = [(i, i + 1) for i in range(count - 1)]
        backward = [(target, source) for source, target in forward]
        low = lax.ppermute(
            lax.slice_in_dim(block, block.shape[dim] - width, None, axis=dim), axis, forward
        )
        high = lax.ppermute(lax.slice_in_dim(block, 0, width, axis=dim), axis, backward)
        block = jnp.concatenate([low, block, high], axis=dim)
    return block


def layer_norm(values, gain, shift):
    center = values - jnp.mean(values, -1, keepdims=True)
    spread = jnp.mean(center * center, -1, keepdims=True)
    return center * lax.rsqrt(spread + epsilon) * gain + shift


def exact_gelu(values):
    return jax.nn.gelu(values, approximate=False)


def clip_ident(lengths, rows):
    first = lengths[:, 0:1]
    second = first + lengths[:, 1:2]
    ident = (rows[None, :] >= first).astype(jnp.int32) + (rows[None, :] >= second).astype(jnp.int32)
    start = jnp.where(ident >= 1, first, 0) + jnp.where(ident >= 2, lengths[:, 1:2], 0)
    inside = (rows >= 0) & (rows < LONG)
    return (jnp.where(inside[None, :], ident, -1), rows[None, :] - start)


def position_table(row_in_clip, width):
    quarter = width // 4
    omega = 1.0 / 10000.0 ** (jnp.arange(quarter, dtype=jnp.float32) / quarter)
    row_angle = row_in_clip.astype(jnp.float32)[..., None] * omega
    freq_angle = jnp.arange(FREQ, dtype=jnp.float32)[:, None] * omega
    row_part = jnp.concatenate([jnp.sin(row_angle), jnp.cos(row_angle)], -1)
    freq_part = jnp.concatenate([jnp.sin(freq_angle), jnp.cos(freq_angle)], -1)
    shape = row_in_clip.shape + (FREQ, width // 2)
    return jnp.concatenate(
        [jnp.broadcast_to(row_part[..., None, :], shape), jnp.broadcast_to(freq_part, shape)], -1
    )


def to_windows(tensor):
    slots, extent, freq, width = tensor.shape
    tensor = jnp.concatenate([tensor[:, :, 2:], tensor[:, :, :2]], 2)
    tensor = tensor.reshape(slots, extent // 4, 4, 2, 4, HEADS, width // HEADS)
    return tensor.transpose(0, 1, 3, 5, 2, 4, 6).reshape(
        slots, extent // 4, 2, HEADS, 16, width // HEADS
    )


def from_windows(tensor):
    slots, count, pairs, heads, tokens, size = tensor.shape
    tensor = tensor.reshape(slots, count, 2, heads, 4, 4, size).transpose(0, 1, 4, 2, 5, 3, 6)
    tensor = tensor.reshape(slots, count * 4, FREQ, heads * size)
    return jnp.concatenate([tensor[:, :, -2:], tensor[:, :, :-2]], 2)


def window_mask(ident):
    slots, extent = ident.shape
    tokens = jnp.repeat(ident.reshape(slots, extent // 4, 4), 4, axis=2)
    same = (tokens[..., :, None] == tokens[..., None, :]) & (tokens[..., None, :] >= 0)
    return same[:, :, None, None]


def scores_of(query_win, key_win, allowed, scale):
    raw = (
        jnp.einsum("swghqd,swghkd->swghqk", query_win, key_win, preferred_element_type=jnp.float32)
        * scale
    )
    return jnp.where(allowed, raw, -1e30)


def on_device(
    encoded,
    visible_pos,
    clip_len,
    cotangent,
    embed_weight,
    embed_bias,
    mask_token,
    attn_gain,
    attn_shift,
    qkv_weight,
    query_bias,
    value_bias,
    out_weight,
    out_bias,
    mlp_gain,
    mlp_shift,
    up_weight,
    up_bias,
    down_weight,
    down_bias,
):
    groups = lax.axis_size("clip")
    band_index = lax.axis_index("band")
    slot_dev = cotangent.shape[1]
    rows_dev = cotangent.shape[2]
    width = cotangent.shape[4]
    vis_dev = encoded.shape[1]
    capacity = 3 * ((vis_dev + groups - 1) // groups)
    cells = slot_dev * rows_dev * FREQ
    scale = (width // HEADS) ** (-0.5)
    embed_shift = embed_bias.astype(jnp.float32)
    mask_float = mask_token.astype(jnp.float32)
    gain_one = attn_gain.astype(jnp.float32)
    shift_one = attn_shift.astype(jnp.float32)
    gain_two = mlp_gain.astype(jnp.float32)
    shift_two = mlp_shift.astype(jnp.float32)
    qkv_shift = jnp.concatenate(
        [
            query_bias.astype(jnp.float32),
            jnp.zeros((width,), jnp.float32),
            value_bias.astype(jnp.float32),
        ]
    )
    out_shift = out_bias.astype(jnp.float32)
    up_shift = up_bias.astype(jnp.float32)
    down_shift = down_bias.astype(jnp.float32)
    own_rows = band_index * rows_dev + jnp.arange(rows_dev)
    ext_rows = band_index * rows_dev - 2 + jnp.arange(rows_dev + 4)
    pad_rows = ((0, 0), (2, 2), (0, 0), (0, 0))
    outputs = []
    grads_enc = []
    totals = None
    for index in range(encoded.shape[0]):
        enc_block = encoded[index]
        place_block = visible_pos[index]
        length_block = clip_len[index]
        cot_block = cotangent[index]
        proj = (
            jnp.dot(enc_block, embed_weight, preferred_element_type=jnp.float32) + embed_shift
        ).astype(jnp.bfloat16)
        slot_global = place_block // (LONG * FREQ)
        target = slot_global // slot_dev
        row_global = place_block // FREQ % LONG
        local_cell = (
            slot_global % slot_dev * rows_dev + row_global % rows_dev
        ) * FREQ + place_block % FREQ
        hits = (target[:, None] == jnp.arange(groups)[None, :]).astype(jnp.int32)
        rank = jnp.sum(jnp.cumsum(hits, 0) * hits, 1) - 1
        bucket = target * capacity + rank
        select = jnp.arange(groups * capacity)[:, None] == bucket[None, :]
        select_low = select.astype(jnp.bfloat16)
        packed = jnp.dot(select_low, proj, preferred_element_type=jnp.float32).astype(jnp.bfloat16)
        packed = packed.reshape(groups, capacity, width)
        places = jnp.sum(jnp.where(select, local_cell[None, :] + 1, 0), 1) - 1
        places = places.reshape(groups, capacity)
        got_tokens = lax.all_to_all(packed, "clip", split_axis=0, concat_axis=0, tiled=True)
        got_places = lax.all_to_all(places, "clip", split_axis=0, concat_axis=0, tiled=True)
        match = jnp.arange(cells)[:, None] == got_places.reshape(-1)[None, :]
        match_low = match.astype(jnp.bfloat16)
        filled = jnp.dot(
            match_low, got_tokens.reshape(-1, width), preferred_element_type=jnp.float32
        )
        seen = jnp.any(match, 1)
        unused, row_in_clip = clip_ident(length_block, own_rows)
        table = position_table(row_in_clip, width).reshape(cells, width)
        hidden = jnp.where(seen[:, None], filled, mask_float[None, :]) + table
        normed_one, pull_one = jax.vjp(layer_norm, hidden, gain_one, shift_one)
        normed_low = normed_one.astype(jnp.bfloat16)
        mixed = (
            jnp.dot(normed_low, qkv_weight, preferred_element_type=jnp.float32) + qkv_shift
        ).astype(jnp.bfloat16)
        mixed = mixed.reshape(slot_dev, rows_dev, FREQ, 3 * width)
        queries = mixed[..., :width]
        key_value = mixed[..., width:]
        ext_pairs = extended(key_value, (("band", 1),), 2)
        ident_ext, unused_rows = clip_ident(length_block, ext_rows)
        allowed = window_mask(ident_ext)
        query_win = to_windows(jnp.pad(queries, pad_rows))
        key_win = to_windows(ext_pairs[..., :width])
        value_win = to_windows(ext_pairs[..., width:])
        scores = scores_of(query_win, key_win, allowed, scale)
        row_peak = jnp.max(scores, -1, keepdims=True)
        row_total = jnp.sum(jnp.exp(scores - row_peak), -1, keepdims=True)
        log_total = row_peak + jnp.log(row_total)
        probs = jnp.exp(scores - log_total)
        attended = jnp.einsum(
            "swghqk,swghkd->swghqd",
            probs.astype(jnp.bfloat16),
            value_win,
            preferred_element_type=jnp.float32,
        )
        attended = from_windows(attended.astype(jnp.bfloat16))[:, 2 : 2 + rows_dev].reshape(
            cells, width
        )
        middle = (
            hidden + jnp.dot(attended, out_weight, preferred_element_type=jnp.float32) + out_shift
        )
        normed_two, pull_two = jax.vjp(layer_norm, middle, gain_two, shift_two)
        normed_two_low = normed_two.astype(jnp.bfloat16)
        expand = jnp.dot(normed_two_low, up_weight, preferred_element_type=jnp.float32) + up_shift
        activated, pull_gelu = jax.vjp(exact_gelu, expand)
        activated_low = activated.astype(jnp.bfloat16)
        result = (
            middle
            + jnp.dot(activated_low, down_weight, preferred_element_type=jnp.float32)
            + down_shift
        )
        output = result.astype(jnp.bfloat16).reshape(cot_block.shape)
        grad_result = cot_block.reshape(cells, width).astype(jnp.float32)
        grad_branch_two = cot_block.reshape(cells, width)
        grad_down_w = jnp.dot(activated_low.T, grad_branch_two, preferred_element_type=jnp.float32)
        grad_down_b = jnp.sum(grad_result, 0)
        grad_active = jnp.dot(grad_branch_two, down_weight.T, preferred_element_type=jnp.float32)
        (grad_expand,) = pull_gelu(grad_active)
        grad_expand_low = grad_expand.astype(jnp.bfloat16)
        grad_up_w = jnp.dot(normed_two_low.T, grad_expand_low, preferred_element_type=jnp.float32)
        grad_up_b = jnp.sum(grad_expand_low.astype(jnp.float32), 0)
        grad_normed_two = jnp.dot(grad_expand_low, up_weight.T, preferred_element_type=jnp.float32)
        grad_mid_part, grad_gain_two, grad_shift_two = pull_two(grad_normed_two)
        grad_middle = grad_result + grad_mid_part
        grad_branch_one = grad_middle.astype(jnp.bfloat16)
        grad_out_w = jnp.dot(attended.T, grad_branch_one, preferred_element_type=jnp.float32)
        grad_out_b = jnp.sum(grad_branch_one.astype(jnp.float32), 0)
        grad_attended = jnp.dot(grad_branch_one, out_weight.T, preferred_element_type=jnp.float32)
        grad_attended = grad_attended.astype(jnp.bfloat16).reshape(slot_dev, rows_dev, FREQ, width)
        grad_win = to_windows(jnp.pad(grad_attended, pad_rows))
        grad_probs = jnp.einsum(
            "swghqd,swghkd->swghqk", grad_win, value_win, preferred_element_type=jnp.float32
        )
        probs_again = jnp.exp(scores_of(query_win, key_win, allowed, scale) - log_total)
        inner = jnp.sum(probs_again * grad_probs, -1, keepdims=True)
        grad_scores = (probs_again * (grad_probs - inner)).astype(jnp.bfloat16)
        grad_query = (
            jnp.einsum(
                "swghqk,swghkd->swghqd", grad_scores, key_win, preferred_element_type=jnp.float32
            )
            * scale
        )
        grad_key = (
            jnp.einsum(
                "swghqk,swghqd->swghkd", grad_scores, query_win, preferred_element_type=jnp.float32
            )
            * scale
        )
        grad_value = jnp.einsum(
            "swghqk,swghqd->swghkd",
            probs_again.astype(jnp.bfloat16),
            grad_win,
            preferred_element_type=jnp.float32,
        )
        grad_query = from_windows(grad_query)[:, 2 : 2 + rows_dev]
        grad_pairs_ext = jnp.concatenate([from_windows(grad_key), from_windows(grad_value)], -1)
        rims = jnp.concatenate([grad_pairs_ext[:, :2], grad_pairs_ext[:, -2:]], 1)
        got_rims = extended(rims.astype(jnp.bfloat16), (("band", 1),), 2).astype(rims.dtype)
        lower_pad = ((0, 0), (0, rows_dev - 2), (0, 0), (0, 0))
        upper_pad = ((0, 0), (rows_dev - 2, 0), (0, 0), (0, 0))
        grad_pairs = (
            grad_pairs_ext[:, 2 : 2 + rows_dev]
            + jnp.pad(got_rims[:, :2], lower_pad)
            + jnp.pad(got_rims[:, -2:], upper_pad)
        )
        grad_mixed = (
            jnp.concatenate([grad_query, grad_pairs], -1)
            .reshape(cells, 3 * width)
            .astype(jnp.bfloat16)
        )
        grad_qkv_w = jnp.dot(normed_low.T, grad_mixed, preferred_element_type=jnp.float32)
        column_sums = jnp.sum(grad_mixed.astype(jnp.float32), 0)
        grad_query_b = column_sums[:width]
        grad_value_b = column_sums[2 * width :]
        grad_normed_one = jnp.dot(grad_mixed, qkv_weight.T, preferred_element_type=jnp.float32)
        grad_hid_part, grad_gain_one, grad_shift_one = pull_one(grad_normed_one)
        grad_hidden = grad_middle + grad_hid_part
        grad_mask = jnp.sum(jnp.where(seen[:, None], 0.0, grad_hidden), 0)
        grad_filled = grad_hidden.astype(jnp.bfloat16)
        returned = jnp.dot(match_low.T, grad_filled, preferred_element_type=jnp.float32).astype(
            jnp.bfloat16
        )
        came_back = lax.all_to_all(
            returned.reshape(groups, capacity, width),
            "clip",
            split_axis=0,
            concat_axis=0,
            tiled=True,
        )
        grad_proj = jnp.dot(
            select_low.T, came_back.reshape(-1, width), preferred_element_type=jnp.float32
        )
        grad_proj = grad_proj.astype(jnp.bfloat16)
        grad_embed_w = jnp.dot(enc_block.T, grad_proj, preferred_element_type=jnp.float32)
        grad_embed_b = jnp.sum(grad_proj.astype(jnp.float32), 0)
        grad_enc = jnp.dot(grad_proj, embed_weight.T, preferred_element_type=jnp.float32).astype(
            jnp.bfloat16
        )
        grads = (
            grad_embed_w,
            grad_embed_b,
            grad_mask,
            grad_gain_one,
            grad_shift_one,
            grad_qkv_w,
            grad_query_b,
            grad_value_b,
            grad_out_w,
            grad_out_b,
            grad_gain_two,
            grad_shift_two,
            grad_up_w,
            grad_up_b,
            grad_down_w,
            grad_down_b,
        )
        output, grad_enc, grads = (output, grad_enc, grads)
        if totals is None:
            totals = grads
        else:
            totals = tuple((earlier + later for earlier, later in zip(totals, grads)))
        outputs.append(output)
        grads_enc.append(grad_enc)
    totals = lax.psum(totals, ("clip", "band"))
    return (
        jnp.stack(outputs),
        jnp.stack(grads_enc),
        totals[0],
        totals[1],
        totals[2],
        totals[3],
        totals[4],
        totals[5],
        totals[6],
        totals[7],
        totals[8],
        totals[9],
        totals[10],
        totals[11],
        totals[12],
        totals[13],
        totals[14],
        totals[15],
    )


def solution(mesh):
    placed = (
        P(None, ("clip", "band"), None),
        P(None, ("clip", "band")),
        P(None, "clip", None),
        P(None, "clip", "band", None, None),
        P(),
        P(),
        P(),
        P(),
        P(),
        P(),
        P(),
        P(),
        P(),
        P(),
        P(),
        P(),
        P(),
        P(),
        P(),
        P(),
    )
    return jax.shard_map(
        on_device,
        mesh=mesh,
        in_specs=placed,
        out_specs=(
            P(None, "clip", "band", None, None),
            P(None, ("clip", "band"), None),
            P(),
            P(),
            P(),
            P(),
            P(),
            P(),
            P(),
            P(),
            P(),
            P(),
            P(),
            P(),
            P(),
            P(),
            P(),
            P(),
        ),
        check_vma=False,
    )
```

profile of v0, /device:TPU:1, one launch (start us, length us, event | category | flops | bytes accessed | tf_op | source)
XLA Modules:
  0.0 757.3 jit_solution(17510280268591273718)
XLA Ops:
  11.3 8.6 %all-to-all-start = ((s32[16,1,9]{2,1,0:T(1,128)}), s32[16,1,9]{2,1,0:T(1,128)}, u32[]{:S(2)}, u32[]{:S(2)}) async-start(s32[16,1,9]{2,1,0:T(1,128)} %bitcast.5), calls=%async_computation | async-start | bytes 16384 | tf_op jit(solution)/shard_map/all_to_all | solution.py:167
  49.2 2.6 fusion.242
  69.9 6.6 all-to-all-start.2
  84.8 6.7 all-to-all-start.4
  92.4 5.4 all-to-all-done.4
  97.8 3.5 all-to-all-start.6
  102.7 4.9 all-to-all-done.6
  107.6 3.5 all-to-all-start.1
  113.2 5.2 all-to-all-done.1
  118.4 3.5 all-to-all-start.3
  126.1 3.2 all-to-all-done.3
  129.2 3.5 all-to-all-start.5
  140.8 5.7 all-to-all-start.7
  161.7 10.6 %collective-permute-start = (bf16[1,2,8,1024]{3,2,1,0:T(8,128)(2,1)}, bf16[1,2,8,1024]{3,2,1,0:T(8,128)(2,1)S(1)}, u32[]{:S(2)}, u32[]{:S(2)}) collective-permute-start(bf16[1,2,8,1024]{3,2,1,0:T(8,128)(2,1)} %get-tuple-element.212), channel_id=1, source_target_pairs={{0,1},{1,2},{2,3},{3,4},{4,5},{5,6},{6,7},{8,9},{9,10},{10,11},{11... | collective-permute-start | bytes 98312 | tf_op jit(solution)/shard_map/ppermute | solution.py:19
  180.1 3.6 collective-permute-start.2
  189.1 2.6 copy.211
  197.5 3.6 collective-permute-start.4
  207.2 3.6 collective-permute-start.6
  253.7 5.5 multiply_convert_fusion.7
  259.1 5.4 multiply_convert_fusion.6
  281.9 2.7 reshape.2319
  287.5 5.4 multiply_convert_fusion.5
  310.1 3.1 reshape.2332
  316.1 4.9 multiply_convert_fusion.4
  333.3 2.6 multiply_reduce_fusion.7
  338.1 2.7 reshape.2368
  350.2 3.0 reshape.2373
  363.5 3.6 collective-permute-start.14
  374.7 3.0 add_add_fusion.1
  377.7 2.8 add_add_fusion
  393.0 3.0 reshape.2335
  405.3 3.0 reshape.2340
  428.4 3.1 reshape.2351
  458.6 3.6 collective-permute-start.8
  464.2 3.6 collective-permute-start.10
  469.8 3.6 collective-permute-start.12
  474.4 7.4 all-to-all-start.11
  513.1 2.7 convolution_add_fusion.2
  520.4 6.8 all-to-all-start.8
  528.4 7.9 %all-to-all-done.8 = bf16[16,9,512]{2,1,0:T(8,128)(2,1)S(1)} async-done(((bf16[16,9,512]{2,1,0:T(8,128)(2,1)}), bf16[16,9,512]{2,1,0:T(8,128)(2,1)S(1)}, u32[]{:S(2)}, u32[]{:S(2)}) %all-to-all-start.8) | async-done | bytes 147488 | tf_op jit(solution)/shard_map/all_to_all | solution.py:289
  536.3 3.5 all-to-all-start.9
  540.2 7.4 all-to-all-done.9
  547.6 3.8 all-to-all-start.10
  552.0 6.7 all-to-all-done.10
  572.9 65.4 %all-reduce.16 = (f32[512]{0:T(512)}, f32[512]{0:T(512)}, f32[512]{0:T(512)}, f32[512]{0:T(512)}, f32[512]{0:T(512)}, /*index=5*/f32[512]{0:T(512)}, f32[512]{0:...) all-reduce(f32[512]{0:T(512)S(1)} %add_add_fusion.26, ...), channel_id=1, replica_groups=mesh['clip'=16,'band'=8] {'clip','band'}, use_global_device_ids=true, to_apply=%region_65.66 | all-reduce | flops 7168 | bytes 57344 | tf_op jit(solution)/shard_map/psum | solution.py:330
  638.3 97.0 %all-reduce.20.cloned.1.call-done = (f32[768,512]{0,1:T(8,128)}, f32[512,1536]{1,0:T(8,128)}, f32[512,512]{1,0:T(8,128)}, f32[512,2048]{1,0:T(8,128)}, f32[2048,512]{1,0:T(8,128)}) async-done(((f32[768,512]{0,1:T(8,128)}, f32[512,1536]{1,0:T(8,128)}, f32[512,512]{1,0:T(8,128)}, f32[512,2048]{1,0:T(8,128)}, f32[2048,512]{1,0:T(8,128)}), (f32[768,512]{0,1:T(8,128)}, f32[512,1536]{1,0:T(8,128)}, ...) | async-done | bytes 14155792 | tf_op jit(solution)/shard_map/psum | solution.py:330
  735.3 3.0 copy.257
  738.3 3.9 copy.323
  (1050 shorter events, 365.8 us)
Async XLA Ops:
  7.2 246.4 %copy-start = (bf16[512,2048]{1,0:T(8,128)(2,1)S(1)}, bf16[512,2048]{1,0:T(8,128)(2,1)}, u32[]{:S(2)}) copy-start(bf16[512,2048]{1,0:T(8,128)(2,1)} %param.36) | copy-start | bytes 6291460
  7.2 28.1 %copy-start.294 = (bf16[512]{0:T(512)(128)(2,1)S(1)}, bf16[512]{0:T(512)(128)(2,1)}, u32[]{:S(2)}) copy-start(bf16[512]{0:T(512)(128)(2,1)} %param.25) | copy-start | bytes 3076
  7.2 28.2 %copy-start.14 = (bf16[768,512]{1,0:T(8,128)(2,1)S(1)}, bf16[768,512]{1,0:T(8,128)(2,1)}, u32[]{:S(2)}) copy-start(bf16[768,512]{1,0:T(8,128)(2,1)} %param.24) | copy-start | bytes 2359300
  10.5 26.1 %copy-start.261 = (s32[38]{0:T(128)}, s32[38]{0:T(128)S(1)}, u32[]{:S(2)}) copy-start(s32[38]{0:T(128)S(1)} %get-tuple-element.273) | copy-start | bytes 460
  10.5 31.7 %copy-start.259 = (s32[38]{0:T(128)}, s32[38]{0:T(128)S(1)}, u32[]{:S(2)}) copy-start(s32[38]{0:T(128)S(1)} %get-tuple-element.274) | copy-start | bytes 460
  10.5 32.3 %copy-start.257 = (s32[38]{0:T(128)}, s32[38]{0:T(128)S(1)}, u32[]{:S(2)}) copy-start(s32[38]{0:T(128)S(1)} %get-tuple-element.275) | copy-start | bytes 460
  11.3 58.6 %all-to-all-start = ((s32[16,1,9]{2,1,0:T(1,128)}), s32[16,1,9]{2,1,0:T(1,128)}, u32[]{:S(2)}, u32[]{:S(2)}) async-start(s32[16,1,9]{2,1,0:T(1,128)} %bitcast.5), calls=%async_computation | async-start | bytes 16384 | tf_op jit(solution)/shard_map/all_to_all | solution.py:167
  37.9 84.2 %copy-start.174 = (f32[512]{0:T(512)}, f32[512]{0:T(512)S(1)}, u32[]{:S(2)}) copy-start(f32[512]{0:T(512)S(1)} %convert_element_type.712) | copy-start | bytes 6148
  63.4 59.4 %copy-start.275 = (f32[1536]{0:T(1024)}, f32[1536]{0:T(1024)S(1)}, u32[]{:S(2)}) copy-start(f32[1536]{0:T(1024)S(1)} %pad_maximum_fusion.51) | copy-start | bytes 18436
  64.0 58.8 %copy-start.165 = (f32[512]{0:T(512)}, f32[512]{0:T(512)S(1)}, u32[]{:S(2)}) copy-start(f32[512]{0:T(512)S(1)} %convert_element_type.718) | copy-start | bytes 6148
  64.7 58.1 %copy-start.176 = (f32[512]{0:T(512)}, f32[512]{0:T(512)S(1)}, u32[]{:S(2)}) copy-start(f32[512]{0:T(512)S(1)} %convert_element_type.719) | copy-start | bytes 6148
  69.9 14.9 %all-to-all-start.2 = ((s32[16,1,9]{2,1,0:T(1,128)}), s32[16,1,9]{2,1,0:T(1,128)S(1)}, u32[]{:S(2)}, u32[]{:S(2)}) async-start(s32[16,1,9]{2,1,0:T(1,128)} %bitcast.29), calls=%async_computation.2 | async-start | bytes 16384 | tf_op jit(solution)/shard_map/all_to_all | solution.py:167
  84.8 38.0 %copy-start.207 = (s32[144]{0:T(256)}, s32[144]{0:T(256)S(1)}, u32[]{:S(2)}) copy-start(s32[144]{0:T(256)S(1)} %eq.273) | copy-start | bytes 1732
  84.8 13.0 %all-to-all-start.4 = ((s32[16,1,9]{2,1,0:T(1,128)}), s32[16,1,9]{2,1,0:T(1,128)S(1)}, u32[]{:S(2)}, u32[]{:S(2)}) async-start(s32[16,1,9]{2,1,0:T(1,128)} %bitcast.53), calls=%async_computation.4 | async-start | bytes 16384 | tf_op jit(solution)/shard_map/all_to_all | solution.py:167
  91.6 31.0 %copy-start.283 = (pred[192]{0:T(512)(128)(4,1)}, pred[192]{0:T(512)(128)(4,1)S(1)}, u32[]{:S(2)}) copy-start(pred[192]{0:T(512)(128)(4,1)S(1)} %fusion.155) | copy-start | bytes 580
  92.4 30.4 %copy-start.212 = (s32[144]{0:T(256)}, s32[144]{0:T(256)S(1)}, u32[]{:S(2)}) copy-start(s32[144]{0:T(256)S(1)} %eq.287) | copy-start | bytes 1732
  97.8 9.8 %all-to-all-start.6 = ((s32[16,1,9]{2,1,0:T(1,128)}), s32[16,1,9]{2,1,0:T(1,128)S(1)}, u32[]{:S(2)}, u32[]{:S(2)}) async-start(s32[16,1,9]{2,1,0:T(1,128)} %bitcast.77), calls=%async_computation.6 | async-start | bytes 16384 | tf_op jit(solution)/shard_map/all_to_all | solution.py:167
  107.6 10.8 %all-to-all-start.1 = ((bf16[16,9,512]{2,1,0:T(8,128)(2,1)}), bf16[16,9,512]{2,1,0:T(8,128)(2,1)S(1)}, u32[]{:S(2)}, u32[]{:S(2)}) async-start(bf16[16,9,512]{2,1,0:T(8,128)(2,1)} %reshape.2282), calls=%async_computation.1 | async-start | bytes 524288 | tf_op jit(solution)/shard_map/all_to_all | solution.py:166
  118.4 10.8 %all-to-all-start.3 = ((bf16[16,9,512]{2,1,0:T(8,128)(2,1)}), bf16[16,9,512]{2,1,0:T(8,128)(2,1)S(1)}, u32[]{:S(2)}, u32[]{:S(2)}) async-start(bf16[16,9,512]{2,1,0:T(8,128)(2,1)} %reshape.2295), calls=%async_computation.3 | async-start | bytes 524288 | tf_op jit(solution)/shard_map/all_to_all | solution.py:166
  122.5 105.4 %copy-start.26 = (f32[192,512]{1,0:T(8,128)}, f32[192,512]{1,0:T(8,128)S(1)}, u32[]{:S(2)}) copy-start(f32[192,512]{1,0:T(8,128)S(1)} %get-tuple-element.332) | copy-start | bytes 1179652
  129.2 10.8 %all-to-all-start.5 = ((bf16[16,9,512]{2,1,0:T(8,128)(2,1)}), bf16[16,9,512]{2,1,0:T(8,128)(2,1)S(1)}, u32[]{:S(2)}, u32[]{:S(2)}) async-start(bf16[16,9,512]{2,1,0:T(8,128)(2,1)} %reshape.2308), calls=%async_computation.5 | async-start | bytes 524288 | tf_op jit(solution)/shard_map/all_to_all | solution.py:166
  140.8 14.3 %all-to-all-start.7 = ((bf16[16,9,512]{2,1,0:T(8,128)(2,1)}), bf16[16,9,512]{2,1,0:T(8,128)(2,1)S(1)}, u32[]{:S(2)}, u32[]{:S(2)}) async-start(bf16[16,9,512]{2,1,0:T(8,128)(2,1)} %reshape.2321), calls=%async_computation.7 | async-start | bytes 524288 | tf_op jit(solution)/shard_map/all_to_all | solution.py:166
  161.7 43.5 %collective-permute-start = (bf16[1,2,8,1024]{3,2,1,0:T(8,128)(2,1)}, bf16[1,2,8,1024]{3,2,1,0:T(8,128)(2,1)S(1)}, u32[]{:S(2)}, u32[]{:S(2)}) collective-permute-start(bf16[1,2,8,1024]{3,2,1,0:T(8,128)(2,1)} %get-tuple-element.212), channel_id=1, source_target_pairs={{0,1},{1,2},{2,3},{3,4},{4,5},{5,6},{6,7},{8,9},{9,10},{10,11},{11... | collective-permute-start | bytes 98312 | tf_op jit(solution)/shard_map/ppermute | solution.py:19
  172.3 34.8 %collective-permute-start.1 = (bf16[1,2,8,1024]{3,2,1,0:T(8,128)(2,1)}, bf16[1,2,8,1024]{3,2,1,0:T(8,128)(2,1)}, u32[]{:S(2)}, u32[]{:S(2)}) collective-permute-start(bf16[1,2,8,1024]{3,2,1,0:T(8,128)(2,1)} %get-tuple-element.213), channel_id=1, source_target_pairs={{1,0},{2,1},{3,2},{4,3},{5,4},{6,5},{7,6},{9,8},{10,9},{11,10},{12... | collective-permute-start | bytes 98312 | tf_op jit(solution)/shard_map/ppermute | solution.py:22
  180.1 50.0 %collective-permute-start.2 = (bf16[1,2,8,1024]{3,2,1,0:T(8,128)(2,1)}, bf16[1,2,8,1024]{3,2,1,0:T(8,128)(2,1)S(1)}, u32[]{:S(2)}, u32[]{:S(2)}) collective-permute-start(bf16[1,2,8,1024]{3,2,1,0:T(8,128)(2,1)} %get-tuple-element.214), channel_id=1, source_target_pairs={{0,1},{1,2},{2,3},{3,4},{4,5},{5,6},{6,7},{8,9},{9,10},{10,11},{11... | collective-permute-start | bytes 98312 | tf_op jit(solution)/shard_map/ppermute | solution.py:19
  183.7 48.7 %collective-permute-start.3 = (bf16[1,2,8,1024]{3,2,1,0:T(8,128)(2,1)}, bf16[1,2,8,1024]{3,2,1,0:T(8,128)(2,1)}, u32[]{:S(2)}, u32[]{:S(2)}) collective-permute-start(bf16[1,2,8,1024]{3,2,1,0:T(8,128)(2,1)} %get-tuple-element.215), channel_id=1, source_target_pairs={{1,0},{2,1},{3,2},{4,3},{5,4},{6,5},{7,6},{9,8},{10,9},{11,10},{12... | collective-permute-start | bytes 98312 | tf_op jit(solution)/shard_map/ppermute | solution.py:22
  197.5 67.0 %collective-permute-start.4 = (bf16[1,2,8,1024]{3,2,1,0:T(8,128)(2,1)}, bf16[1,2,8,1024]{3,2,1,0:T(8,128)(2,1)}, u32[]{:S(2)}, u32[]{:S(2)}) collective-permute-start(bf16[1,2,8,1024]{3,2,1,0:T(8,128)(2,1)} %get-tuple-element.216), channel_id=1, source_target_pairs={{0,1},{1,2},{2,3},{3,4},{4,5},{5,6},{6,7},{8,9},{9,10},{10,11},{11... | collective-permute-start | bytes 98312 | tf_op jit(solution)/shard_map/ppermute | solution.py:19
  205.2 59.3 %collective-permute-start.5 = (bf16[1,2,8,1024]{3,2,1,0:T(8,128)(2,1)}, bf16[1,2,8,1024]{3,2,1,0:T(8,128)(2,1)}, u32[]{:S(2)}, u32[]{:S(2)}) collective-permute-start(bf16[1,2,8,1024]{3,2,1,0:T(8,128)(2,1)} %get-tuple-element.217), channel_id=1, source_target_pairs={{1,0},{2,1},{3,2},{4,3},{5,4},{6,5},{7,6},{9,8},{10,9},{11,10},{12... | collective-permute-start | bytes 98312 | tf_op jit(solution)/shard_map/ppermute | solution.py:22
  207.2 85.7 %collective-permute-start.6 = (bf16[1,2,8,1024]{3,2,1,0:T(8,128)(2,1)}, bf16[1,2,8,1024]{3,2,1,0:T(8,128)(2,1)}, u32[]{:S(2)}, u32[]{:S(2)}) collective-permute-start(bf16[1,2,8,1024]{3,2,1,0:T(8,128)(2,1)} %get-tuple-element.218), channel_id=1, source_target_pairs={{0,1},{1,2},{2,3},{3,4},{4,5},{5,6},{6,7},{8,9},{9,10},{10,11},{11... | collective-permute-start | bytes 98312 | tf_op jit(solution)/shard_map/ppermute | solution.py:19
  230.0 62.9 %collective-permute-start.7 = (bf16[1,2,8,1024]{3,2,1,0:T(8,128)(2,1)}, bf16[1,2,8,1024]{3,2,1,0:T(8,128)(2,1)}, u32[]{:S(2)}, u32[]{:S(2)}) collective-permute-start(bf16[1,2,8,1024]{3,2,1,0:T(8,128)(2,1)} %get-tuple-element.219), channel_id=1, source_target_pairs={{1,0},{2,1},{3,2},{4,3},{5,4},{6,5},{7,6},{9,8},{10,9},{11,10},{12... | collective-permute-start | bytes 98312 | tf_op jit(solution)/shard_map/ppermute | solution.py:22
  363.5 21.4 %collective-permute-start.14 = (bf16[1,2,8,1024]{3,2,1,0:T(8,128)(2,1)}, bf16[1,2,8,1024]{3,2,1,0:T(8,128)(2,1)}, u32[]{:S(2)}, u32[]{:S(2)}) collective-permute-start(bf16[1,2,8,1024]{3,2,1,0:T(8,128)(2,1)} %get-tuple-element.200), channel_id=1, source_target_pairs={{0,1},{1,2},{2,3},{3,4},{4,5},{5,6},{6,7},{8,9},{9,10},{10,11},{11... | collective-permute-start | bytes 98312 | tf_op jit(solution)/shard_map/ppermute | solution.py:19
  367.1 17.7 %collective-permute-start.15 = (bf16[1,2,8,1024]{3,2,1,0:T(8,128)(2,1)}, bf16[1,2,8,1024]{3,2,1,0:T(8,128)(2,1)}, u32[]{:S(2)}, u32[]{:S(2)}) collective-permute-start(bf16[1,2,8,1024]{3,2,1,0:T(8,128)(2,1)} %get-tuple-element.201), channel_id=1, source_target_pairs={{1,0},{2,1},{3,2},{4,3},{5,4},{6,5},{7,6},{9,8},{10,9},{11,10},{12... | collective-permute-start | bytes 98312 | tf_op jit(solution)/shard_map/ppermute | solution.py:22
  391.5 23.8 %copy-start.125 = (bf16[192,512]{1,0:T(8,128)(2,1)}, bf16[192,512]{1,0:T(8,128)(2,1)S(1)}, u32[]{:S(2)}) copy-start(bf16[192,512]{1,0:T(8,128)(2,1)S(1)} %get-tuple-element.209) | copy-start | bytes 589828
  458.2 23.6 %copy-start.116 = (bf16[1,28,8,512]{3,2,1,0:T(8,128)(2,1)S(1)}, bf16[1,28,8,512]{3,2,1,0:T(8,128)(2,1)}, u32[]{:S(2)}) copy-start(bf16[1,28,8,512]{3,2,1,0:T(8,128)(2,1)} %copy-done.115) | copy-start | bytes 688132
  458.6 43.1 %collective-permute-start.8 = (bf16[1,2,8,1024]{3,2,1,0:T(8,128)(2,1)}, bf16[1,2,8,1024]{3,2,1,0:T(8,128)(2,1)}, u32[]{:S(2)}, u32[]{:S(2)}) collective-permute-start(bf16[1,2,8,1024]{3,2,1,0:T(8,128)(2,1)} %get-tuple-element.194), channel_id=1, source_target_pairs={{0,1},{1,2},{2,3},{3,4},{4,5},{5,6},{6,7},{8,9},{9,10},{10,11},{11... | collective-permute-start | bytes 98312 | tf_op jit(solution)/shard_map/ppermute | solution.py:19
  462.2 39.5 %collective-permute-start.9 = (bf16[1,2,8,1024]{3,2,1,0:T(8,128)(2,1)}, bf16[1,2,8,1024]{3,2,1,0:T(8,128)(2,1)}, u32[]{:S(2)}, u32[]{:S(2)}) collective-permute-start(bf16[1,2,8,1024]{3,2,1,0:T(8,128)(2,1)} %get-tuple-element.195), channel_id=1, source_target_pairs={{1,0},{2,1},{3,2},{4,3},{5,4},{6,5},{7,6},{9,8},{10,9},{11,10},{12... | collective-permute-start | bytes 98312 | tf_op jit(solution)/shard_map/ppermute | solution.py:22
  464.2 29.8 %collective-permute-start.10 = (bf16[1,2,8,1024]{3,2,1,0:T(8,128)(2,1)}, bf16[1,2,8,1024]{3,2,1,0:T(8,128)(2,1)}, u32[]{:S(2)}, u32[]{:S(2)}) collective-permute-start(bf16[1,2,8,1024]{3,2,1,0:T(8,128)(2,1)} %get-tuple-element.196), channel_id=1, source_target_pairs={{0,1},{1,2},{2,3},{3,4},{4,5},{5,6},{6,7},{8,9},{9,10},{10,11},{11... | collective-permute-start | bytes 98312 | tf_op jit(solution)/shard_map/ppermute | solution.py:19
  467.8 28.2 %collective-permute-start.11 = (bf16[1,2,8,1024]{3,2,1,0:T(8,128)(2,1)}, bf16[1,2,8,1024]{3,2,1,0:T(8,128)(2,1)}, u32[]{:S(2)}, u32[]{:S(2)}) collective-permute-start(bf16[1,2,8,1024]{3,2,1,0:T(8,128)(2,1)} %get-tuple-element.197), channel_id=1, source_target_pairs={{1,0},{2,1},{3,2},{4,3},{5,4},{6,5},{7,6},{9,8},{10,9},{11,10},{12... | collective-permute-start | bytes 98312 | tf_op jit(solution)/shard_map/ppermute | solution.py:22
  469.8 30.1 %collective-permute-start.12 = (bf16[1,2,8,1024]{3,2,1,0:T(8,128)(2,1)}, bf16[1,2,8,1024]{3,2,1,0:T(8,128)(2,1)}, u32[]{:S(2)}, u32[]{:S(2)}) collective-permute-start(bf16[1,2,8,1024]{3,2,1,0:T(8,128)(2,1)} %get-tuple-element.198), channel_id=1, source_target_pairs={{0,1},{1,2},{2,3},{3,4},{4,5},{5,6},{6,7},{8,9},{9,10},{10,11},{11... | collective-permute-start | bytes 98312 | tf_op jit(solution)/shard_map/ppermute | solution.py:19
  474.4 45.9 %all-to-all-start.11 = ((bf16[16,9,512]{2,1,0:T(8,128)(2,1)}), bf16[16,9,512]{2,1,0:T(8,128)(2,1)}, u32[]{:S(2)}, u32[]{:S(2)}) async-start(bf16[16,9,512]{2,1,0:T(8,128)(2,1)} %reshape.2376), calls=%async_computation.11 | async-start | bytes 524288 | tf_op jit(solution)/shard_map/all_to_all | solution.py:289
  494.0 5.9 collective-permute-start.13
  520.4 31.4 %copy-start.260 = (s32[38]{0:T(128)S(1)}, s32[38]{0:T(128)}, u32[]{:S(2)}) copy-start(s32[38]{0:T(128)} %copy-done.259) | copy-start | bytes 460
  520.4 16.0 %all-to-all-start.8 = ((bf16[16,9,512]{2,1,0:T(8,128)(2,1)}), bf16[16,9,512]{2,1,0:T(8,128)(2,1)S(1)}, u32[]{:S(2)}, u32[]{:S(2)}) async-start(bf16[16,9,512]{2,1,0:T(8,128)(2,1)} %reshape.2343), calls=%async_computation.8 | async-start | bytes 524288 | tf_op jit(solution)/shard_map/all_to_all | solution.py:289
  527.2 31.6 %copy-start.258 = (s32[38]{0:T(128)S(1)}, s32[38]{0:T(128)}, u32[]{:S(2)}) copy-start(s32[38]{0:T(128)} %copy-done.257) | copy-start | bytes 460
  528.2 30.8 %copy-start.157 = (bf16[1,38,768]{2,0,1:T(2,128)(2,1)S(1)}, bf16[1,38,768]{2,0,1:T(2,128)(2,1)}, u32[]{:S(2)}) copy-start(bf16[1,38,768]{2,0,1:T(2,128)(2,1)} %copy-done.156) | copy-start | bytes 175108
  536.3 11.2 %all-to-all-start.9 = ((bf16[16,9,512]{2,1,0:T(8,128)(2,1)}), bf16[16,9,512]{2,1,0:T(8,128)(2,1)S(1)}, u32[]{:S(2)}, u32[]{:S(2)}) async-start(bf16[16,9,512]{2,1,0:T(8,128)(2,1)} %reshape.2354), calls=%async_computation.9 | async-start | bytes 524288 | tf_op jit(solution)/shard_map/all_to_all | solution.py:289
  547.6 11.1 %all-to-all-start.10 = ((bf16[16,9,512]{2,1,0:T(8,128)(2,1)}), bf16[16,9,512]{2,1,0:T(8,128)(2,1)S(1)}, u32[]{:S(2)}, u32[]{:S(2)}) async-start(bf16[16,9,512]{2,1,0:T(8,128)(2,1)} %reshape.2365), calls=%async_computation.10 | async-start | bytes 524288 | tf_op jit(solution)/shard_map/all_to_all | solution.py:289
  551.4 183.9 %all-reduce.20.cloned.1.call-start = ((), (), s32[]{:S(2)}) async-start(), calls=%async_computation.12 | async-start | bytes 28311552 | tf_op jit(solution)/shard_map/psum | solution.py:330
  (283 other events, 1011.0 us)
Sparse Core Ops, SparseCore 0:
  562.1 173.1 all-reduce.19
where the time goes:
time: 772 us; the launch traced here: 757 us
  local copies, waits for them, and re-layouts  206 us (27%)
  waiting for transfers between devices  139 us (18%)
  matrix products  117 us (15%)
  starting transfers between devices  116 us (15%)
  other arithmetic  90.9 us (12%)
  blocking collectives  65.4 us (8%)
  between operations  24.3 us (3%)
    psum x1, waiting for transfers between devices, on_device(): totals = lax.psum(totals, ('clip', 'band'))  97 us
    reshape x32, local copies, waits for them, and re-layouts, to_windows(): tensor = tensor.reshape(slots, extent // 4, 4, 2, 4, HEADS, width // HEADS)  66.4 us
    psum x1, blocking collectives, on_device(): totals = lax.psum(totals, ('clip', 'band'))  65.4 us
    unnamed x610, local copies, waits for them, and re-layouts  38.8 us
    ppermute x8, starting transfers between devices, extended(): lax.ppermute(lax.slice_in_dim(block, block.shape[dim] - width, None, axis...  36.1 us
    reshape x16, local copies, waits for them, and re-layouts, from_windows(): tensor = tensor.reshape(slots, count * 4, FREQ, heads * size)  34.9 us
    all_to_all x4, starting transfers between devices, on_device(): lax.all_to_all(places, 'clip', split_axis=0, concat_axis=0, tiled=True)  25.4 us
    all_to_all x4, waiting for transfers between devices, on_device(): lax.all_to_all(returned.reshape(groups, capacity, width), 'clip', split_a...  22 us
  transfers between devices with their start and end apart: 29, of which 9 were waited for; matrix products, arithmetic and copies ran while one was open for 30% of the time, Pallas kernels for 0%

commit v1 on v0

v1 whole, which is shorter than its diff:
```python
import jax
import jax.numpy as jnp
import numpy as np
from jax import lax
from jax.experimental import pallas as pl
from jax.experimental.pallas import tpu as pltpu
from jax.sharding import PartitionSpec as P

HEADS = 16
FREQ = 8
LONG = 192
MICRO = 4
ROWS = 24
CELLS = ROWS * FREQ
ALL = MICRO * CELLS
EXT = CELLS + 32
TOK = 48
CAP = 9
BLK = 40
SRC = 16
GOT = SRC * BLK
D = 512
FF = 2048
ENC = 768
CHUNK = 128
CHUNKS = MICRO * EXT // CHUNK
EPS = 1e-06
SCALE = (D // HEADS) ** (-0.5)
F32 = jnp.float32
BF16 = jnp.bfloat16

NN = (((1,), (0,)), ((), ()))
NT = (((1,), (1,)), ((), ()))
TN = (((0,), (0,)), ((), ()))


def dot(left, right, dims=NN):
    return lax.dot_general(left, right, dims, preferred_element_type=F32)


def iota(shape, dim):
    return lax.broadcasted_iota(jnp.int32, shape, dim)


def one_hot(hit):
    return jnp.where(hit, 1.0, 0.0).astype(BF16)


def call(kernel, name, out_shape, args, scratch=(), smem=0, flops=0):
    specs = [pl.BlockSpec(memory_space=pltpu.SMEM)] * smem
    specs += [pl.BlockSpec(memory_space=pltpu.VMEM)] * (len(args) - smem)
    outs = [jax.ShapeDtypeStruct(shape, dtype) for shape, dtype in out_shape]
    size = sum(a.size * a.dtype.itemsize for a in args) + sum(
        o.size * o.dtype.itemsize for o in outs
    )
    return pl.pallas_call(
        kernel,
        name=name,
        out_shape=outs,
        in_specs=specs,
        out_specs=[pl.BlockSpec(memory_space=pltpu.VMEM)] * len(outs),
        scratch_shapes=list(scratch),
        compiler_params=pltpu.CompilerParams(vmem_limit_bytes=56 * 2**20),
        cost_estimate=pl.CostEstimate(flops=flops, bytes_accessed=size, transcendentals=0),
    )(*args)


def pack_kernel(row, col, enc, out, dest):
    count = MICRO * TOK
    key_r, key_c = row[1:2, :], col[:, 1:2]
    same = key_c == key_r
    low = iota((count, count), 0)
    high = iota((count, count), 1)
    rank_r = jnp.sum(jnp.where(same & (low < high), 1, 0), axis=0, keepdims=True)
    rank_c = jnp.sum(jnp.where(same & (high < low), 1, 0), axis=1, keepdims=True)
    place_r = row[2:3, :] * CAP + rank_r
    place_c = col[:, 2:3] * CAP + rank_c
    dest_r = row[0:1, :] * BLK + place_r
    dest[...] = col[:, 0:1] * BLK + place_c
    select = one_hot(iota((GOT, count), 0) == dest_r)
    to_dev = jnp.where(
        iota((SRC, count), 0) == row[0:1, :], row[3:4, :].astype(F32), 0.0
    ).astype(BF16)
    to_lane = one_hot(iota((count, ENC), 1) == place_c)
    places = dot(to_dev, to_lane).astype(BF16)
    spread = one_hot(iota((GOT, SRC), 0) == iota((GOT, SRC), 1) * BLK + (BLK - 4))
    out[...] = (dot(select, enc[...]) + dot(spread, places)).astype(BF16)


def norm_parts(values):
    center = values - jnp.mean(values, -1, keepdims=True)
    inverse = lax.rsqrt(jnp.mean(center * center, -1, keepdims=True) + EPS)
    return center * inverse, inverse


def norm_back(grad, normal, inverse, gain):
    scaled = grad * gain
    return inverse * (
        scaled
        - jnp.mean(scaled, -1, keepdims=True)
        - normal * jnp.mean(scaled * normal, -1, keepdims=True)
    )


def enter_kernel(
    idx_r, idx_c, got, table, embed_w, qkv_w, vecs, qkv_b,
    hidden_o, normed_o, mixed_o, filled_o, seen_o, cell_o, low_o, high_o,
):
    hit = one_hot(iota((SRC, GOT), 1) == iota((SRC, GOT), 0) * BLK + (BLK - 4))
    numbers = dot(hit, got[:, :128]).astype(BF16)
    spread_r = dot(numbers, one_hot(iota((SRC, GOT), 0) == idx_r[0:1, :]), TN)
    value_r = jnp.sum(
        jnp.where(iota((128, GOT), 0) == idx_r[1:2, :], spread_r, 0.0), axis=0, keepdims=True
    )
    cell_r = jnp.where(
        value_r > 0.5, idx_r[2:3, :] * CELLS + value_r.astype(jnp.int32) - 1, -1
    )
    spread_c = dot(one_hot(iota((GOT, SRC), 1) == idx_c[:, 0:1]), numbers)
    value_c = jnp.sum(
        jnp.where(iota((GOT, 128), 1) == idx_c[:, 1:2], spread_c, 0.0), axis=1, keepdims=True
    )
    cell_o[...] = jnp.where(
        value_c > 0.5, idx_c[:, 2:3] * CELLS + value_c.astype(jnp.int32) - 1, -1
    )
    for m in range(MICRO):
        rows = slice(m * CELLS, (m + 1) * CELLS)
        match = jnp.where(iota((CELLS, GOT), 0) + m * CELLS == cell_r, 1.0, 0.0)
        seen = jnp.sum(match, axis=1, keepdims=True)
        filled = dot(match.astype(BF16), got[...]).astype(BF16)
        filled_o[rows, :] = filled
        seen_o[rows, :] = seen
        proj = (dot(filled, embed_w[...]) + vecs[0:1, :]).astype(BF16).astype(F32)
        hidden = jnp.where(seen > 0.5, proj, vecs[1:2, :]) + table[rows, :]
        hidden_o[rows, :] = hidden
        normal, unused = norm_parts(hidden)
        normed = (normal * vecs[2:3, :] + vecs[3:4, :]).astype(BF16)
        normed_o[rows, :] = normed
        mixed = (dot(normed, qkv_w[...]) + qkv_b[...]).astype(BF16)
        mixed_o[rows, :] = mixed
        low_o[m] = mixed[:16, D:]
        high_o[m] = mixed[CELLS - 16 :, D:]


def spread_rows(source, column, width, low, high, target):
    for m in range(MICRO):
        base = m * EXT
        if low is None:
            target[base : base + 16, :] = jnp.zeros((16, width), BF16)
            target[base + 16 + CELLS : base + EXT, :] = jnp.zeros((16, width), BF16)
        else:
            target[base : base + 16, :] = low[m, :, column - D : column - D + width]
            target[base + 16 + CELLS : base + EXT, :] = high[m, :, column - D : column - D + width]
        target[base + 16 : base + 16 + CELLS, :] = source[
            m * CELLS : (m + 1) * CELLS, column : column + width
        ]


def expand_lanes(packed, lanes):
    return jnp.concatenate([packed * lanes[w : w + 1, :] for w in range(4)], axis=0)


def compress(full, lanes):
    out = full[0:32, :] * lanes[0:1, :]
    for w in range(1, 4):
        out = out + full[32 * w : 32 * w + 32, :] * lanes[w : w + 1, :]
    return out


def attend_kernel(
    mixed, low, high, mask, lanes, lanes32, head_mask, attended_o, probs_o, q_s, k_s, v_s, a_s
):
    spread_rows(mixed, 0, D, None, None, q_s)
    spread_rows(mixed, D, D, low, high, k_s)
    spread_rows(mixed, 2 * D, D, low, high, v_s)
    lane_low = lanes[...]
    lane_f = lanes32[...]

    def step(c, carry):
        rows = pl.ds(pl.multiple_of(c * CHUNK, CHUNK), CHUNK)
        allowed = mask[c] > 0.5
        allowed = jnp.concatenate([allowed, allowed], axis=1)
        for j in range(2):
            cols = slice(256 * j, 256 * j + 256)
            q = q_s[rows, cols]
            k = k_s[rows, cols]
            v_t = jnp.transpose(v_s[rows, cols])
            parts = []
            for pair in range(4):
                q_m = jnp.concatenate(
                    [q * head_mask[2 * pair + i : 2 * pair + i + 1, :] for i in range(2)], axis=0
                )
                scores = compress(dot(k, q_m, NT), lane_f) * SCALE
                scores = jnp.where(allowed, scores, -1e30)
                grown = jnp.exp(scores - jnp.max(scores, axis=0, keepdims=True))
                probs = grown / jnp.sum(grown, axis=0, keepdims=True)
                start = (8 * j + 2 * pair) * CHUNK
                probs_o[c, :, start : start + 256] = probs
                full = expand_lanes(probs.astype(BF16), lane_low)
                for i in range(2):
                    h = 2 * pair + i
                    parts.append(
                        dot(v_t[32 * h : 32 * h + 32, :], full[:, CHUNK * i : CHUNK * i + CHUNK])
                    )
            out_t = jnp.concatenate(parts, axis=0).astype(BF16)
            a_s[rows, cols] = jnp.transpose(out_t)
        return carry

    lax.fori_loop(0, CHUNKS, step, 0)
    for m in range(MICRO):
        attended_o[m * CELLS : (m + 1) * CELLS, :] = a_s[m * EXT + 16 : m * EXT + 16 + CELLS, :]


def gelu_parts(x):
    size = jnp.abs(x) * (0.5**0.5)
    bell = jnp.exp(-0.5 * x * x)
    t = 1.0 / (1.0 + 0.3275911 * size)
    poly = t * (
        0.254829592
        + t * (-0.284496736 + t * (1.421413741 + t * (-1.453152027 + t * 1.061405429)))
    )
    tail = 0.5 * poly * bell
    share = jnp.where(x >= 0, 1.0 - tail, tail)
    return x * share, share + x * bell * 0.3989422804014327


def mlp_kernel(
    core, hidden, attended, cot, out_w, up_w, down_w, vecs, up_b,
    output_o, gmid_o, gatt_o, grads_o, gout_o, sums_o, act_s, gexp_s, n2_s, gb_s, n2t_s,
):
    tile = 256
    sums_o[...] = jnp.zeros((8, D), F32)

    def forward(i, carry):
        rows = pl.ds(pl.multiple_of(i * tile, tile), tile)
        middle = hidden[rows, :] + dot(attended[rows, :], out_w[...]) + vecs[0:1, :]
        normal, inverse = norm_parts(middle)
        normed = (normal * vecs[1:2, :] + vecs[2:3, :]).astype(BF16)
        n2_s[rows, :] = normed
        g = cot[rows, :]
        result = middle + vecs[3:4, :]
        grad = jnp.zeros((tile, D), F32)
        for f in range(4):
            cols = slice(512 * f, 512 * f + 512)
            expand = dot(normed, up_w[:, cols]) + up_b[0:1, cols]
            value, slope = gelu_parts(expand)
            act = value.astype(BF16)
            act_s[rows, cols] = act
            result = result + dot(act, down_w[cols, :])
            g_exp = (dot(g, down_w[cols, :], NT) * slope).astype(BF16)
            gexp_s[rows, cols] = g_exp
            sums_o[4 + f : 5 + f, :] += jnp.sum(g_exp.astype(F32), axis=0, keepdims=True)
            grad = grad + dot(g_exp, up_w[:, cols], NT)
        output_o[rows, :] = result.astype(BF16)
        g_float = g.astype(F32)
        g_mid = g_float + norm_back(grad, normal, inverse, vecs[1:2, :])
        gmid_o[rows, :] = g_mid
        g_low = g_mid.astype(BF16)
        gb_s[rows, :] = g_low
        gatt_o[rows, :] = dot(g_low, out_w[...], NT).astype(BF16)
        sums_o[0:1, :] += jnp.sum(g_low.astype(F32), axis=0, keepdims=True)
        sums_o[1:2, :] += jnp.sum(grad * normal, axis=0, keepdims=True)
        sums_o[2:3, :] += jnp.sum(grad, axis=0, keepdims=True)
        sums_o[3:4, :] += jnp.sum(g_float, axis=0, keepdims=True)
        return carry

    lax.fori_loop(0, ALL // tile, forward, 0)
    n2t_s[...] = jnp.transpose(n2_s[...])

    def weights(f, carry):
        cols = pl.ds(pl.multiple_of(f * 512, 512), 512)
        half = f // 2
        slot = jnp.where(half == core[0], 0, 1)
        place = pl.multiple_of((f % 2) * 512, 512)
        grads_o[slot, pl.ds(place, 512), :] = dot(act_s[:, cols], cot[...], TN).astype(BF16)
        grads_o[slot, pl.ds(1024 + place, 512), :] = dot(n2t_s[...], gexp_s[:, cols]).astype(BF16)
        return carry

    lax.fori_loop(0, 4, weights, 0)
    gout_o[...] = dot(attended[...], gb_s[...], TN).astype(BF16)


def attend_back_kernel(
    mixed, low, high, probs_i, gatt, lanes, lanes32, head_mask,
    gmixed_o, low_o, high_o, rim_o, q_s, k_s, v_s, g_s, dq_s, dkv_s,
):
    spread_rows(mixed, 0, D, None, None, q_s)
    spread_rows(mixed, D, D, low, high, k_s)
    spread_rows(mixed, 2 * D, D, low, high, v_s)
    spread_rows(gatt, 0, D, None, None, g_s)
    lane_low = lanes[...]
    lane_f = lanes32[...]

    def step(c, carry):
        rows = pl.ds(pl.multiple_of(c * CHUNK, CHUNK), CHUNK)
        for j in range(2):
            cols = slice(256 * j, 256 * j + 256)
            q = q_s[rows, cols]
            g = g_s[rows, cols]
            v = v_s[rows, cols]
            k_t = jnp.transpose(k_s[rows, cols])
            parts = []
            d_key = jnp.zeros((CHUNK, 256), F32)
            d_value = jnp.zeros((CHUNK, 256), F32)
            for pair in range(4):
                masks = [head_mask[2 * pair + i : 2 * pair + i + 1, :] for i in range(2)]
                q_m = jnp.concatenate([q * one for one in masks], axis=0)
                g_m = jnp.concatenate([g * one for one in masks], axis=0)
                start = (8 * j + 2 * pair) * CHUNK
                probs = probs_i[c, :, start : start + 256]
                g_probs = compress(dot(v, g_m, NT), lane_f)
                inner = jnp.sum(probs * g_probs, axis=0, keepdims=True)
                g_scores = (probs * (g_probs - inner)).astype(BF16)
                d_value = d_value + dot(expand_lanes(probs.astype(BF16), lane_low), g_m)
                full = expand_lanes(g_scores, lane_low)
                d_key = d_key + dot(full, q_m)
                for i in range(2):
                    h = 2 * pair + i
                    parts.append(
                        dot(k_t[32 * h : 32 * h + 32, :], full[:, CHUNK * i : CHUNK * i + CHUNK])
                    )
            dq_t = (jnp.concatenate(parts, axis=0) * SCALE).astype(BF16)
            dq_s[rows, cols] = jnp.transpose(dq_t)
            dkv_s[rows, cols] = d_key * SCALE
            dkv_s[rows, slice(D + 256 * j, D + 256 * j + 256)] = d_value
        return carry

    lax.fori_loop(0, CHUNKS, step, 0)
    for m in range(MICRO):
        base = m * EXT
        rows = slice(m * CELLS, (m + 1) * CELLS)
        gmixed_o[rows, :D] = dq_s[base + 16 : base + 16 + CELLS, :]
        gmixed_o[rows, D:] = dkv_s[base + 16 : base + 16 + CELLS, :].astype(BF16)
        low_o[m] = dkv_s[base : base + 16, :].astype(BF16)
        high_o[m] = dkv_s[base + 16 + CELLS : base + EXT, :].astype(BF16)
        rim_o[m, 0] = dkv_s[base + 16 : base + 32, :]
        rim_o[m, 1] = dkv_s[base + CELLS : base + CELLS + 16, :]


def leave_kernel(
    core, gmixed, from_low, from_high, rim, hidden, normed, filled, seen, cell, gmid, qkv_w, vecs,
    gout, sums, grads_o, ret_o, gm_s, gf_s, nt_s, ft_s,
):
    first, second = core[0], 1 - core[0]
    small = jnp.zeros((1, D), F32)
    gain_sum, shift_sum, mask_sum, embed_sum, query_sum, value_sum = [small] * 6
    for m in range(MICRO):
        base = m * CELLS
        rows = slice(base, base + CELLS)
        gm_s[rows, :] = gmixed[rows, :]
        gm_s[base : base + 16, D:] = (rim[m, 0] + from_low[m].astype(F32)).astype(BF16)
        gm_s[base + CELLS - 16 : base + CELLS, D:] = (rim[m, 1] + from_high[m].astype(F32)).astype(
            BF16
        )
        gm = gm_s[rows, :]
        grad = dot(gm, qkv_w[...], NT)
        normal, inverse = norm_parts(hidden[rows, :])
        g_hidden = gmid[rows, :] + norm_back(grad, normal, inverse, vecs[2:3, :])
        there = seen[rows, :] > 0.5
        g_low = g_hidden.astype(BF16)
        gf_s[rows, :] = g_low
        gain_sum += jnp.sum(grad * normal, axis=0, keepdims=True)
        shift_sum += jnp.sum(grad, axis=0, keepdims=True)
        mask_sum += jnp.sum(jnp.where(there, 0.0, g_hidden), axis=0, keepdims=True)
        embed_sum += jnp.sum(jnp.where(there, g_low.astype(F32), 0.0), axis=0, keepdims=True)
        query_sum += jnp.sum(gm[:, :D].astype(F32), axis=0, keepdims=True)
        value_sum += jnp.sum(gm[:, 2 * D :].astype(F32), axis=0, keepdims=True)
    nt_s[...] = jnp.transpose(normed[...])
    ft_s[...] = jnp.transpose(filled[...])
    ret_o[...] = dot(one_hot(iota((GOT, ALL), 1) == cell[...]), gf_s[...]).astype(BF16)

    def weights(b, carry):
        cols = pl.ds(pl.multiple_of(b * 512, 512), 512)
        grads_o[first, cols, :] = dot(nt_s[...], gm_s[:, cols]).astype(BF16)
        return carry

    lax.fori_loop(0, 3, weights, 0)
    grads_o[second, 0:512, :] = gout[...]
    grads_o[second, 512:1280, :] = dot(ft_s[...], gf_s[...]).astype(BF16)
    grads_o[second, 1280:1296, :] = jnp.concatenate(
        [
            embed_sum, mask_sum, gain_sum, shift_sum, query_sum, value_sum,
            small, small, sums[...],
        ],
        axis=0,
    ).astype(BF16)
    grads_o[second, 1296:1536, :] = jnp.zeros((240, D), BF16)


def return_kernel(dest, came, embed_w, out):
    select = one_hot(iota((MICRO * TOK, GOT), 1) == dest[...])
    g_proj = dot(select, came[...]).astype(BF16)
    out[...] = dot(g_proj, embed_w[...], NT).astype(BF16)


def clip_ident(lengths, rows):
    first = lengths[:, 0:1]
    second = first + lengths[:, 1:2]
    ident = (rows[None, :] >= first).astype(jnp.int32) + (rows[None, :] >= second).astype(jnp.int32)
    start = jnp.where(ident >= 1, first, 0) + jnp.where(ident >= 2, lengths[:, 1:2], 0)
    inside = (rows >= 0) & (rows < LONG)
    return (jnp.where(inside[None, :], ident, -1), rows[None, :] - start)


def position_table(row_in_clip, width):
    quarter = width // 4
    omega = 1.0 / 10000.0 ** (jnp.arange(quarter, dtype=jnp.float32) / quarter)
    row_angle = row_in_clip.astype(jnp.float32)[..., None] * omega
    freq_angle = jnp.arange(FREQ, dtype=jnp.float32)[:, None] * omega
    row_part = jnp.concatenate([jnp.sin(row_angle), jnp.cos(row_angle)], -1)
    freq_part = jnp.concatenate([jnp.sin(freq_angle), jnp.cos(freq_angle)], -1)
    shape = row_in_clip.shape + (FREQ, width // 2)
    return jnp.concatenate(
        [jnp.broadcast_to(row_part[..., None, :], shape), jnp.broadcast_to(freq_part, shape)], -1
    )


def window_mask(ident):
    cells = jnp.repeat(ident.reshape(MICRO * 7, 4), FREQ, axis=1)
    freq = np.tile((np.arange(FREQ) + 2) % 8 // 4, 4)
    same = (cells[:, :, None] == cells[:, None, :]) & (cells[:, :, None] >= 0)
    same = same & jnp.asarray(freq[:, None] == freq[None, :])[None]
    return same.astype(F32).reshape(CHUNKS, 4, 32, 32).transpose(0, 2, 1, 3).reshape(CHUNKS, 32, CHUNK)


def on_device(
    encoded, visible_pos, clip_len, cotangent, embed_weight, embed_bias, mask_token, attn_gain,
    attn_shift, qkv_weight, query_bias, value_bias, out_weight, out_bias, mlp_gain, mlp_shift,
    up_weight, up_bias, down_weight, down_bias,
):
    both = ("clip", "band")
    groups = lax.axis_size("clip")
    bands = lax.axis_size("band")
    band = lax.axis_index("band")
    side = band % 2
    core = side.astype(jnp.int32).reshape(1)
    halves = [
        [c * bands + 2 * x + k for c in range(groups) for x in range(bands // 2)] for k in range(2)
    ]
    swap = [(i, i ^ 1) for i in range(bands)]
    forward = [(i, i + 1) for i in range(bands - 1)]
    backward = [(b, a) for a, b in forward]
    chips = groups * bands // 2

    def to_all(block):
        return lax.all_to_all(
            block, both, split_axis=0, concat_axis=0, tiled=True, axis_index_groups=halves
        )

    def chip_sum(grads):
        rows = grads.shape[1] // chips
        other = lax.ppermute(grads[1], "band", swap)
        mine = (grads[0].astype(F32) + other.astype(F32)).astype(BF16)
        return mine.reshape(chips, rows, D)

    def total(parts):
        return jnp.sum(parts.astype(F32), 0).astype(BF16)

    pos = jnp.pad(visible_pos, ((0, 0), (0, TOK - visible_pos.shape[1])), constant_values=-1)
    micro = lax.broadcasted_iota(jnp.int32, pos.shape, 0)
    target = jnp.where(pos < 0, 99, pos // (LONG * FREQ))
    number = pos // FREQ % LONG % ROWS * FREQ + pos % FREQ + 1
    meta = jnp.stack(
        [x.reshape(-1) for x in (target, target * MICRO + micro, micro, number)] * 2
    )
    enc = jnp.pad(encoded, ((0, 0), (0, TOK - encoded.shape[1]), (0, 0))).reshape(MICRO * TOK, ENC)
    packed, dest = call(
        pack_kernel, "pack", [((GOT, ENC), BF16), ((MICRO * TOK, 1), jnp.int32)],
        (meta, meta.T, enc), flops=GOT * MICRO * TOK * ENC * 2,
    )
    got = lax.all_to_all(
        packed.reshape(SRC, BLK, ENC), "clip", split_axis=0, concat_axis=0, tiled=True
    ).reshape(GOT, ENC)

    place = np.arange(GOT)
    within = place % BLK
    index = np.zeros((8, GOT), np.int32)
    index[0], index[1], index[2] = place // BLK, within, np.where(within < 36, within // CAP, 99)
    lane = np.arange(256) % CHUNK // 32
    lanes = np.zeros((8, 256), np.float32)
    for w in range(4):
        lanes[w] = lane == w
    head_mask = (np.arange(256)[None, :] // 32 == np.arange(8)[:, None]).astype(np.float32)
    lanes_f = jnp.asarray(lanes)
    lanes_low = jnp.asarray(lanes, BF16)
    head_mask = jnp.asarray(head_mask, BF16)

    unused, row_in_clip = clip_ident(clip_len[:, 0], band * ROWS + jnp.arange(ROWS))
    table = position_table(row_in_clip, D).reshape(ALL, D)
    ident_ext, unused = clip_ident(clip_len[:, 0], band * ROWS - 2 + jnp.arange(ROWS + 4))
    mask = window_mask(ident_ext)
    zero = jnp.zeros((D,), BF16)
    vecs_one = jnp.stack([embed_bias, mask_token, attn_gain, attn_shift] * 2).astype(F32)
    vecs_two = jnp.stack([out_bias, mlp_gain, mlp_shift, down_bias] * 2).astype(F32)
    qkv_b = jnp.concatenate([query_bias, zero, value_bias]).astype(F32)[None]
    up_b = up_bias.astype(F32)[None]

    hidden, normed, mixed, filled, seen, cell, low, high = call(
        enter_kernel, "enter",
        [
            ((ALL, D), F32), ((ALL, D), BF16), ((ALL, 3 * D), BF16), ((ALL, ENC), BF16),
            ((ALL, 1), F32), ((GOT, 1), jnp.int32),
            ((MICRO, 16, 2 * D), BF16), ((MICRO, 16, 2 * D), BF16),
        ],
        (
            jnp.asarray(index), jnp.asarray(np.ascontiguousarray(index.T)), got, table,
            embed_weight, qkv_weight, vecs_one, qkv_b,
        ),
        flops=2 * ALL * (GOT * ENC + ENC * D + 3 * D * D),
    )
    from_low = lax.ppermute(high, "band", forward)
    from_high = lax.ppermute(low, "band", backward)
    ext = MICRO * EXT
    attended, probs = call(
        attend_kernel, "attend",
        [((ALL, D), BF16), ((CHUNKS, 32, HEADS * CHUNK), F32)],
        (mixed, from_low, from_high, mask, lanes_low, lanes_f, head_mask),
        scratch=[pltpu.VMEM((ext, D), BF16)] * 4,
        flops=ext * HEADS * CHUNK * 256 * 4,
    )
    cot = cotangent.reshape(ALL, D)
    output, gmid, gatt, grads_one, gout, sums = call(
        mlp_kernel, "mlp",
        [
            ((ALL, D), BF16), ((ALL, D), F32), ((ALL, D), BF16), ((2, FF, D), BF16),
            ((D, D), BF16), ((8, D), F32),
        ],
        (core, hidden, attended, cot, out_weight, up_weight, down_weight, vecs_two, up_b),
        scratch=[
            pltpu.VMEM((ALL, FF), BF16), pltpu.VMEM((ALL, FF), BF16), pltpu.VMEM((ALL, D), BF16),
            pltpu.VMEM((ALL, D), BF16), pltpu.VMEM((D, ALL), BF16),
        ],
        smem=1, flops=2 * ALL * (6 * D * FF + 3 * D * D),
    )
    chip_one = chip_sum(grads_one)
    gatt, chip_one = lax.optimization_barrier((gatt, chip_one))
    parts_one = to_all(chip_one)
    gmixed, low, high, rim = call(
        attend_back_kernel, "attend_back",
        [
            ((ALL, 3 * D), BF16), ((MICRO, 16, 2 * D), BF16), ((MICRO, 16, 2 * D), BF16),
            ((MICRO, 2, 16, 2 * D), F32),
        ],
        (mixed, from_low, from_high, probs, gatt, lanes_low, lanes_f, head_mask),
        scratch=[pltpu.VMEM((ext, D), BF16)] * 5 + [pltpu.VMEM((ext, 2 * D), F32)],
        flops=ext * HEADS * CHUNK * 256 * 8,
    )
    from_low = lax.ppermute(high, "band", forward)
    from_high = lax.ppermute(low, "band", backward)
    grads_two, returned = call(
        leave_kernel, "leave",
        [((2, 3 * D, D), BF16), ((GOT, D), BF16)],
        (
            core, gmixed, from_low, from_high, rim, hidden, normed, filled, seen, cell, gmid,
            qkv_weight, vecs_one, gout, sums,
        ),
        scratch=[
            pltpu.VMEM((ALL, 3 * D), BF16), pltpu.VMEM((ALL, D), BF16),
            pltpu.VMEM((D, ALL), BF16), pltpu.VMEM((ENC, ALL), BF16),
        ],
        smem=1, flops=2 * ALL * (6 * D * D + GOT * D + ENC * D),
    )
    parts_one, grads_two = lax.optimization_barrier((parts_one, grads_two))
    total_one = lax.all_gather(total(parts_one), both, axis=0)
    total_one = total_one.reshape(chips, 2, -1, D)
    half_one = [total_one[:, k].reshape(-1, D).astype(F32) for k in range(2)]
    mine = total(to_all(chip_sum(grads_two)))
    mine = to_all(jnp.broadcast_to(mine[None], (chips,) + mine.shape)).reshape(-1, D)
    mine, returned = lax.optimization_barrier((mine, returned))
    other = lax.ppermute(mine, "band", swap)
    half_two = (
        jnp.where(side == 0, mine, other).astype(F32),
        jnp.where(side == 0, other, mine).astype(F32),
    )
    came = lax.all_to_all(
        returned.reshape(SRC, BLK, D), "clip", split_axis=0, concat_axis=0, tiled=True
    ).reshape(GOT, D)
    (grad_enc,) = call(
        return_kernel, "return", [((MICRO * TOK, ENC), BF16)], (dest, came, embed_weight),
        flops=2 * MICRO * TOK * D * (GOT + ENC),
    )
    grad_enc = grad_enc.reshape(MICRO, TOK, ENC)[:, : encoded.shape[1]]

    down = jnp.concatenate([half_one[0][:1024], half_one[1][:1024]], 0)
    up = jnp.concatenate([h[1024 + 512 * b : 1536 + 512 * b] for h in half_one for b in range(2)], 1)
    qkv = jnp.concatenate([half_two[0][512 * b : 512 * b + 512] for b in range(3)], 1)
    rest = half_two[1]
    small = rest[1280:1296]
    return (
        output.reshape(cotangent.shape), grad_enc, rest[512:1280], small[0], small[1], small[2],
        small[3], qkv, small[4], small[5], rest[:512], small[8], small[9], small[10], up,
        small[12:16].reshape(FF), down, small[11],
    )


def solution(mesh):
    whole = P()
    return jax.shard_map(
        on_device,
        mesh=mesh,
        in_specs=(
            P(None, ("clip", "band"), None),
            P(None, ("clip", "band")),
            P(None, "clip", None),
            P(None, "clip", "band", None, None),
        )
        + (whole,) * 16,
        out_specs=(P(None, "clip", "band", None, None), P(None, ("clip", "band"), None))
        + (whole,) * 16,
        check_vma=False,
    )
```

time: 772 us -> 282 us (0.37); the launches traced: 757 us -> 281 us
  local copies, waits for them, and re-layouts: 206 us -> 19.9 us
  matrix products: 117 us -> 0 us
  waiting for transfers between devices: 139 us -> 36.4 us
  Pallas kernels: 0 us -> 89.7 us
  starting transfers between devices: 116 us -> 35 us
  other arithmetic: 90.9 us -> 22.9 us
  between operations: 24.3 us -> 14.6 us
    reshape x80 -> x0, local copies, waits for them, and re-layouts: 132 us -> none  [the longest x32 66.4 us: to_windows(): tensor = tensor.reshape(slots, extent // 4, 4, 2, 4, HEADS, width // HEADS)]
    dot_general x96 -> x0, matrix products: 117 us -> none  [the longest x4 21.1 us: on_device(): jnp.dot(normed_two_low, up_weight, preferred_element_type=jnp.float32)]
    psum x1 -> x0, waiting for transfers between devices: 97 us -> none  [on_device(): totals = lax.psum(totals, ('clip', 'band'))]
    pallas_call x0 -> x7, Pallas kernels: none -> 89.7 us  [call(): pl.pallas_call(kernel, name=name, out_shape=outs, in_specs=specs, out_spe...]
    psum x1 -> x0, blocking collectives: 65.4 us -> none  [on_device(): totals = lax.psum(totals, ('clip', 'band'))]
    all_to_all x0 -> x2, blocking collectives: none -> 62 us  [to_all(): lax.all_to_all(block, both, split_axis=0, concat_axis=0, tiled=True, axis...]
    all_to_all x12 -> x3, starting transfers between devices: 63.1 us -> 18.3 us  [the longest x1 8.6 us: on_device(): lax.all_to_all(packed.reshape(SRC, BLK, ENC), 'clip', split_axis=0, conca...]
    ppermute x16 -> x7, starting transfers between devices: 52.2 us -> 16.7 us  [the longest x2 9.54 us: on_device(): from_low = lax.ppermute(high, 'band', forward)]
  transfers between devices with their start and end apart: 29 -> 11, of which waited for: 9 -> 7; matrix products, arithmetic and copies ran while one was open for 30% -> 7% of each run, Pallas kernels for 0% -> 13%
where the time goes in v1:
time: 282 us; the launch traced here: 281 us
  Pallas kernels  89.7 us (32%)
  blocking collectives  62 us (22%)
  waiting for transfers between devices  36.4 us (13%)
  starting transfers between devices  35 us (12%)
  other arithmetic  22.9 us (8%)
  local copies, waits for them, and re-layouts  19.9 us (7%)
  between operations  14.6 us (5%)
    pallas_call x7, Pallas kernels, call(): pl.pallas_call(kernel, name=name, out_shape=outs, in_specs=specs, out_spe...  89.7 us
    all_to_all x2, blocking collectives, to_all(): lax.all_to_all(block, both, split_axis=0, concat_axis=0, tiled=True, axis...  62 us
    all_to_all x1, waiting for transfers between devices, on_device(): lax.all_to_all(returned.reshape(SRC, BLK, D), 'clip', split_axis=0, conca...  14 us
    ppermute x2, starting transfers between devices, on_device(): from_low = lax.ppermute(high, 'band', forward)  9.54 us
    all_to_all x1, starting transfers between devices, on_device(): lax.all_to_all(packed.reshape(SRC, BLK, ENC), 'clip', split_axis=0, conca...  8.6 us
    ppermute x2, waiting for transfers between devices, on_device(): from_high = lax.ppermute(low, 'band', backward)  7.96 us
    all_to_all x1, waiting for transfers between devices, on_device(): lax.all_to_all(packed.reshape(SRC, BLK, ENC), 'clip', split_axis=0, conca...  7.42 us
    ppermute x2, waiting for transfers between devices, chip_sum(): other = lax.ppermute(grads[1], 'band', swap)  6.94 us
  transfers between devices with their start and end apart: 11, of which 7 were waited for; matrix products, arithmetic and copies ran while one was open for 7% of the time, Pallas kernels for 13%

profile of v1, /device:TPU:1, one launch (start us, length us, event | category | flops | bytes accessed | tf_op | source)
XLA Modules:
  0.0 280.7 jit_solution(18038864297400829901)
XLA Ops:
  7.3 0.8 iota_add_fusion
  8.5 0.8 copy.66
  9.3 1.0 copy.75
  10.2 0.7 pad.9.clone
  11.0 3.1 %pack.1 = (bf16[640,768]{1,0:T(8,128)(2,1)}, s32[192,1]{1,0:T(8,128)}) custom-call(s32[8,192]{1,0:T(8,128)} %copy-done.3, s32[192,8]{1,0:T(8,128)} %bitcast.73, bf16[192,768]{1,0:T(8,128)(2,1)} %bitcast.71), custom_call_target="tpu_custom_call" | custom-call | flops 188743680 | bytes 1291008 | tf_op jit(solution)/shard_map/pack/pallas_call | solution.py:56
  14.0 8.6 %all-to-all-start = ((bf16[16,40,768]{2,1,0:T(8,128)(2,1)}), bf16[16,40,768]{2,1,0:T(8,128)(2,1)S(1)}, u32[]{:S(2)}, u32[]{:S(2)}) async-start(bf16[16,40,768]{2,1,0:T(8,128)(2,1)} %bitcast.70), calls=%async_computation | async-start | bytes 1966080 | tf_op jit(solution)/shard_map/all_to_all | solution.py:470
  28.1 1.3 pad_maximum_fusion.3
  30.0 7.4 %all-to-all-done = bf16[16,40,768]{2,1,0:T(8,128)(2,1)S(1)} async-done(((bf16[16,40,768]{2,1,0:T(8,128)(2,1)}), bf16[16,40,768]{2,1,0:T(8,128)(2,1)S(1)}, u32[]{:S(2)}, u32[]{:S(2)}) %all-to-all-start) | async-done | bytes 983072 | tf_op jit(solution)/shard_map/all_to_all | solution.py:470
  37.4 0.9 copy-done.2
  38.4 9.6 %enter.1 = (f32[768,512]{1,0:T(8,128)}, bf16[768,512]{1,0:T(8,128)(2,1)}, bf16[768,1536]{1,0:T(8,128)(2,1)}, bf16[768,768]{1,0:T(8,128)(2,1)}, f32[768,1]{1,0:T(...) custom-call(s32[8,640]{1,0:T(8,128)} %constant.111.clone.idx_r, ...), custom_call_target="tpu_custom_call" | custom-call | flops 2566914048 | bytes 11144704 | tf_op jit(solution)/shard_map/enter/pallas_call | solution.py:56
  47.9 6.0 %collective-permute-start = (bf16[4,16,1024]{2,1,0:T(8,128)(2,1)}, bf16[4,16,1024]{2,1,0:T(8,128)(2,1)S(1)}, u32[]{:S(2)}, u32[]{:S(2)}) collective-permute-start(bf16[4,16,1024]{2,1,0:T(8,128)(2,1)} %get-tuple-element.51), channel_id=1, source_target_pairs={{0,1},{1,2},{2,3},{3,4},{4,5},{5,6},{6,7},{8,9},{9,10},{10,11},{11... | collective-permute-start | bytes 393224 | tf_op jit(solution)/shard_map/ppermute | solution.py:510
  54.0 2.1 collective-permute-start.1
  56.1 0.7 and_convert_fusion.mask
  56.8 3.7 %collective-permute-done.1.high = bf16[4,16,1024]{2,1,0:T(8,128)(2,1)S(1)} collective-permute-done((bf16[4,16,1024]{2,1,0:T(8,128)(2,1)}, bf16[4,16,1024]{2,1,0:T(8,128)(2,1)S(1)}, u32[]{:S(2)}, u32[]{:S(2)}) %collective-permute-start.1) | collective-permute-done | bytes 131104 | tf_op jit(solution)/shard_map/ppermute | solution.py:511
  60.5 0.7 copy-done.18
  61.1 16.0 %attend.1 = (bf16[768,512]{1,0:T(8,128)(2,1)}, f32[7,32,2048]{2,1,0:T(8,128)}) custom-call(bf16[768,1536]{1,0:T(8,128)(2,1)} %get-tuple-element.50.mixed, bf16[4,16,1024]{2,1,0:T(8,128)(2,1)} %copy-done.17, bf16[4,16,1024]{2,1,0:T(8,128)(2,1)} %copy-done.18, f32[7,32,128]{2,1,0:T(8,128)} %and_convert_fusion.mask, bf16[8,256]{1,0:T(8,128)(2,1)} %constant.108.clone.lanes, ...), custom_call_target="tpu_custom_call" | custom-call | flops 1879048192 | bytes 5373952 | tf_op jit(solution)/shard_map/attend/pallas_call | solution.py:56
  77.2 25.4 %mlp.1 = (bf16[768,512]{1,0:T(8,128)(2,1)}, f32[768,512]{1,0:T(8,128)}, bf16[768,512]{1,0:T(8,128)(2,1)}, bf16[2,2048,512]{2,1,0:T(8,128)(2,1)}, bf16[512,512]{1,0:T(8,128)(2,1)}, /*index=5*/f32[8,512]{1,0:T(8,128)}) custom-call(s32[1]{0:T(128)} %bitcast.core, f32[768,512]{1,0:T(8,128)} %get-tuple-element.49.hidden, ...), custom_call_target="tpu_custom_call" | custom-call | flops 10871635968 | bytes 15769604 | tf_op jit(solution)/shard_map/mlp/pallas_call | solution.py:56
  102.6 1.9 slice_bitcast_fusion
  104.5 4.1 %collective-permute-done.2 = bf16[2048,512]{1,0:T(8,128)(2,1)S(1)} collective-permute-done((bf16[2048,512]{1,0:T(8,128)(2,1)S(1)}, bf16[2048,512]{1,0:T(8,128)(2,1)S(1)}, u32[]{:S(2)}, u32[]{:S(2)}) %collective-permute-start.2) | collective-permute-done | bytes 2097184 | tf_op jit(solution)/shard_map/ppermute | solution.py:451
  108.7 1.9 fusion
  110.6 6.1 %all-to-all-start.1 = ((bf16[64,32,512]{2,1,0:T(8,128)(2,1)}), bf16[64,32,512]{2,1,0:T(8,128)(2,1)S(1)}, u32[]{:S(2)}, u32[]{:S(2)}) async-start(bf16[64,32,512]{2,1,0:T(8,128)(2,1)} %bitcast.15), calls=%async_computation.1 | async-start | bytes 4194304 | tf_op jit(solution)/shard_map/all_to_all | solution.py:445
  116.8 21.3 %attend_back.1 = (bf16[768,1536]{1,0:T(8,128)(2,1)}, bf16[4,16,1024]{2,1,0:T(8,128)(2,1)}, bf16[4,16,1024]{2,1,0:T(8,128)(2,1)}, f32[4,2,16,1024]{3,2,1,0:T(8,128)}) custom-call(bf16[768,1536]{1,0:T(8,128)(2,1)} %get-tuple-element.50.mixed, bf16[4,16,1024]{2,1,0:T(8,128)(2,1)} %copy-done.17, bf16[4,16,1024]{2,1,0:T(8,128)(2,1)} %copy-done.18, ...), custom_call_target="tpu_custom_call" | custom-call | flops 3758096384 | bytes 8404992 | tf_op jit(solution)/shard_map/attend_back/pallas_call | solution.py:56
  138.0 3.5 %collective-permute-start.3 = (bf16[4,16,1024]{2,1,0:T(8,128)(2,1)}, bf16[4,16,1024]{2,1,0:T(8,128)(2,1)S(1)}, u32[]{:S(2)}, u32[]{:S(2)}) collective-permute-start(bf16[4,16,1024]{2,1,0:T(8,128)(2,1)} %get-tuple-element.62), channel_id=1, source_target_pairs={{0,1},{1,2},{2,3},{3,4},{4,5},{5,6},{6,7},{8,9},{9,10},{10,11},{11... | collective-permute-start | bytes 393224 | tf_op jit(solution)/shard_map/ppermute | solution.py:547
  141.5 2.1 collective-permute-start.4
  143.8 4.3 %collective-permute-done.4.from_high = bf16[4,16,1024]{2,1,0:T(8,128)(2,1)S(1)} collective-permute-done((bf16[4,16,1024]{2,1,0:T(8,128)(2,1)}, bf16[4,16,1024]{2,1,0:T(8,128)(2,1)S(1)}, u32[]{:S(2)}, u32[]{:S(2)}) %collective-permute-start.4) | collective-permute-done | bytes 131104 | tf_op jit(solution)/shard_map/ppermute | solution.py:548
  148.0 0.6 copy-done.20
  148.7 11.6 %leave.1 = (bf16[2,1536,512]{2,1,0:T(8,128)(2,1)}, bf16[640,512]{1,0:T(8,128)(2,1)}) custom-call(s32[1]{0:T(128)} %bitcast.core, bf16[768,1536]{1,0:T(8,128)(2,1)} %get-tuple-element.61.gmixed, bf16[4,16,1024]{2,1,0:T(8,128)(2,1)} %copy-done.19, bf16[4,16,1024]{2,1,0:T(8,128)(2,1)} %copy-done.20, f32[4,2,16,1024]{3,2,1,0:T(8,128)} %get-tuple-element.64.rim, ...), custom_call_target="tpu_custom_call" | custom-call | flops 3523215360 | bytes 14194180 | tf_op jit(solution)/shard_map/leave/pallas_call | solution.py:56
  160.3 2.7 slice_bitcast_fusion.1
  162.9 0.9 reduce_sum.25
  163.9 2.8 collective-permute-done.5
  166.7 2.3 fusion.1
  169.0 33.6 %all_to_all.25 = bf16[64,24,512]{2,1,0:T(8,128)(2,1)S(1)} all-to-all(bf16[64,24,512]{2,1,0:T(8,128)(2,1)S(1)} %bitcast.60), channel_id=1, replica_groups={{0,2,4,6,8,10,12,14,16,18,20,22,24,26,28,30,32,34,36,38,40,42,44,46,48,..., dimensions={0} | all-to-all | bytes 3145728 | tf_op jit(solution)/shard_map/all_to_all | solution.py:445
  203.0 28.3 %all_to_all.26 = bf16[64,24,512]{2,1,0:T(8,128)(2,1)S(1)} all-to-all(bf16[64,24,512]{2,1,0:T(8,128)(2,1)S(1)} %broadcast_in_dim.84), channel_id=1, replica_groups={{0,2,4,6,8,10,12,14,16,18,20,22,24,26,28,30,32,34,36,38,40,42,44,46,48,..., dimensions={0} | all-to-all | bytes 3145728 | tf_op jit(solution)/shard_map/all_to_all | solution.py:445
  231.3 2.8 %collective-permute-start.6 = (bf16[1536,512]{1,0:T(8,128)(2,1)S(1)}, bf16[1536,512]{1,0:T(8,128)(2,1)}, u32[]{:S(2)}, u32[]{:S(2)}) collective-permute-start(bf16[1536,512]{1,0:T(8,128)(2,1)S(1)} %bitcast.58), channel_id=1, source_target_pairs={{0,1},{1,0},{2,3},{3,2},{4,5},{5,4},{6,7},{7,6},{8,9},{9,8},{10,11... | collective-permute-start | bytes 4718600 | tf_op jit(solution)/shard_map/ppermute | solution.py:569
  234.1 3.6 %all-to-all-start.4 = ((bf16[16,40,512]{2,1,0:T(8,128)(2,1)}), bf16[16,40,512]{2,1,0:T(8,128)(2,1)S(1)}, u32[]{:S(2)}, u32[]{:S(2)}) async-start(bf16[16,40,512]{2,1,0:T(8,128)(2,1)} %bitcast.20), calls=%async_computation.4 | async-start | bytes 1310720 | tf_op jit(solution)/shard_map/all_to_all | solution.py:574
  237.7 14.0 %all-to-all-done.4 = bf16[16,40,512]{2,1,0:T(8,128)(2,1)S(1)} async-done(((bf16[16,40,512]{2,1,0:T(8,128)(2,1)}), bf16[16,40,512]{2,1,0:T(8,128)(2,1)S(1)}, u32[]{:S(2)}, u32[]{:S(2)}) %all-to-all-start.4) | async-done | bytes 655392 | tf_op jit(solution)/shard_map/all_to_all | solution.py:574
  251.7 0.8 copy-done.1
  252.6 2.8 %return.1 = bf16[192,768]{1,0:T(8,128)(2,1)} custom-call(s32[192,1]{1,0:T(8,128)} %get-tuple-element.55.dest, bf16[640,512]{1,0:T(8,128)(2,1)} %bitcast.66, bf16[768,512]{1,0:T(8,128)(2,1)} %embed_w.3), custom_call_target="tpu_custom_call" | custom-call | flops 276824064 | bytes 1737472 | tf_op jit(solution)/shard_map/return/pallas_call | solution.py:56
  255.4 1.0 slice.169
  256.4 0.8 copy.74
  257.1 1.8 select_convert_fusion
  259.0 1.3 slice.170
  260.3 1.0 slice.180
  261.9 0.6 fusion.18
  262.8 1.9 pad_maximum_fusion.2
  264.7 3.0 %slice_convert_fusion.1 = (f32[64,1,32,512]{3,2,1,0:T(8,128)S(1)}, f32[64,1,32,512]{3,2,1,0:T(8,128)S(1)}) fusion(bf16[64,2,32,512]{3,2,1,0:T(8,128)(2,1)} %bitcast.61), kind=kLoop, calls=%fused_computation.8 | loop fusion | flops 2097152 | bytes 12582912 | tf_op jit(solution)/shard_map/convert_element_type | solution.py:565
  268.9 2.6 pad_maximum_fusion.1
  271.4 2.4 pad_maximum_fusion
  (114 shorter events, 8.8 us)
Async XLA Ops:
  7.2 18.9 %copy-start.5 = (pred[32,32]{1,0:T(32,128)(4,1)S(1)}, pred[32,32]{1,0:T(32,128)(4,1)}, u32[]{:S(2)}) copy-start(pred[32,32]{1,0:T(32,128)(4,1)} %constant.110.clone) | copy-start | bytes 3076
  7.2 15.5 %copy-start.6 = (s32[4,1,3]{0,1,2:T(1,128)S(1)}, s32[4,1,3]{0,1,2:T(1,128)}, u32[]{:S(2)}) copy-start(s32[4,1,3]{0,1,2:T(1,128)} %param.28) | copy-start | bytes 148
  7.2 16.8 %copy-start.7 = (bf16[512]{0:T(512)(128)(2,1)S(1)}, bf16[512]{0:T(512)(128)(2,1)}, u32[]{:S(2)}) copy-start(bf16[512]{0:T(512)(128)(2,1)} %param.31) | copy-start | bytes 3076
  7.2 16.8 %copy-start.8 = (bf16[512]{0:T(512)(128)(2,1)S(1)}, bf16[512]{0:T(512)(128)(2,1)}, u32[]{:S(2)}) copy-start(bf16[512]{0:T(512)(128)(2,1)} %param.32) | copy-start | bytes 3076
  7.2 16.8 %copy-start.9 = (bf16[512]{0:T(512)(128)(2,1)S(1)}, bf16[512]{0:T(512)(128)(2,1)}, u32[]{:S(2)}) copy-start(bf16[512]{0:T(512)(128)(2,1)} %param.33) | copy-start | bytes 3076
  7.2 16.8 %copy-start.10 = (bf16[512]{0:T(512)(128)(2,1)S(1)}, bf16[512]{0:T(512)(128)(2,1)}, u32[]{:S(2)}) copy-start(bf16[512]{0:T(512)(128)(2,1)} %param.34) | copy-start | bytes 3076
  7.3 17.5 %copy-start.11 = (bf16[512]{0:T(512)(128)(2,1)S(1)}, bf16[512]{0:T(512)(128)(2,1)}, u32[]{:S(2)}) copy-start(bf16[512]{0:T(512)(128)(2,1)} %param.36) | copy-start | bytes 3076
  7.3 17.5 %copy-start.12 = (bf16[512]{0:T(512)(128)(2,1)S(1)}, bf16[512]{0:T(512)(128)(2,1)}, u32[]{:S(2)}) copy-start(bf16[512]{0:T(512)(128)(2,1)} %param.37) | copy-start | bytes 3076
  7.3 18.9 %copy-start.13 = (bf16[512]{0:T(512)(128)(2,1)S(1)}, bf16[512]{0:T(512)(128)(2,1)}, u32[]{:S(2)}) copy-start(bf16[512]{0:T(512)(128)(2,1)} %param.39) | copy-start | bytes 3076
  7.3 18.9 %copy-start.14 = (bf16[512]{0:T(512)(128)(2,1)S(1)}, bf16[512]{0:T(512)(128)(2,1)}, u32[]{:S(2)}) copy-start(bf16[512]{0:T(512)(128)(2,1)} %param.40) | copy-start | bytes 3076
  7.3 19.0 %copy-start.15 = (bf16[512]{0:T(512)(128)(2,1)S(1)}, bf16[512]{0:T(512)(128)(2,1)}, u32[]{:S(2)}) copy-start(bf16[512]{0:T(512)(128)(2,1)} %param.41) | copy-start | bytes 3076
  7.3 19.0 %copy-start.16 = (bf16[512]{0:T(512)(128)(2,1)S(1)}, bf16[512]{0:T(512)(128)(2,1)}, u32[]{:S(2)}) copy-start(bf16[512]{0:T(512)(128)(2,1)} %param.45) | copy-start | bytes 3076
  7.3 19.6 %copy-start.4 = (bf16[2048]{0:T(1024)(128)(2,1)S(1)}, bf16[2048]{0:T(1024)(128)(2,1)}, u32[]{:S(2)}) copy-start(bf16[2048]{0:T(1024)(128)(2,1)} %param.43) | copy-start | bytes 12292
  8.5 2.5 copy-start.3
  14.0 23.4 %all-to-all-start = ((bf16[16,40,768]{2,1,0:T(8,128)(2,1)}), bf16[16,40,768]{2,1,0:T(8,128)(2,1)S(1)}, u32[]{:S(2)}, u32[]{:S(2)}) async-start(bf16[16,40,768]{2,1,0:T(8,128)(2,1)} %bitcast.70), calls=%async_computation | async-start | bytes 1966080 | tf_op jit(solution)/shard_map/all_to_all | solution.py:470
  37.4 0.9 copy-start.2
  47.9 8.8 %collective-permute-start = (bf16[4,16,1024]{2,1,0:T(8,128)(2,1)}, bf16[4,16,1024]{2,1,0:T(8,128)(2,1)S(1)}, u32[]{:S(2)}, u32[]{:S(2)}) collective-permute-start(bf16[4,16,1024]{2,1,0:T(8,128)(2,1)} %get-tuple-element.51), channel_id=1, source_target_pairs={{0,1},{1,2},{2,3},{3,4},{4,5},{5,6},{6,7},{8,9},{9,10},{10,11},{11... | collective-permute-start | bytes 393224 | tf_op jit(solution)/shard_map/ppermute | solution.py:510
  54.0 6.5 %collective-permute-start.1 = (bf16[4,16,1024]{2,1,0:T(8,128)(2,1)}, bf16[4,16,1024]{2,1,0:T(8,128)(2,1)S(1)}, u32[]{:S(2)}, u32[]{:S(2)}) collective-permute-start(bf16[4,16,1024]{2,1,0:T(8,128)(2,1)} %get-tuple-element.52), channel_id=1, source_target_pairs={{1,0},{2,1},{3,2},{4,3},{5,4},{6,5},{7,6},{9,8},{10,9},{11,10},{12... | collective-permute-start | bytes 393224 | tf_op jit(solution)/shard_map/ppermute | solution.py:511
  56.8 3.7 %copy-start.17 = (bf16[4,16,1024]{2,1,0:T(8,128)(2,1)}, bf16[4,16,1024]{2,1,0:T(8,128)(2,1)S(1)}, u32[]{:S(2)}) copy-start(bf16[4,16,1024]{2,1,0:T(8,128)(2,1)S(1)} %collective-permute-done.low) | copy-start | bytes 393220
  60.5 0.7 copy-start.18
  102.6 6.1 %copy-start = (bf16[2,2048,512]{2,1,0:T(8,128)(2,1)S(1)}, bf16[2,2048,512]{2,1,0:T(8,128)(2,1)}, u32[]{:S(2)}) copy-start(bf16[2,2048,512]{2,1,0:T(8,128)(2,1)} %get-tuple-element.57) | copy-start | bytes 12582916
  104.4 4.2 %collective-permute-start.2 = (bf16[2048,512]{1,0:T(8,128)(2,1)S(1)}, bf16[2048,512]{1,0:T(8,128)(2,1)S(1)}, u32[]{:S(2)}, u32[]{:S(2)}) collective-permute-start(bf16[2048,512]{1,0:T(8,128)(2,1)S(1)} %slice_bitcast_fusion), channel_id=1, source_target_pairs={{0,1},{1,0},{2,3},{3,2},{4,5},{5,4},{6,7},{7,6},{8,9},{9,8},{10,11... | collective-permute-start | bytes 6291464 | tf_op jit(solution)/shard_map/ppermute | solution.py:451
  110.6 49.7 %all-to-all-start.1 = ((bf16[64,32,512]{2,1,0:T(8,128)(2,1)}), bf16[64,32,512]{2,1,0:T(8,128)(2,1)S(1)}, u32[]{:S(2)}, u32[]{:S(2)}) async-start(bf16[64,32,512]{2,1,0:T(8,128)(2,1)} %bitcast.15), calls=%async_computation.1 | async-start | bytes 4194304 | tf_op jit(solution)/shard_map/all_to_all | solution.py:445
  116.7 148.0 %all-gather.3.cloned.1.call-start = ((), (), s32[]{:S(2)}) async-start(), calls=%async_computation.5 | async-start | bytes 4227072 | tf_op jit(solution)/shard_map/all_gather | solution.py:563
  138.0 5.8 %collective-permute-start.3 = (bf16[4,16,1024]{2,1,0:T(8,128)(2,1)}, bf16[4,16,1024]{2,1,0:T(8,128)(2,1)S(1)}, u32[]{:S(2)}, u32[]{:S(2)}) collective-permute-start(bf16[4,16,1024]{2,1,0:T(8,128)(2,1)} %get-tuple-element.62), channel_id=1, source_target_pairs={{0,1},{1,2},{2,3},{3,4},{4,5},{5,6},{6,7},{8,9},{9,10},{10,11},{11... | collective-permute-start | bytes 393224 | tf_op jit(solution)/shard_map/ppermute | solution.py:547
  141.5 6.5 %collective-permute-start.4 = (bf16[4,16,1024]{2,1,0:T(8,128)(2,1)}, bf16[4,16,1024]{2,1,0:T(8,128)(2,1)S(1)}, u32[]{:S(2)}, u32[]{:S(2)}) collective-permute-start(bf16[4,16,1024]{2,1,0:T(8,128)(2,1)} %get-tuple-element.63), channel_id=1, source_target_pairs={{1,0},{2,1},{3,2},{4,3},{5,4},{6,5},{7,6},{9,8},{10,9},{11,10},{12... | collective-permute-start | bytes 393224 | tf_op jit(solution)/shard_map/ppermute | solution.py:548
  143.8 4.3 %copy-start.19 = (bf16[4,16,1024]{2,1,0:T(8,128)(2,1)}, bf16[4,16,1024]{2,1,0:T(8,128)(2,1)S(1)}, u32[]{:S(2)}) copy-start(bf16[4,16,1024]{2,1,0:T(8,128)(2,1)S(1)} %collective-permute-done.3.from_low) | copy-start | bytes 393220
  148.0 0.6 copy-start.20
  162.9 3.8 %collective-permute-start.5 = (bf16[1536,512]{1,0:T(8,128)(2,1)}, bf16[1536,512]{1,0:T(8,128)(2,1)}, u32[]{:S(2)}, u32[]{:S(2)}) collective-permute-start(bf16[1536,512]{1,0:T(8,128)(2,1)} %slice_bitcast_fusion.1), channel_id=1, source_target_pairs={{0,1},{1,0},{2,3},{3,2},{4,5},{5,4},{6,7},{7,6},{8,9},{9,8},{10,11... | collective-permute-start | bytes 4718600 | tf_op jit(solution)/shard_map/ppermute | solution.py:451
  231.3 25.8 %collective-permute-start.6 = (bf16[1536,512]{1,0:T(8,128)(2,1)S(1)}, bf16[1536,512]{1,0:T(8,128)(2,1)}, u32[]{:S(2)}, u32[]{:S(2)}) collective-permute-start(bf16[1536,512]{1,0:T(8,128)(2,1)S(1)} %bitcast.58), channel_id=1, source_target_pairs={{0,1},{1,0},{2,3},{3,2},{4,5},{5,4},{6,7},{7,6},{8,9},{9,8},{10,11... | collective-permute-start | bytes 4718600 | tf_op jit(solution)/shard_map/ppermute | solution.py:569
  234.1 17.6 %all-to-all-start.4 = ((bf16[16,40,512]{2,1,0:T(8,128)(2,1)}), bf16[16,40,512]{2,1,0:T(8,128)(2,1)S(1)}, u32[]{:S(2)}, u32[]{:S(2)}) async-start(bf16[16,40,512]{2,1,0:T(8,128)(2,1)} %bitcast.20), calls=%async_computation.4 | async-start | bytes 1310720 | tf_op jit(solution)/shard_map/all_to_all | solution.py:574
  251.7 0.8 copy-start.1
Sparse Core Ops, SparseCore 0:
  164.0 96.0 all-gather.2

commit v2 on v1

v2 whole, which is shorter than its diff:
```python
import jax
import jax.numpy as jnp
import numpy as np
from jax import lax
from jax.experimental import pallas as pl
from jax.experimental.pallas import tpu as pltpu
from jax.sharding import PartitionSpec as P

HEADS = 16
FREQ = 8
LONG = 192
MICRO = 4
ROWS = 24
CELLS = ROWS * FREQ
ALL = MICRO * CELLS
CAP = 9
BLK = 40
SRC = 16
GOT = SRC * BLK
D = 512
FF = 2048
ENC = 768
EPS = 1e-06
SCALE = (D // HEADS) ** (-0.5)
F32 = jnp.float32
BF16 = jnp.bfloat16

NN = (((1,), (0,)), ((), ()))
NT = (((1,), (1,)), ((), ()))
TN = (((0,), (0,)), ((), ()))


def dot(left, right, dims=NN):
    return lax.dot_general(left, right, dims, preferred_element_type=F32)


def iota(shape, dim):
    return lax.broadcasted_iota(jnp.int32, shape, dim)


def one_hot(hit):
    return jnp.where(hit, 1.0, 0.0).astype(BF16)


def call(kernel, name, out_shape, args, scratch=(), smem=0, flops=0, vmem=16):
    specs = [pl.BlockSpec(memory_space=pltpu.SMEM)] * smem
    specs += [pl.BlockSpec(memory_space=pltpu.VMEM)] * (len(args) - smem)
    outs = [jax.ShapeDtypeStruct(shape, dtype) for shape, dtype in out_shape]
    size = sum(a.size * a.dtype.itemsize for a in args) + sum(
        o.size * o.dtype.itemsize for o in outs
    )
    return pl.pallas_call(
        kernel,
        name=name,
        out_shape=outs,
        in_specs=specs,
        out_specs=[pl.BlockSpec(memory_space=pltpu.VMEM)] * len(outs),
        scratch_shapes=list(scratch),
        compiler_params=pltpu.CompilerParams(vmem_limit_bytes=vmem * 2**20),
        cost_estimate=pl.CostEstimate(flops=flops, bytes_accessed=size, transcendentals=0),
    )(*args)


def pack_kernel(band, pos, enc, out, dest):
    count = pos.shape[1]
    low = iota((count, count), 0)
    high = iota((count, count), 1)
    packed = jnp.zeros((GOT, ENC), F32)
    places = jnp.zeros((SRC, 128), F32)
    for m in range(MICRO):
        cell_r = pos[m : m + 1, :]
        cell_c = jnp.sum(jnp.where(low == high, cell_r, 0), axis=1, keepdims=True)
        slot = LONG * FREQ
        dev_r = jnp.sum(
            jnp.where(cell_r >= slot * iota((SRC, count), 0) + slot, 1, 0), axis=0, keepdims=True
        )
        dev_c = jnp.sum(
            jnp.where(cell_c >= slot * iota((count, SRC), 1) + slot, 1, 0), axis=1, keepdims=True
        )
        same = dev_c == dev_r
        rank_r = jnp.sum(jnp.where(same & (low < high), 1, 0), axis=0, keepdims=True)
        rank_c = jnp.sum(jnp.where(same & (high < low), 1, 0), axis=1, keepdims=True)
        dest[m] = dev_c * BLK + m * CAP + rank_c
        select = one_hot(iota((GOT, count), 0) == dev_r * BLK + m * CAP + rank_r)
        packed = packed + dot(select, enc[m])
        number = cell_r - dev_r * slot - band[0] * CELLS + 1
        to_dev = jnp.where(iota((SRC, count), 0) == dev_r, number.astype(F32), 0.0).astype(BF16)
        to_lane = one_hot(iota((count, 128), 1) == m * CAP + rank_c)
        places = places + dot(to_dev, to_lane)
    spread = one_hot(iota((GOT, SRC), 0) == iota((GOT, SRC), 1) * BLK + (BLK - 4))
    out[:, :128] = (packed[:, :128] + dot(spread, places.astype(BF16))).astype(BF16)
    out[:, 128:] = packed[:, 128:].astype(BF16)


def norm_parts(values):
    center = values - jnp.mean(values, -1, keepdims=True)
    inverse = lax.rsqrt(jnp.mean(center * center, -1, keepdims=True) + EPS)
    return center * inverse, inverse


def norm_back(grad, normal, inverse, gain):
    scaled = grad * gain
    return inverse * (
        scaled
        - jnp.mean(scaled, -1, keepdims=True)
        - normal * jnp.mean(scaled * normal, -1, keepdims=True)
    )


def enter_kernel(
    idx_r, idx_c, got, table, embed_w, qkv_w, vecs, qkv_b,
    hidden_o, normed_o, mixed_o, filled_o, seen_o, cell_o, low_o, high_o,
):
    hit = one_hot(iota((SRC, GOT), 1) == iota((SRC, GOT), 0) * BLK + (BLK - 4))
    numbers = dot(hit, got[:, :128]).astype(BF16)
    spread_r = dot(numbers, one_hot(iota((SRC, GOT), 0) == idx_r[0:1, :]), TN)
    value_r = jnp.sum(
        jnp.where(iota((128, GOT), 0) == idx_r[1:2, :], spread_r, 0.0), axis=0, keepdims=True
    )
    cell_r = jnp.where(
        value_r > 0.5, idx_r[2:3, :] * CELLS + value_r.astype(jnp.int32) - 1, -1
    )
    spread_c = dot(one_hot(iota((GOT, SRC), 1) == idx_c[:, 0:1]), numbers)
    value_c = jnp.sum(
        jnp.where(iota((GOT, 128), 1) == idx_c[:, 1:2], spread_c, 0.0), axis=1, keepdims=True
    )
    cell_o[...] = jnp.where(
        value_c > 0.5, idx_c[:, 2:3] * CELLS + value_c.astype(jnp.int32) - 1, -1
    )
    for m in range(MICRO):
        rows = slice(m * CELLS, (m + 1) * CELLS)
        match = jnp.where(iota((CELLS, GOT), 0) + m * CELLS == cell_r, 1.0, 0.0)
        seen = jnp.sum(match, axis=1, keepdims=True)
        filled = dot(match.astype(BF16), got[...]).astype(BF16)
        filled_o[rows, :] = filled
        seen_o[rows, :] = seen
        proj = (dot(filled, embed_w[...]) + vecs[0:1, :]).astype(BF16).astype(F32)
        hidden = jnp.where(seen > 0.5, proj, vecs[1:2, :]) + table[rows, :]
        hidden_o[rows, :] = hidden
        normal, unused = norm_parts(hidden)
        normed = (normal * vecs[2:3, :] + vecs[3:4, :]).astype(BF16)
        normed_o[rows, :] = normed
        mixed = (dot(normed, qkv_w[...]) + qkv_b[...]).astype(BF16)
        mixed_o[rows, :] = mixed
        low_o[m] = mixed[:16, D:]
        high_o[m] = mixed[CELLS - 16 :, D:]


def head_rows(block, heads):
    return jnp.concatenate([block * heads[h : h + 1, :] for h in range(4)], axis=0)


def own_head(full, lane_head):
    out = full[0:32, :]
    for h in range(1, 4):
        out = jnp.where(lane_head == h, full[32 * h : 32 * h + 32, :], out)
    return out


def window_loop(edge, inner):
    def inside(p, carry):
        places = []
        for m in range(MICRO):
            base = pl.multiple_of(m * CELLS + 32 * p - 16, 16)
            places.append((m * 7 + p, pl.ds(base, 32)))
        inner(places)
        return carry

    def ends(i, carry):
        places = []
        for j in range(2):
            m = 2 * i + j
            first = pl.multiple_of(m * CELLS, 16)
            last = pl.multiple_of(m * CELLS + CELLS - 16, 16)
            places.append((m, m * 7, pl.ds(first, 16), 0))
            places.append((m, m * 7 + 6, pl.ds(last, 16), 1))
        edge(places)
        return carry

    lax.fori_loop(1, 6, inside, 0)
    lax.fori_loop(0, MICRO // 2, ends, 0)


def with_halo(own, halo, side):
    return jnp.concatenate([own, halo] if side else [halo, own], axis=0)


COLS = [[slice(D * i + 128 * g, D * i + 128 * g + 128) for i in range(3)] for g in range(4)]


def load_inner(mixed, places, grads=None):
    items = []
    for w, rows in places:
        for g in range(4):
            item = [mixed[rows, c] for c in COLS[g]]
            items.append((w, g, *item, None if grads is None else grads[rows, COLS[g][0]]))
    return items


def load_edge(mixed, low, high, places, grads=None):
    zero = jnp.zeros((16, 128), BF16)
    items = []
    for m, w, rows, side in places:
        halo = high if side else low
        for g in range(4):
            cols = COLS[g]
            q = with_halo(mixed[rows, cols[0]], zero, side)
            k = with_halo(mixed[rows, cols[1]], halo[m, :, cols[0]], side)
            v = with_halo(mixed[rows, cols[2]], halo[m, :, cols[1]], side)
            grad = None if grads is None else with_halo(grads[rows, cols[0]], zero, side)
            items.append((w, g, q, k, v, grad))
    return items


def attend_kernel(mixed, low, high, mask, heads_i, attended_o, probs_o):
    heads = heads_i[...]
    lane_head = iota((32, 128), 1) // 32

    def windows(items):
        scores = [dot(k, head_rows(q, heads), NT) * SCALE for w, g, q, k, v, _ in items]
        probs = []
        for (w, g, *_), score in zip(items, scores):
            score = jnp.where(mask[w] > 0.5, score, -1e30)
            grown = jnp.exp(score - jnp.max(score, axis=0, keepdims=True))
            one = grown * (1.0 / jnp.sum(grown, axis=0, keepdims=True))
            probs_o[w, :, 128 * g : 128 * g + 128] = one
            probs.append(one.astype(BF16))
        full = [dot(one, item[4], TN) for item, one in zip(items, probs)]
        return [own_head(one, lane_head).astype(BF16) for one in full]

    def inner(places):
        outs = windows(load_inner(mixed, places))
        for i, (w, rows) in enumerate(places):
            for g in range(4):
                attended_o[rows, COLS[g][0]] = outs[4 * i + g]

    def edge(places):
        outs = windows(load_edge(mixed, low, high, places))
        for i, (m, w, rows, side) in enumerate(places):
            for g in range(4):
                out = outs[4 * i + g]
                attended_o[rows, COLS[g][0]] = out[:16] if side else out[16:]

    window_loop(edge, inner)


def gelu_parts(x):
    size = jnp.abs(x) * (0.5**0.5)
    bell = jnp.exp(-0.5 * x * x)
    t = 1.0 / (1.0 + 0.3275911 * size)
    poly = t * (
        0.254829592
        + t * (-0.284496736 + t * (1.421413741 + t * (-1.453152027 + t * 1.061405429)))
    )
    tail = 0.5 * poly * bell
    share = jnp.where(x >= 0, 1.0 - tail, tail)
    return x * share, share + x * bell * 0.3989422804014327


def before_kernel(cot, down_w, g_act_o):
    for f in range(4):
        cols = slice(512 * f, 512 * f + 512)
        g_act_o[:, cols] = dot(cot[...], down_w[cols, :], NT)


def mlp_kernel(
    core, hidden, attended, cot, g_act, out_w, up_w, vecs, up_b,
    middle_o, act_o, gexp_o, keep_o, send_o, n2_s, n2t_s,
):
    tile = 256
    blocks = [slice(512 * f, 512 * f + 512) for f in range(4)]

    def forward(i, carry):
        rows = pl.ds(pl.multiple_of(i * tile, tile), tile)
        middle = hidden[rows, :] + dot(attended[rows, :], out_w[...]) + vecs[0:1, :]
        middle_o[rows, :] = middle
        normal, unused = norm_parts(middle)
        normed = (normal * vecs[1:2, :] + vecs[2:3, :]).astype(BF16)
        n2_s[rows, :] = normed
        expand = [dot(normed, up_w[:, cols]) for cols in blocks]
        for cols, one in zip(blocks, expand):
            value, slope = gelu_parts(one + up_b[0:1, cols])
            act_o[rows, cols] = value.astype(BF16)
            gexp_o[rows, cols] = (g_act[rows, cols] * slope).astype(BF16)
        return carry

    lax.fori_loop(0, ALL // tile, forward, 0)
    n2t_s[...] = jnp.transpose(n2_s[...])
    for grads_o, half in ((keep_o, core[0]), (send_o, 1 - core[0])):
        for b in range(2):
            cols = pl.ds(pl.multiple_of(half * 1024 + 512 * b, 512), 512)
            rows = slice(512 * b, 512 * b + 512)
            grads_o[rows, :] = dot(act_o[:, cols], cot[...], TN).astype(BF16)
            rows = slice(1024 + 512 * b, 1536 + 512 * b)
            grads_o[rows, :] = dot(n2t_s[...], gexp_o[:, cols]).astype(BF16)


def mlp_back_kernel(
    middle_i, attended, cot, act, gexp, out_w, up_w, down_w, vecs,
    output_o, gmid_o, gatt_o, gout_o, sums_o, gb_s,
):
    tile = 256
    sums_o[...] = jnp.zeros((8, D), F32)

    def step(i, carry):
        rows = pl.ds(pl.multiple_of(i * tile, tile), tile)
        middle = middle_i[rows, :]
        grad = dot(gexp[rows, :], up_w[...], NT)
        output_o[rows, :] = (middle + vecs[3:4, :] + dot(act[rows, :], down_w[...])).astype(BF16)
        normal, inverse = norm_parts(middle)
        g_float = cot[rows, :].astype(F32)
        g_mid = g_float + norm_back(grad, normal, inverse, vecs[1:2, :])
        gmid_o[rows, :] = g_mid
        g_low = g_mid.astype(BF16)
        gb_s[rows, :] = g_low
        gatt_o[rows, :] = dot(g_low, out_w[...], NT).astype(BF16)
        sums_o[0:1, :] += jnp.sum(g_low.astype(F32), axis=0, keepdims=True)
        sums_o[1:2, :] += jnp.sum(grad * normal, axis=0, keepdims=True)
        sums_o[2:3, :] += jnp.sum(grad, axis=0, keepdims=True)
        sums_o[3:4, :] += jnp.sum(g_float, axis=0, keepdims=True)
        for f in range(4):
            part = gexp[rows, 512 * f : 512 * f + 512].astype(F32)
            sums_o[4 + f : 5 + f, :] += jnp.sum(part, axis=0, keepdims=True)
        return carry

    lax.fori_loop(0, ALL // tile, step, 0)
    gout_o[...] = dot(attended[...], gb_s[...], TN).astype(BF16)


def attend_back_kernel(
    mixed, low, high, probs_i, gatt, heads_i, gmixed_o, low_o, high_o, rim_o
):
    heads = heads_i[...]
    lane_head = iota((32, 128), 1) // 32

    def windows(items):
        q_m = [head_rows(q, heads) for w, g, q, k, v, grad in items]
        g_m = [head_rows(grad, heads) for w, g, q, k, v, grad in items]
        g_probs = [dot(item[4], one, NT) for item, one in zip(items, g_m)]
        low_probs, g_scores = [], []
        for (w, g, *_), g_prob in zip(items, g_probs):
            probs = probs_i[w, :, 128 * g : 128 * g + 128]
            inner = jnp.sum(probs * g_prob, axis=0, keepdims=True)
            g_scores.append((probs * (g_prob - inner)).astype(BF16))
            low_probs.append(probs.astype(BF16))
        d_value = [dot(one, grad) for one, grad in zip(low_probs, g_m)]
        d_key = [dot(one, q) * SCALE for one, q in zip(g_scores, q_m)]
        full = [dot(one, item[3], TN) for item, one in zip(items, g_scores)]
        d_query = [(own_head(one, lane_head) * SCALE).astype(BF16) for one in full]
        return list(zip(d_query, d_key, d_value))

    def inner(places):
        outs = windows(load_inner(mixed, places, gatt))
        for i, (w, rows) in enumerate(places):
            for g in range(4):
                for col, value in zip(COLS[g], outs[4 * i + g]):
                    gmixed_o[rows, col] = value.astype(BF16)

    def edge(places):
        outs = windows(load_edge(mixed, low, high, places, gatt))
        for i, (m, w, rows, side) in enumerate(places):
            out = high_o if side else low_o
            own, far = (slice(0, 16), slice(16, 32)) if side else (slice(16, 32), slice(0, 16))
            for g in range(4):
                cols = COLS[g]
                d_query, d_key, d_value = outs[4 * i + g]
                gmixed_o[rows, cols[0]] = d_query[own]
                rim_o[m, side, :, cols[0]] = d_key[own]
                rim_o[m, side, :, cols[1]] = d_value[own]
                out[m, :, cols[0]] = d_key[far].astype(BF16)
                out[m, :, cols[1]] = d_value[far].astype(BF16)

    window_loop(edge, inner)
    for m in range(MICRO):
        for base in (m * CELLS, m * CELLS + CELLS - 16):
            gmixed_o[base : base + 16, D:] = jnp.zeros((16, 2 * D), BF16)


def leave_kernel(
    core, gmixed, from_low, from_high, rim, hidden, normed, filled, seen, cell, gmid, qkv_w, vecs,
    gout, sums, keep_o, send_o, ret_o, gm_s, gf_s, nt_s, ft_s,
):
    small = jnp.zeros((1, D), F32)
    gain_sum, shift_sum, mask_sum, embed_sum, query_sum, value_sum = [small] * 6
    for m in range(MICRO):
        base = m * CELLS
        rows = slice(base, base + CELLS)
        gm_s[rows, :] = gmixed[rows, :]
        gm_s[base : base + 16, D:] = (rim[m, 0] + from_low[m].astype(F32)).astype(BF16)
        gm_s[base + CELLS - 16 : base + CELLS, D:] = (rim[m, 1] + from_high[m].astype(F32)).astype(
            BF16
        )
        gm = gm_s[rows, :]
        grad = dot(gm, qkv_w[...], NT)
        normal, inverse = norm_parts(hidden[rows, :])
        g_hidden = gmid[rows, :] + norm_back(grad, normal, inverse, vecs[2:3, :])
        there = seen[rows, :] > 0.5
        g_low = g_hidden.astype(BF16)
        gf_s[rows, :] = g_low
        gain_sum += jnp.sum(grad * normal, axis=0, keepdims=True)
        shift_sum += jnp.sum(grad, axis=0, keepdims=True)
        mask_sum += jnp.sum(jnp.where(there, 0.0, g_hidden), axis=0, keepdims=True)
        embed_sum += jnp.sum(jnp.where(there, g_low.astype(F32), 0.0), axis=0, keepdims=True)
        query_sum += jnp.sum(gm[:, :D].astype(F32), axis=0, keepdims=True)
        value_sum += jnp.sum(gm[:, 2 * D :].astype(F32), axis=0, keepdims=True)
    nt_s[...] = jnp.transpose(normed[...])
    ft_s[...] = jnp.transpose(filled[...])
    ret_o[...] = dot(one_hot(iota((GOT, ALL), 1) == cell[...]), gf_s[...]).astype(BF16)


    def write(first, second):
        def weights(b, carry):
            cols = pl.ds(pl.multiple_of(b * 512, 512), 512)
            first[cols, :] = dot(nt_s[...], gm_s[:, cols]).astype(BF16)
            return carry

        lax.fori_loop(0, 3, weights, 0)
        second[0:512, :] = gout[...]
        second[512:1280, :] = dot(ft_s[...], gf_s[...]).astype(BF16)
        second[1280:1296, :] = jnp.concatenate(
            [
                embed_sum, mask_sum, gain_sum, shift_sum, query_sum, value_sum,
                small, small, sums[...],
            ],
            axis=0,
        ).astype(BF16)
        second[1296:1536, :] = jnp.zeros((240, D), BF16)

    @pl.when(core[0] == 0)
    def _():
        write(keep_o, send_o)

    @pl.when(core[0] != 0)
    def _():
        write(send_o, keep_o)


def return_kernel(dest, came, embed_w, out):
    for m in range(MICRO):
        select = one_hot(iota((dest.shape[1], GOT), 1) == dest[m])
        g_proj = dot(select, came[...]).astype(BF16)
        out[m] = dot(g_proj, embed_w[...], NT).astype(BF16)


def unpack_one_kernel(down_i, up_i, down_o, up_o):
    down_o[...] = down_i[...].reshape(512, D).astype(F32)
    up_o[...] = up_i[...].reshape(512, D).astype(F32)


def unpack_one(gathered):
    block = (16, 1, 32, D)
    return pl.pallas_call(
        unpack_one_kernel,
        name="unpack_one",
        grid=(4,),
        out_shape=[jax.ShapeDtypeStruct((FF, D), F32), jax.ShapeDtypeStruct((D, FF), F32)],
        in_specs=[
            pl.BlockSpec(block, lambda i: (i % 2, i // 2, 0, 0)),
            pl.BlockSpec(block, lambda i: (2 + i % 2, i // 2, 0, 0)),
        ],
        out_specs=[
            pl.BlockSpec((512, D), lambda i: (i, 0)),
            pl.BlockSpec((512, D), lambda i: (0, i)),
        ],
        compiler_params=pltpu.CompilerParams(vmem_limit_bytes=16 * 2**20),
        cost_estimate=pl.CostEstimate(flops=0, bytes_accessed=12 * 2**20, transcendentals=0),
    )(gathered, gathered)


def unpack_two_kernel(core, mine, other, qkv_o, embed_o, out_o, small_o):
    def write(first, second):
        for b in range(3):
            qkv_o[:, 512 * b : 512 * b + 512] = first[512 * b : 512 * b + 512, :].astype(F32)
        out_o[...] = second[0:512, :].astype(F32)
        embed_o[...] = second[512:1280, :].astype(F32)
        small_o[...] = second[1280:1296, :].astype(F32)

    @pl.when(core[0] == 0)
    def _():
        write(mine, other)

    @pl.when(core[0] != 0)
    def _():
        write(other, mine)


def clip_ident(lengths, rows):
    first = lengths[:, 0:1]
    second = first + lengths[:, 1:2]
    ident = (rows[None, :] >= first).astype(jnp.int32) + (rows[None, :] >= second).astype(jnp.int32)
    start = jnp.where(ident >= 1, first, 0) + jnp.where(ident >= 2, lengths[:, 1:2], 0)
    inside = (rows >= 0) & (rows < LONG)
    return (jnp.where(inside[None, :], ident, -1), rows[None, :] - start)


def position_table(row_in_clip, width):
    quarter = width // 4
    omega = 1.0 / 10000.0 ** (jnp.arange(quarter, dtype=jnp.float32) / quarter)
    row_angle = row_in_clip.astype(jnp.float32)[..., None] * omega
    freq_angle = jnp.arange(FREQ, dtype=jnp.float32)[:, None] * omega
    row_part = jnp.concatenate([jnp.sin(row_angle), jnp.cos(row_angle)], -1)
    freq_part = jnp.concatenate([jnp.sin(freq_angle), jnp.cos(freq_angle)], -1)
    shape = row_in_clip.shape + (FREQ, width // 2)
    return jnp.concatenate(
        [jnp.broadcast_to(row_part[..., None, :], shape), jnp.broadcast_to(freq_part, shape)], -1
    )


def window_mask(ident):
    cells = jnp.repeat(ident.reshape(MICRO * 7, 4), FREQ, axis=1)
    freq = np.tile((np.arange(FREQ) + 2) % 8 // 4, 4)
    same = (cells[:, :, None] == cells[:, None, :]) & (cells[:, :, None] >= 0)
    same = same & jnp.asarray(freq[:, None] == freq[None, :])[None]
    return jnp.tile(same.astype(F32), (1, 1, 4))


def on_device(
    encoded, visible_pos, clip_len, cotangent, embed_weight, embed_bias, mask_token, attn_gain,
    attn_shift, qkv_weight, query_bias, value_bias, out_weight, out_bias, mlp_gain, mlp_shift,
    up_weight, up_bias, down_weight, down_bias,
):
    both = ("clip", "band")
    groups = lax.axis_size("clip")
    bands = lax.axis_size("band")
    band = lax.axis_index("band")
    side = band % 2
    core = side.astype(jnp.int32).reshape(1)
    halves = [
        [c * bands + 2 * x + k for c in range(groups) for x in range(bands // 2)] for k in range(2)
    ]
    swap = [(i, i ^ 1) for i in range(bands)]
    forward = [(i, i + 1) for i in range(bands - 1)]
    backward = [(b, a) for a, b in forward]
    chips = groups * bands // 2

    def to_all(block):
        return lax.all_to_all(
            block, both, split_axis=0, concat_axis=0, tiled=True, axis_index_groups=halves
        )

    def chip_sum(keep, send):
        other = lax.ppermute(send, "band", swap)
        mine = (keep.astype(F32) + other.astype(F32)).astype(BF16)
        return mine.reshape(chips, -1, D)

    def total(parts):
        return jnp.sum(parts.astype(F32), 0).astype(BF16)

    vis = visible_pos.shape[1]
    packed, dest = call(
        pack_kernel, "pack", [((GOT, ENC), BF16), ((MICRO, vis, 1), jnp.int32)],
        (band.astype(jnp.int32).reshape(1), visible_pos, encoded), smem=1,
        flops=GOT * MICRO * vis * ENC * 2,
    )
    cot = cotangent.reshape(ALL, D)
    (g_act,) = call(
        before_kernel, "before", [((ALL, FF), F32)], (cot, down_weight), flops=2 * ALL * D * FF,
    )
    got = lax.all_to_all(
        packed.reshape(SRC, BLK, ENC), "clip", split_axis=0, concat_axis=0, tiled=True
    ).reshape(GOT, ENC)

    place = np.arange(GOT)
    within = place % BLK
    index = np.zeros((8, GOT), np.int32)
    index[0], index[1], index[2] = place // BLK, within, np.where(within < 36, within // CAP, 99)
    heads = jnp.asarray(np.arange(128)[None, :] // 32 == np.arange(16)[:, None] % 4, BF16)

    unused, row_in_clip = clip_ident(clip_len[:, 0], band * ROWS + jnp.arange(ROWS))
    table = position_table(row_in_clip, D).reshape(ALL, D)
    ident_ext, unused = clip_ident(clip_len[:, 0], band * ROWS - 2 + jnp.arange(ROWS + 4))
    mask = window_mask(ident_ext)
    zero = jnp.zeros((D,), BF16)
    vecs_one = jnp.stack([embed_bias, mask_token, attn_gain, attn_shift] * 2).astype(F32)
    vecs_two = jnp.stack([out_bias, mlp_gain, mlp_shift, down_bias] * 2).astype(F32)
    qkv_b = jnp.concatenate([query_bias, zero, value_bias]).astype(F32)[None]
    up_b = up_bias.astype(F32)[None]

    hidden, normed, mixed, filled, seen, cell, low, high = call(
        enter_kernel, "enter",
        [
            ((ALL, D), F32), ((ALL, D), BF16), ((ALL, 3 * D), BF16), ((ALL, ENC), BF16),
            ((ALL, 1), F32), ((GOT, 1), jnp.int32),
            ((MICRO, 16, 2 * D), BF16), ((MICRO, 16, 2 * D), BF16),
        ],
        (
            jnp.asarray(index), jnp.asarray(np.ascontiguousarray(index.T)), got, table,
            embed_weight, qkv_weight, vecs_one, qkv_b,
        ),
        flops=2 * ALL * (GOT * ENC + ENC * D + 3 * D * D),
    )
    from_low = lax.ppermute(high, "band", forward)
    from_high = lax.ppermute(low, "band", backward)
    attended, probs = call(
        attend_kernel, "attend",
        [((ALL, D), BF16), ((MICRO * 7, 32, D), F32)],
        (mixed, from_low, from_high, mask, heads),
        flops=MICRO * 7 * 4 * 2**20,
    )
    middle, act, gexp, keep, send = call(
        mlp_kernel, "mlp",
        [
            ((ALL, D), F32), ((ALL, FF), BF16), ((ALL, FF), BF16), ((FF, D), BF16), ((FF, D), BF16),
        ],
        (core, hidden, attended, cot, g_act, out_weight, up_weight, vecs_two, up_b),
        scratch=[pltpu.VMEM((ALL, D), BF16), pltpu.VMEM((D, ALL), BF16)],
        smem=1, flops=2 * ALL * (3 * D * FF + D * D), vmem=24,
    )
    chip_one = chip_sum(keep, send)
    act, chip_one = lax.optimization_barrier((act, chip_one))
    output, gmid, gatt, gout, sums = call(
        mlp_back_kernel, "mlp_back",
        [
            ((ALL, D), BF16), ((ALL, D), F32), ((ALL, D), BF16), ((D, D), BF16), ((8, D), F32),
        ],
        (middle, attended, cot, act, gexp, out_weight, up_weight, down_weight, vecs_two),
        scratch=[pltpu.VMEM((ALL, D), BF16)],
        flops=2 * ALL * (2 * D * FF + 2 * D * D), vmem=24,
    )
    parts_one = to_all(chip_one)
    gmixed, low, high, rim = call(
        attend_back_kernel, "attend_back",
        [
            ((ALL, 3 * D), BF16), ((MICRO, 16, 2 * D), BF16), ((MICRO, 16, 2 * D), BF16),
            ((MICRO, 2, 16, 2 * D), F32),
        ],
        (mixed, from_low, from_high, probs, gatt, heads),
        flops=MICRO * 7 * 4 * 2**22,
    )
    from_low = lax.ppermute(high, "band", forward)
    from_high = lax.ppermute(low, "band", backward)
    keep, send, returned = call(
        leave_kernel, "leave",
        [((3 * D, D), BF16), ((3 * D, D), BF16), ((GOT, D), BF16)],
        (
            core, gmixed, from_low, from_high, rim, hidden, normed, filled, seen, cell, gmid,
            qkv_weight, vecs_one, gout, sums,
        ),
        scratch=[
            pltpu.VMEM((ALL, 3 * D), BF16), pltpu.VMEM((ALL, D), BF16),
            pltpu.VMEM((D, ALL), BF16), pltpu.VMEM((ENC, ALL), BF16),
        ],
        smem=1, flops=2 * ALL * (6 * D * D + GOT * D + ENC * D),
    )
    parts_one, chip_two = lax.optimization_barrier((parts_one, chip_sum(keep, send)))
    total_one = lax.all_gather(total(parts_one), both, axis=0).reshape(chips, 2, -1, D)
    mine = total(to_all(chip_two))
    mine = to_all(jnp.broadcast_to(mine[None], (chips,) + mine.shape)).reshape(-1, D)
    mine, returned = lax.optimization_barrier((mine, returned))
    other = lax.ppermute(mine, "band", swap)
    qkv, g_embed, g_out, small = call(
        unpack_two_kernel, "unpack_two",
        [((D, 3 * D), F32), ((ENC, D), F32), ((D, D), F32), ((16, D), F32)],
        (core, mine, other), smem=1,
    )
    came = lax.all_to_all(
        returned.reshape(SRC, BLK, D), "clip", split_axis=0, concat_axis=0, tiled=True
    ).reshape(GOT, D)
    (grad_enc,) = call(
        return_kernel, "return", [((MICRO, vis, ENC), BF16)], (dest, came, embed_weight),
        flops=2 * MICRO * vis * D * (GOT + ENC),
    )
    down, up = unpack_one(total_one)
    return (
        output.reshape(cotangent.shape), grad_enc, g_embed, small[0], small[1], small[2],
        small[3], qkv, small[4], small[5], g_out, small[8], small[9], small[10], up,
        small[12:16].reshape(FF), down, small[11],
    )


def solution(mesh):
    whole = P()
    return jax.shard_map(
        on_device,
        mesh=mesh,
        in_specs=(
            P(None, ("clip", "band"), None),
            P(None, ("clip", "band")),
            P(None, "clip", None),
            P(None, "clip", "band", None, None),
        )
        + (whole,) * 16,
        out_specs=(P(None, "clip", "band", None, None), P(None, ("clip", "band"), None))
        + (whole,) * 16,
        check_vma=False,
    )
```

time: 282 us -> 244 us (0.87)
  Pallas kernels: 89.7 us -> 53.6 us
  waiting for transfers between devices: 36.4 us -> 51.6 us
  other arithmetic: 22.9 us -> 8.96 us
  local copies, waits for them, and re-layouts: 19.9 us -> 10.8 us
  blocking collectives: 62 us -> 70.7 us
    pallas_call x7 -> x10, Pallas kernels: 89.7 us -> 49.9 us  [call(): pl.pallas_call(kernel, name=name, out_shape=outs, in_specs=specs, out_spe...]
    all_to_all x1, waiting for transfers between devices: 0.01 us -> 26.3 us  [to_all(): lax.all_to_all(block, both, split_axis=0, concat_axis=0, tiled=True, axis...]
    all_to_all x0 -> x1, blocking collectives: none -> 15.7 us  [on_device(): lax.all_to_all(returned.reshape(SRC, BLK, D), 'clip', split_axis=0, conca...]
    all_to_all x1 -> x0, waiting for transfers between devices: 14 us -> none  [on_device(): lax.all_to_all(returned.reshape(SRC, BLK, D), 'clip', split_axis=0, conca...]
    all_to_all x2, blocking collectives: 62 us -> 54.9 us  [to_all(): lax.all_to_all(block, both, split_axis=0, concat_axis=0, tiled=True, axis...]
    concatenate x3 -> x0, other arithmetic: 6.81 us -> none  [the longest x1 2.55 us: on_device(): down = jnp.concatenate([half_one[0][:1024], half_one[1][:1024]], 0)]
    slice x7 -> x0, local copies, waits for them, and re-layouts: 4.71 us -> none  [the longest x1 1.26 us: on_device(): rest[512:1280]]
    squeeze x2 -> x0, local copies, waits for them, and re-layouts: 4.53 us -> none  [chip_sum(): other = lax.ppermute(grads[1], 'band', swap)]
  transfers between devices with their start and end apart: 11 -> 10, of which waited for: 7 -> 6; matrix products, arithmetic and copies ran while one was open for 7% -> 4% of each run, Pallas kernels for 13% -> 3%
where the time goes in v2:
time: 244 us; the launch traced here: 243 us
  blocking collectives  70.7 us (29%)
  Pallas kernels  53.6 us (22%)
  waiting for transfers between devices  51.6 us (21%)
  starting transfers between devices  32.4 us (13%)
  between operations  14.7 us (6%)
  local copies, waits for them, and re-layouts  10.8 us (4%)
  other arithmetic  8.96 us (4%)
    all_to_all x2, blocking collectives, to_all(): lax.all_to_all(block, both, split_axis=0, concat_axis=0, tiled=True, axis...  54.9 us
    pallas_call x10, Pallas kernels, call(): pl.pallas_call(kernel, name=name, out_shape=outs, in_specs=specs, out_spe...  49.9 us
    all_to_all x1, waiting for transfers between devices, to_all(): lax.all_to_all(block, both, split_axis=0, concat_axis=0, tiled=True, axis...  26.3 us
    all_to_all x1, blocking collectives, on_device(): lax.all_to_all(returned.reshape(SRC, BLK, D), 'clip', split_axis=0, conca...  15.7 us
    all_to_all x1, waiting for transfers between devices, on_device(): lax.all_to_all(packed.reshape(SRC, BLK, ENC), 'clip', split_axis=0, conca...  11.1 us
    ppermute x2, starting transfers between devices, on_device(): from_low = lax.ppermute(high, 'band', forward)  9.19 us
    all_to_all x1, starting transfers between devices, on_device(): lax.all_to_all(packed.reshape(SRC, BLK, ENC), 'clip', split_axis=0, conca...  8.6 us
    unnamed x57, local copies, waits for them, and re-layouts  8.04 us
  transfers between devices with their start and end apart: 10, of which 6 were waited for; matrix products, arithmetic and copies ran while one was open for 4% of the time, Pallas kernels for 3%

profile of v2, /device:TPU:1, one launch (start us, length us, event | category | flops | bytes accessed | tf_op | source)
XLA Modules:
  0.0 242.8 jit_solution(1019605139217292324)
XLA Ops:
  7.3 1.0 copy.47.enc
  8.4 0.7 copy-done.10
  9.1 2.5 %pack.1 = (bf16[640,768]{1,0:T(8,128)(2,1)}, s32[4,38,1]{2,1,0:T(8,128)S(1)}) custom-call(s32[1]{0:T(128)} %bitcast.1.band, s32[4,38]{1,0:T(4,128)S(1)} %copy-done.10, bf16[4,38,768]{2,1,0:T(8,128)(2,1)S(1)} %copy.47.enc), custom_call_target="tpu_custom_call" | custom-call | flops 149422080 | bytes 1217732 | tf_op jit(solution)/shard_map/pack/pallas_call | solution.py:52
  11.5 8.6 %all-to-all-start = ((bf16[16,40,768]{2,1,0:T(8,128)(2,1)}), bf16[16,40,768]{2,1,0:T(8,128)(2,1)S(1)}, u32[]{:S(2)}, u32[]{:S(2)}) async-start(bf16[16,40,768]{2,1,0:T(8,128)(2,1)} %bitcast.2), calls=%async_computation | async-start | bytes 1966080 | tf_op jit(solution)/shard_map/all_to_all | solution.py:559
  20.3 0.1 copy.48
  20.4 0.2 slice_reduce_fusion.1
  21.3 0.1 copy.51
  21.6 0.3 and_convert_fusion
  21.9 0.3 tile.4
  22.3 0.8 tile.10.mask
  23.2 0.3 multiply_sine_fusion
  23.6 0.2 pad_maximum_fusion
  23.9 11.1 %all-to-all-done = bf16[16,40,768]{2,1,0:T(8,128)(2,1)S(1)} async-done(((bf16[16,40,768]{2,1,0:T(8,128)(2,1)}), bf16[16,40,768]{2,1,0:T(8,128)(2,1)S(1)}, u32[]{:S(2)}, u32[]{:S(2)}) %all-to-all-start) | async-done | bytes 983072 | tf_op jit(solution)/shard_map/all_to_all | solution.py:559
  34.9 1.1 copy-done.3
  36.0 1.4 copy-done.7
  37.5 5.0 %enter.1 = (f32[768,512]{1,0:T(8,128)S(1)}, bf16[768,512]{1,0:T(8,128)(2,1)S(1)}, bf16[768,1536]{1,0:T(8,128)(2,1)S(1)}, bf16[768,768]{1,0:T(8,128)(2,1)S(1)}, f...) custom-call(s32[8,640]{1,0:T(8,128)S(1)} %copy-done.12, ...), custom_call_target="tpu_custom_call" | custom-call | flops 2566914048 | bytes 11144704 | tf_op jit(solution)/shard_map/enter/pallas_call | solution.py:52
  42.5 6.1 %collective-permute-start = (bf16[4,16,1024]{2,1,0:T(8,128)(2,1)S(1)}, bf16[4,16,1024]{2,1,0:T(8,128)(2,1)S(1)}, u32[]{:S(2)}, u32[]{:S(2)}) collective-permute-start(bf16[4,16,1024]{2,1,0:T(8,128)(2,1)S(1)} %get-tuple-element.62), channel_id=1, source_target_pairs={{0,1},{1,2},{2,3},{3,4},{4,5},{5,6},{6,7},{8,9},{9,10},{10,11},{11... | collective-permute-start | bytes 393224 | tf_op jit(solution)/shard_map/ppermute | solution.py:592
  48.6 2.1 collective-permute-start.1
  50.7 1.8 before.1.g_act
  52.6 2.3 collective-permute-done.1.high
  54.8 4.7 %attend.1 = (bf16[768,512]{1,0:T(8,128)(2,1)S(1)}, f32[28,32,512]{2,1,0:T(8,128)S(1)}) custom-call(bf16[768,1536]{1,0:T(8,128)(2,1)S(1)} %get-tuple-element.61.mixed, bf16[4,16,1024]{2,1,0:T(8,128)(2,1)S(1)} %collective-permute-done.low, bf16[4,16,1024]{2,1,0:T(8,128)(2,1)S(1)} %collective-permute-done.1.high, f32[28,32,128]{2,1,0:T(8,128)S(1)} %tile.10.mask, ...), custom_call_target="tpu_custom_call" | custom-call | flops 117440512 | bytes 5705728 | tf_op jit(solution)/shard_map/attend/pallas_call | solution.py:52
  59.6 12.2 %mlp.1 = (f32[768,512]{1,0:T(8,128)S(1)}, bf16[768,2048]{1,0:T(8,128)(2,1)S(1)}, bf16[768,2048]{1,0:T(8,128)(2,1)S(1)}, bf16[2048,512]{1,0:T(8,128)(2,1)S(1)}, bf16[2048,512]{1,0:T(8,128)(2,1)S(1)}) custom-call(s32[1]{0:T(128)} %bitcast.core, f32[768,512]{1,0:T(8,128)S(1)} %get-tuple-element.60.hidden, bf16[768,512]{1,0:T(8,128)(2,1)S(1)} %get-tuple-element.64.attended, ...), custom_call_target="tpu_custom_call" | custom-call | flops 5234491392 | bytes 24141828 | tf_op jit(solution)/shard_map/mlp/pallas_call | solution.py:52
  71.9 4.1 %collective-permute-done.2 = bf16[2048,512]{1,0:T(8,128)(2,1)S(1)} collective-permute-done((bf16[2048,512]{1,0:T(8,128)(2,1)S(1)}, bf16[2048,512]{1,0:T(8,128)(2,1)S(1)}, u32[]{:S(2)}, u32[]{:S(2)}) %collective-permute-start.2) | collective-permute-done | bytes 2097184 | tf_op jit(solution)/shard_map/ppermute | solution.py:542
  76.1 2.0 add_convert_fusion
  78.1 6.3 %mlp_back.1 = (bf16[768,512]{1,0:T(8,128)(2,1)}, f32[768,512]{1,0:T(8,128)S(1)}, bf16[768,512]{1,0:T(8,128)(2,1)S(1)}, bf16[512,512]{1,0:T(8,128)(2,1)S(1)}, f32[8,512]{1,0:T(8,128)S(1)}) custom-call(f32[768,512]{1,0:T(8,128)S(1)} %get-tuple-element.65.middle_i, bf16[768,512]{1,0:T(8,128)(2,1)S(1)} %get-tuple-element.64.attended, ...), custom_call_target="tpu_custom_call" | custom-call | flops 4026531840 | bytes 17858560 | tf_op jit(solution)/shard_map/mlp_back/pallas_call | solution.py:52
  84.4 5.8 %attend_back.1 = (bf16[768,1536]{1,0:T(8,128)(2,1)S(1)}, bf16[4,16,1024]{2,1,0:T(8,128)(2,1)S(1)}, bf16[4,16,1024]{2,1,0:T(8,128)(2,1)S(1)}, f32[4,2,16,1024]{3,2,1,0:T(8,128)S(1)}) custom-call(bf16[768,1536]{1,0:T(8,128)(2,1)S(1)} %get-tuple-element.61.mixed, bf16[4,16,1024]{2,1,0:T(8,128)(2,1)S(1)} %collective-permute-done.low, ...), custom_call_target="tpu_custom_call" | custom-call | flops 469762048 | bytes 8392704 | tf_op jit(solution)/shard_map/attend_back/pallas_call | solution.py:52
  90.2 3.1 %collective-permute-start.3 = (bf16[4,16,1024]{2,1,0:T(8,128)(2,1)S(1)}, bf16[4,16,1024]{2,1,0:T(8,128)(2,1)S(1)}, u32[]{:S(2)}, u32[]{:S(2)}) collective-permute-start(bf16[4,16,1024]{2,1,0:T(8,128)(2,1)S(1)} %get-tuple-element.77), channel_id=1, source_target_pairs={{0,1},{1,2},{2,3},{3,4},{4,5},{5,6},{6,7},{8,9},{9,10},{10,11},{11... | collective-permute-start | bytes 393224 | tf_op jit(solution)/shard_map/ppermute | solution.py:630
  93.3 2.1 collective-permute-start.4
  95.5 4.1 %collective-permute-done.4.from_high = bf16[4,16,1024]{2,1,0:T(8,128)(2,1)S(1)} collective-permute-done((bf16[4,16,1024]{2,1,0:T(8,128)(2,1)S(1)}, bf16[4,16,1024]{2,1,0:T(8,128)(2,1)S(1)}, u32[]{:S(2)}, u32[]{:S(2)}) %collective-permute-start.4) | collective-permute-done | bytes 131104 | tf_op jit(solution)/shard_map/ppermute | solution.py:631
  99.6 7.1 %leave.1 = (bf16[1536,512]{1,0:T(8,128)(2,1)S(1)}, bf16[1536,512]{1,0:T(8,128)(2,1)}, bf16[640,512]{1,0:T(8,128)(2,1)S(1)}) custom-call(s32[1]{0:T(128)} %bitcast.core, bf16[768,1536]{1,0:T(8,128)(2,1)S(1)} %get-tuple-element.76.gmixed, bf16[4,16,1024]{2,1,0:T(8,128)(2,1)S(1)} %collective-permute-done.3.from_low, ...), custom_call_target="tpu_custom_call" | custom-call | flops 3523215360 | bytes 14194180 | tf_op jit(solution)/shard_map/leave/pallas_call | solution.py:52
  106.7 5.6 %all-to-all-start.1 = ((bf16[64,32,512]{2,1,0:T(8,128)(2,1)}), bf16[64,32,512]{2,1,0:T(8,128)(2,1)}, u32[]{:S(2)}, u32[]{:S(2)}) async-start(bf16[64,32,512]{2,1,0:T(8,128)(2,1)} %bitcast.50), calls=%async_computation.1 | async-start | bytes 4194304 | tf_op jit(solution)/shard_map/all_to_all | solution.py:537
  112.4 3.0 %add_convert_fusion.1 = bf16[1536,512]{1,0:T(8,128)(2,1)} fusion(bf16[1536,512]{1,0:T(8,128)(2,1)} %collective-permute-done.5, bf16[1536,512]{1,0:T(8,128)(2,1)S(1)} %get-tuple-element.87), kind=kLoop, calls=%fused_computation.1 | loop fusion | flops 3145728 | bytes 4718592 | tf_op jit(solution)/shard_map/convert_element_type | solution.py:543
  115.4 26.3 %all-to-all-done.1 = bf16[64,32,512]{2,1,0:T(8,128)(2,1)} async-done(((bf16[64,32,512]{2,1,0:T(8,128)(2,1)}), bf16[64,32,512]{2,1,0:T(8,128)(2,1)}, u32[]{:S(2)}, u32[]{:S(2)}) %all-to-all-start.1) | async-done | bytes 2097184 | tf_op jit(solution)/shard_map/all_to_all | solution.py:537
  141.6 2.5 %reduce_sum.25 = bf16[32,512]{1,0:T(8,128)(2,1)} reduce(bf16[64,32,512]{2,1,0:T(8,128)(2,1)} %all-to-all-done.1, bf16[]{:T(256)} %constant.47.clone.1), dimensions={0}, to_apply=%region_1.2 | reduce | flops 1032192 | bytes 2129922 | tf_op jit(solution)/shard_map/reduce_sum | solution.py:547
  144.2 28.2 %all_to_all.25 = bf16[64,24,512]{2,1,0:T(8,128)(2,1)S(1)} all-to-all(bf16[64,24,512]{2,1,0:T(8,128)(2,1)} %bitcast.51), channel_id=1, replica_groups={{0,2,4,6,8,10,12,14,16,18,20,22,24,26,28,30,32,34,36,38,40,42,44,46,48,..., dimensions={0} | all-to-all | bytes 3145728 | tf_op jit(solution)/shard_map/all_to_all | solution.py:537
  172.4 0.2 reduce_sum.24
  172.7 0.1 broadcast_in_dim.79
  172.8 26.7 %all_to_all.26 = bf16[64,24,512]{2,1,0:T(8,128)(2,1)S(1)} all-to-all(bf16[64,24,512]{2,1,0:T(8,128)(2,1)S(1)} %broadcast_in_dim.79), channel_id=1, replica_groups={{0,2,4,6,8,10,12,14,16,18,20,22,24,26,28,30,32,34,36,38,40,42,44,46,48,..., dimensions={0} | all-to-all | bytes 3145728 | tf_op jit(solution)/shard_map/all_to_all | solution.py:537
  199.5 4.7 %collective-permute-start.6 = (bf16[1536,512]{1,0:T(8,128)(2,1)S(1)}, bf16[1536,512]{1,0:T(8,128)(2,1)S(1)}, u32[]{:S(2)}, u32[]{:S(2)}) collective-permute-start(bf16[1536,512]{1,0:T(8,128)(2,1)S(1)} %bitcast.40), channel_id=1, source_target_pairs={{0,1},{1,0},{2,3},{3,2},{4,5},{5,4},{6,7},{7,6},{8,9},{9,8},{10,11... | collective-permute-start | bytes 4718600 | tf_op jit(solution)/shard_map/ppermute | solution.py:650
  204.2 15.7 %all_to_all.27 = bf16[16,40,512]{2,1,0:T(8,128)(2,1)S(1)} all-to-all(bf16[16,40,512]{2,1,0:T(8,128)(2,1)S(1)} %bitcast.48), channel_id=1, replica_groups=mesh['clip'=16,'band'=8] {'clip'}, dimensions={0} | all-to-all | bytes 1310720 | tf_op jit(solution)/shard_map/all_to_all | solution.py:656
  219.9 1.5 return.1
  221.5 0.8 copy.53
  222.2 2.9 %unpack_two.1 = (f32[512,1536]{1,0:T(8,128)}, f32[768,512]{1,0:T(8,128)}, f32[512,512]{1,0:T(8,128)}, f32[16,512]{1,0:T(8,128)S(1)}) custom-call(s32[1]{0:T(128)} %bitcast.core, bf16[1536,512]{1,0:T(8,128)(2,1)S(1)} %bitcast.41, bf16[1536,512]{1,0:T(8,128)(2,1)S(1)} %collective-permute-done.6.other), custom_call_target="tpu_custom_call" | custom-call | bytes 8945668 | tf_op jit(solution)/shard_map/unpack_two/pallas_call | solution.py:52
  225.2 0.6 copy.54
  225.8 0.6 fusion.6
  226.4 3.7 %all-gather.3.cloned.1.call-done = bf16[4096,512]{1,0:T(8,128)(2,1)} async-done(((bf16[32,512]{1,0:T(8,128)(2,1)}), bf16[4096,512]{1,0:T(8,128)(2,1)}) %all-gather.3.cloned.1.call-update) | async-done | bytes 4194320 | tf_op jit(solution)/shard_map/all_gather | solution.py:646
  230.1 2.2 copy-done
  232.3 3.7 %unpack_one.1 = (f32[2048,512]{1,0:T(8,128)}, f32[512,2048]{1,0:T(8,128)}) custom-call(bf16[64,2,32,512]{3,2,1,0:T(8,128)(2,1)S(1)} %bitcast.38, bf16[64,2,32,512]{3,2,1,0:T(8,128)(2,1)S(1)} %bitcast.39), custom_call_target="tpu_custom_call" | custom-call | bytes 12582912 | tf_op jit(solution)/shard_map/unpack_one/pallas_call | solution.py:452
  (97 shorter events, 1.3 us)
Async XLA Ops:
  7.2 14.4 %copy-start.13 = (pred[32,32]{1,0:T(32,128)(4,1)S(1)}, pred[32,32]{1,0:T(32,128)(4,1)}, u32[]{:S(2)}) copy-start(pred[32,32]{1,0:T(32,128)(4,1)} %constant.53.clone) | copy-start | bytes 3076
  7.2 13.1 %copy-start.15 = (s32[4,1,3]{0,1,2:T(1,128)S(1)}, s32[4,1,3]{0,1,2:T(1,128)}, u32[]{:S(2)}) copy-start(s32[4,1,3]{0,1,2:T(1,128)} %param.26) | copy-start | bytes 148
  7.2 13.8 %copy-start.16 = (bf16[512]{0:T(512)(128)(2,1)S(1)}, bf16[512]{0:T(512)(128)(2,1)}, u32[]{:S(2)}) copy-start(bf16[512]{0:T(512)(128)(2,1)} %param.29) | copy-start | bytes 3076
  7.2 13.8 %copy-start.17 = (bf16[512]{0:T(512)(128)(2,1)S(1)}, bf16[512]{0:T(512)(128)(2,1)}, u32[]{:S(2)}) copy-start(bf16[512]{0:T(512)(128)(2,1)} %param.30) | copy-start | bytes 3076
  7.2 13.9 %copy-start.18 = (bf16[512]{0:T(512)(128)(2,1)S(1)}, bf16[512]{0:T(512)(128)(2,1)}, u32[]{:S(2)}) copy-start(bf16[512]{0:T(512)(128)(2,1)} %param.31) | copy-start | bytes 3076
  7.2 13.9 %copy-start.19 = (bf16[512]{0:T(512)(128)(2,1)S(1)}, bf16[512]{0:T(512)(128)(2,1)}, u32[]{:S(2)}) copy-start(bf16[512]{0:T(512)(128)(2,1)} %param.32) | copy-start | bytes 3076
  7.3 13.9 %copy-start.20 = (bf16[512]{0:T(512)(128)(2,1)S(1)}, bf16[512]{0:T(512)(128)(2,1)}, u32[]{:S(2)}) copy-start(bf16[512]{0:T(512)(128)(2,1)} %param.34) | copy-start | bytes 3076
  7.3 13.9 %copy-start.21 = (bf16[512]{0:T(512)(128)(2,1)S(1)}, bf16[512]{0:T(512)(128)(2,1)}, u32[]{:S(2)}) copy-start(bf16[512]{0:T(512)(128)(2,1)} %param.35) | copy-start | bytes 3076
  7.3 13.9 %copy-start.22 = (bf16[512]{0:T(512)(128)(2,1)S(1)}, bf16[512]{0:T(512)(128)(2,1)}, u32[]{:S(2)}) copy-start(bf16[512]{0:T(512)(128)(2,1)} %param.37) | copy-start | bytes 3076
  7.3 13.9 %copy-start.23 = (bf16[512]{0:T(512)(128)(2,1)S(1)}, bf16[512]{0:T(512)(128)(2,1)}, u32[]{:S(2)}) copy-start(bf16[512]{0:T(512)(128)(2,1)} %param.38) | copy-start | bytes 3076
  7.3 13.9 %copy-start.24 = (bf16[512]{0:T(512)(128)(2,1)S(1)}, bf16[512]{0:T(512)(128)(2,1)}, u32[]{:S(2)}) copy-start(bf16[512]{0:T(512)(128)(2,1)} %param.39) | copy-start | bytes 3076
  7.3 13.9 %copy-start.25 = (bf16[512]{0:T(512)(128)(2,1)S(1)}, bf16[512]{0:T(512)(128)(2,1)}, u32[]{:S(2)}) copy-start(bf16[512]{0:T(512)(128)(2,1)} %param.43) | copy-start | bytes 3076
  7.3 14.2 %copy-start.14 = (bf16[2048]{0:T(1024)(128)(2,1)S(1)}, bf16[2048]{0:T(1024)(128)(2,1)}, u32[]{:S(2)}) copy-start(bf16[2048]{0:T(1024)(128)(2,1)} %param.41) | copy-start | bytes 12292
  8.4 0.7 copy-start.10
  11.5 23.4 %all-to-all-start = ((bf16[16,40,768]{2,1,0:T(8,128)(2,1)}), bf16[16,40,768]{2,1,0:T(8,128)(2,1)S(1)}, u32[]{:S(2)}, u32[]{:S(2)}) async-start(bf16[16,40,768]{2,1,0:T(8,128)(2,1)} %bitcast.2), calls=%async_computation | async-start | bytes 1966080 | tf_op jit(solution)/shard_map/all_to_all | solution.py:559
  23.5 11.4 %copy-start.11 = (s32[640,8]{1,0:T(8,128)S(1)}, s32[640,8]{1,0:T(8,128)}, u32[]{:S(2)}) copy-start(s32[640,8]{1,0:T(8,128)} %constant.55.clone.idx_c) | copy-start | bytes 61444
  23.5 11.4 %copy-start.12 = (s32[8,640]{1,0:T(8,128)S(1)}, s32[8,640]{1,0:T(8,128)}, u32[]{:S(2)}) copy-start(s32[8,640]{1,0:T(8,128)} %constant.54.clone.idx_r) | copy-start | bytes 61444
  34.9 1.1 copy-start.3
  36.0 1.4 copy-start.7
  37.5 13.2 %copy-start.1 = (bf16[2048,512]{1,0:T(8,128)(2,1)S(1)}, bf16[2048,512]{1,0:T(8,128)(2,1)}, u32[]{:S(2)}) copy-start(bf16[2048,512]{1,0:T(8,128)(2,1)} %down_w.3) | copy-start | bytes 6291460
  37.5 13.2 %copy-start.2 = (bf16[4,1,24,8,512]{4,3,2,1,0:T(8,128)(2,1)S(1)}, bf16[4,1,24,8,512]{4,3,2,1,0:T(8,128)(2,1)}, u32[]{:S(2)}) copy-start(bf16[4,1,24,8,512]{4,3,2,1,0:T(8,128)(2,1)} %param.27) | copy-start | bytes 2359300
  42.5 10.1 %collective-permute-start = (bf16[4,16,1024]{2,1,0:T(8,128)(2,1)S(1)}, bf16[4,16,1024]{2,1,0:T(8,128)(2,1)S(1)}, u32[]{:S(2)}, u32[]{:S(2)}) collective-permute-start(bf16[4,16,1024]{2,1,0:T(8,128)(2,1)S(1)} %get-tuple-element.62), channel_id=1, source_target_pairs={{0,1},{1,2},{2,3},{3,4},{4,5},{5,6},{6,7},{8,9},{9,10},{10,11},{11... | collective-permute-start | bytes 393224 | tf_op jit(solution)/shard_map/ppermute | solution.py:592
  48.6 6.3 %collective-permute-start.1 = (bf16[4,16,1024]{2,1,0:T(8,128)(2,1)S(1)}, bf16[4,16,1024]{2,1,0:T(8,128)(2,1)S(1)}, u32[]{:S(2)}, u32[]{:S(2)}) collective-permute-start(bf16[4,16,1024]{2,1,0:T(8,128)(2,1)S(1)} %get-tuple-element.63), channel_id=1, source_target_pairs={{1,0},{2,1},{3,2},{4,3},{5,4},{6,5},{7,6},{9,8},{10,9},{11,10},{12... | collective-permute-start | bytes 393224 | tf_op jit(solution)/shard_map/ppermute | solution.py:593
  50.7 4.2 %copy-start.5 = (bf16[16,128]{1,0:T(8,128)(2,1)S(1)}, bf16[16,128]{1,0:T(8,128)(2,1)}, u32[]{:S(2)}) copy-start(bf16[16,128]{1,0:T(8,128)(2,1)} %constant.52.clone.heads_i) | copy-start | bytes 12292
  52.5 7.0 %copy-start.6 = (bf16[512,2048]{1,0:T(8,128)(2,1)S(1)}, bf16[512,2048]{1,0:T(8,128)(2,1)}, u32[]{:S(2)}) copy-start(bf16[512,2048]{1,0:T(8,128)(2,1)} %up_w.3) | copy-start | bytes 6291460
  52.5 7.0 %copy-start.9 = (bf16[512,512]{1,0:T(8,128)(2,1)S(1)}, bf16[512,512]{1,0:T(8,128)(2,1)}, u32[]{:S(2)}) copy-start(bf16[512,512]{1,0:T(8,128)(2,1)} %out_w.3) | copy-start | bytes 1572868
  71.8 4.2 %collective-permute-start.2 = (bf16[2048,512]{1,0:T(8,128)(2,1)S(1)}, bf16[2048,512]{1,0:T(8,128)(2,1)S(1)}, u32[]{:S(2)}, u32[]{:S(2)}) collective-permute-start(bf16[2048,512]{1,0:T(8,128)(2,1)S(1)} %get-tuple-element.68), channel_id=1, source_target_pairs={{0,1},{1,0},{2,3},{3,2},{4,5},{5,4},{6,7},{7,6},{8,9},{9,8},{10,11... | collective-permute-start | bytes 6291464 | tf_op jit(solution)/shard_map/ppermute | solution.py:542
  84.4 15.3 %copy-start.8 = (bf16[512,1536]{1,0:T(8,128)(2,1)S(1)}, bf16[512,1536]{1,0:T(8,128)(2,1)}, u32[]{:S(2)}) copy-start(bf16[512,1536]{1,0:T(8,128)(2,1)} %qkv_w.3) | copy-start | bytes 4718596
  90.2 5.3 %collective-permute-start.3 = (bf16[4,16,1024]{2,1,0:T(8,128)(2,1)S(1)}, bf16[4,16,1024]{2,1,0:T(8,128)(2,1)S(1)}, u32[]{:S(2)}, u32[]{:S(2)}) collective-permute-start(bf16[4,16,1024]{2,1,0:T(8,128)(2,1)S(1)} %get-tuple-element.77), channel_id=1, source_target_pairs={{0,1},{1,2},{2,3},{3,4},{4,5},{5,6},{6,7},{8,9},{9,10},{10,11},{11... | collective-permute-start | bytes 393224 | tf_op jit(solution)/shard_map/ppermute | solution.py:630
  93.3 6.3 %collective-permute-start.4 = (bf16[4,16,1024]{2,1,0:T(8,128)(2,1)S(1)}, bf16[4,16,1024]{2,1,0:T(8,128)(2,1)S(1)}, u32[]{:S(2)}, u32[]{:S(2)}) collective-permute-start(bf16[4,16,1024]{2,1,0:T(8,128)(2,1)S(1)} %get-tuple-element.78), channel_id=1, source_target_pairs={{1,0},{2,1},{3,2},{4,3},{5,4},{6,5},{7,6},{9,8},{10,9},{11,10},{12... | collective-permute-start | bytes 393224 | tf_op jit(solution)/shard_map/ppermute | solution.py:631
  106.7 5.6 %collective-permute-start.5 = (bf16[1536,512]{1,0:T(8,128)(2,1)}, bf16[1536,512]{1,0:T(8,128)(2,1)}, u32[]{:S(2)}, u32[]{:S(2)}) collective-permute-start(bf16[1536,512]{1,0:T(8,128)(2,1)} %get-tuple-element.88), channel_id=1, source_target_pairs={{0,1},{1,0},{2,3},{3,2},{4,5},{5,4},{6,7},{7,6},{8,9},{9,8},{10,11... | collective-permute-start | bytes 4718600 | tf_op jit(solution)/shard_map/ppermute | solution.py:542
  106.7 34.9 %all-to-all-start.1 = ((bf16[64,32,512]{2,1,0:T(8,128)(2,1)}), bf16[64,32,512]{2,1,0:T(8,128)(2,1)}, u32[]{:S(2)}, u32[]{:S(2)}) async-start(bf16[64,32,512]{2,1,0:T(8,128)(2,1)} %bitcast.50), calls=%async_computation.1 | async-start | bytes 4194304 | tf_op jit(solution)/shard_map/all_to_all | solution.py:537
  112.3 117.8 %all-gather.3.cloned.1.call-start = ((), (), s32[]{:S(2)}) async-start(), calls=%async_computation.5 | async-start | bytes 4227072 | tf_op jit(solution)/shard_map/all_gather | solution.py:646
  172.8 47.1 %copy-start.4 = (bf16[768,512]{1,0:T(8,128)(2,1)S(1)}, bf16[768,512]{1,0:T(8,128)(2,1)}, u32[]{:S(2)}) copy-start(bf16[768,512]{1,0:T(8,128)(2,1)} %embed_w.3) | copy-start | bytes 2359300
  199.5 22.8 %collective-permute-start.6 = (bf16[1536,512]{1,0:T(8,128)(2,1)S(1)}, bf16[1536,512]{1,0:T(8,128)(2,1)S(1)}, u32[]{:S(2)}, u32[]{:S(2)}) collective-permute-start(bf16[1536,512]{1,0:T(8,128)(2,1)S(1)} %bitcast.40), channel_id=1, source_target_pairs={{0,1},{1,0},{2,3},{3,2},{4,5},{5,4},{6,7},{7,6},{8,9},{9,8},{10,11... | collective-permute-start | bytes 4718600 | tf_op jit(solution)/shard_map/ppermute | solution.py:650
  230.1 2.2 copy-start
Sparse Core Ops, SparseCore 0:
  144.3 85.7 all-gather.2

commit v3 on v2

--- a/solution.py
+++ b/solution.py
@@ -265,7 +265,7 @@
 
 def mlp_kernel(
     core, hidden, attended, cot, g_act, out_w, up_w, vecs, up_b,
-    middle_o, act_o, gexp_o, keep_o, send_o, n2_s, n2t_s,
+    middle_o, act_o, gexp_o, n2t_o, send_o, n2_s,
 ):
     tile = 256
     blocks = [slice(512 * f, 512 * f + 512) for f in range(4)]
@@ -285,14 +285,21 @@
         return carry
 
     lax.fori_loop(0, ALL // tile, forward, 0)
-    n2t_s[...] = jnp.transpose(n2_s[...])
-    for grads_o, half in ((keep_o, core[0]), (send_o, 1 - core[0])):
-        for b in range(2):
-            cols = pl.ds(pl.multiple_of(half * 1024 + 512 * b, 512), 512)
-            rows = slice(512 * b, 512 * b + 512)
-            grads_o[rows, :] = dot(act_o[:, cols], cot[...], TN).astype(BF16)
-            rows = slice(1024 + 512 * b, 1536 + 512 * b)
-            grads_o[rows, :] = dot(n2t_s[...], gexp_o[:, cols]).astype(BF16)
+    n2t_o[...] = jnp.transpose(n2_s[...])
+    weight_half(1 - core[0], send_o, act_o, gexp_o, n2t_o, cot)
+
+
+def weight_half(half, out, act, gexp, n2t, cot):
+    for b in range(2):
+        cols = pl.ds(pl.multiple_of(half * 1024 + 512 * b, 512), 512)
+        rows = slice(512 * b, 512 * b + 512)
+        out[rows, :] = dot(act[:, cols], cot[...], TN).astype(BF16)
+        rows = slice(1024 + 512 * b, 1536 + 512 * b)
+        out[rows, :] = dot(n2t[...], gexp[:, cols]).astype(BF16)
+
+
+def mlp_keep_kernel(core, act, gexp, n2t, cot, keep_o):
+    weight_half(core[0], keep_o, act, gexp, n2t, cot)
 
 
 def mlp_back_kernel(
@@ -377,62 +384,61 @@
 
 
 def leave_kernel(
-    core, gmixed, from_low, from_high, rim, hidden, normed, filled, seen, cell, gmid, qkv_w, vecs,
-    gout, sums, keep_o, send_o, ret_o, gm_s, gf_s, nt_s, ft_s,
+    core, gmixed, from_low, from_high, rim, hidden, normed, filled, seen, gmid, qkv_w, vecs,
+    gout, sums, gm_o, gf_o, small_o, send_o,
 ):
     small = jnp.zeros((1, D), F32)
     gain_sum, shift_sum, mask_sum, embed_sum, query_sum, value_sum = [small] * 6
     for m in range(MICRO):
         base = m * CELLS
         rows = slice(base, base + CELLS)
-        gm_s[rows, :] = gmixed[rows, :]
-        gm_s[base : base + 16, D:] = (rim[m, 0] + from_low[m].astype(F32)).astype(BF16)
-        gm_s[base + CELLS - 16 : base + CELLS, D:] = (rim[m, 1] + from_high[m].astype(F32)).astype(
+        gm_o[rows, :] = gmixed[rows, :]
+        gm_o[base : base + 16, D:] = (rim[m, 0] + from_low[m].astype(F32)).astype(BF16)
+        gm_o[base + CELLS - 16 : base + CELLS, D:] = (rim[m, 1] + from_high[m].astype(F32)).astype(
             BF16
         )
-        gm = gm_s[rows, :]
+        gm = gm_o[rows, :]
         grad = dot(gm, qkv_w[...], NT)
         normal, inverse = norm_parts(hidden[rows, :])
         g_hidden = gmid[rows, :] + norm_back(grad, normal, inverse, vecs[2:3, :])
         there = seen[rows, :] > 0.5
         g_low = g_hidden.astype(BF16)
-        gf_s[rows, :] = g_low
+        gf_o[rows, :] = g_low
         gain_sum += jnp.sum(grad * normal, axis=0, keepdims=True)
         shift_sum += jnp.sum(grad, axis=0, keepdims=True)
         mask_sum += jnp.sum(jnp.where(there, 0.0, g_hidden), axis=0, keepdims=True)
         embed_sum += jnp.sum(jnp.where(there, g_low.astype(F32), 0.0), axis=0, keepdims=True)
         query_sum += jnp.sum(gm[:, :D].astype(F32), axis=0, keepdims=True)
         value_sum += jnp.sum(gm[:, 2 * D :].astype(F32), axis=0, keepdims=True)
-    nt_s[...] = jnp.transpose(normed[...])
-    ft_s[...] = jnp.transpose(filled[...])
-    ret_o[...] = dot(one_hot(iota((GOT, ALL), 1) == cell[...]), gf_s[...]).astype(BF16)
-
-
-    def write(first, second):
-        def weights(b, carry):
-            cols = pl.ds(pl.multiple_of(b * 512, 512), 512)
-            first[cols, :] = dot(nt_s[...], gm_s[:, cols]).astype(BF16)
-            return carry
-
-        lax.fori_loop(0, 3, weights, 0)
-        second[0:512, :] = gout[...]
-        second[512:1280, :] = dot(ft_s[...], gf_s[...]).astype(BF16)
-        second[1280:1296, :] = jnp.concatenate(
-            [
-                embed_sum, mask_sum, gain_sum, shift_sum, query_sum, value_sum,
-                small, small, sums[...],
-            ],
-            axis=0,
-        ).astype(BF16)
-        second[1296:1536, :] = jnp.zeros((240, D), BF16)
-
-    @pl.when(core[0] == 0)
+    small_o[...] = jnp.concatenate(
+        [
+            embed_sum, mask_sum, gain_sum, shift_sum, query_sum, value_sum,
+            small, small, sums[...],
+        ],
+        axis=0,
+    )
+    one_half(core[0] != 0, send_o, normed, filled, gm_o, gf_o, gout, small_o)
+
+
+def one_half(first, out, normed, filled, gm, gf, gout, small):
+    @pl.when(first)
     def _():
-        write(keep_o, send_o)
-
-    @pl.when(core[0] != 0)
+        turned = jnp.transpose(normed[...])
+        for b in range(3):
+            cols = slice(512 * b, 512 * b + 512)
+            out[cols, :] = dot(turned, gm[:, cols]).astype(BF16)
+
+    @pl.when(jnp.logical_not(first))
     def _():
-        write(send_o, keep_o)
+        out[0:512, :] = gout[...]
+        out[512:1280, :] = dot(jnp.transpose(filled[...]), gf[...]).astype(BF16)
+        out[1280:1296, :] = small[...].astype(BF16)
+        out[1296:1536, :] = jnp.zeros((240, D), BF16)
+
+
+def leave_keep_kernel(core, gm, gf, small, normed, filled, gout, cell, keep_o, ret_o):
+    one_half(core[0] == 0, keep_o, normed, filled, gm, gf, gout, small)
+    ret_o[...] = dot(one_hot(iota((GOT, ALL), 1) == cell[...]), gf[...]).astype(BF16)
 
 
 def return_kernel(dest, came, embed_w, out):
@@ -462,7 +468,7 @@
             pl.BlockSpec((512, D), lambda i: (i, 0)),
             pl.BlockSpec((512, D), lambda i: (0, i)),
         ],
-        compiler_params=pltpu.CompilerParams(vmem_limit_bytes=16 * 2**20),
+        compiler_params=pltpu.CompilerParams(vmem_limit_bytes=58 * 2**20),
         cost_estimate=pl.CostEstimate(flops=0, bytes_accessed=12 * 2**20, transcendentals=0),
     )(gathered, gathered)
 
@@ -538,8 +544,7 @@
             block, both, split_axis=0, concat_axis=0, tiled=True, axis_index_groups=halves
         )
 
-    def chip_sum(keep, send):
-        other = lax.ppermute(send, "band", swap)
+    def chip_sum(keep, other):
         mine = (keep.astype(F32) + other.astype(F32)).astype(BF16)
         return mine.reshape(chips, -1, D)
 
@@ -597,16 +602,21 @@
         (mixed, from_low, from_high, mask, heads),
         flops=MICRO * 7 * 4 * 2**20,
     )
-    middle, act, gexp, keep, send = call(
+    middle, act, gexp, n2t, send = call(
         mlp_kernel, "mlp",
         [
-            ((ALL, D), F32), ((ALL, FF), BF16), ((ALL, FF), BF16), ((FF, D), BF16), ((FF, D), BF16),
+            ((ALL, D), F32), ((ALL, FF), BF16), ((ALL, FF), BF16), ((D, ALL), BF16),
+            ((FF, D), BF16),
         ],
         (core, hidden, attended, cot, g_act, out_weight, up_weight, vecs_two, up_b),
-        scratch=[pltpu.VMEM((ALL, D), BF16), pltpu.VMEM((D, ALL), BF16)],
-        smem=1, flops=2 * ALL * (3 * D * FF + D * D), vmem=24,
-    )
-    chip_one = chip_sum(keep, send)
+        scratch=[pltpu.VMEM((ALL, D), BF16)],
+        smem=1, flops=2 * ALL * (2 * D * FF + D * D), vmem=24,
+    )
+    (keep,) = call(
+        mlp_keep_kernel, "mlp_keep", [((FF, D), BF16)], (core, act, gexp, n2t, cot),
+        smem=1, flops=2 * ALL * D * FF,
+    )
+    chip_one = chip_sum(keep, lax.ppermute(send, "band", swap))
     act, chip_one = lax.optimization_barrier((act, chip_one))
     output, gmid, gatt, gout, sums = call(
         mlp_back_kernel, "mlp_back",
@@ -629,20 +639,23 @@
     )
     from_low = lax.ppermute(high, "band", forward)
     from_high = lax.ppermute(low, "band", backward)
-    keep, send, returned = call(
+    gm, gf, small, send = call(
         leave_kernel, "leave",
-        [((3 * D, D), BF16), ((3 * D, D), BF16), ((GOT, D), BF16)],
+        [((ALL, 3 * D), BF16), ((ALL, D), BF16), ((16, D), F32), ((3 * D, D), BF16)],
         (
-            core, gmixed, from_low, from_high, rim, hidden, normed, filled, seen, cell, gmid,
+            core, gmixed, from_low, from_high, rim, hidden, normed, filled, seen, gmid,
             qkv_weight, vecs_one, gout, sums,
         ),
-        scratch=[
-            pltpu.VMEM((ALL, 3 * D), BF16), pltpu.VMEM((ALL, D), BF16),
-            pltpu.VMEM((D, ALL), BF16), pltpu.VMEM((ENC, ALL), BF16),
-        ],
-        smem=1, flops=2 * ALL * (6 * D * D + GOT * D + ENC * D),
-    )
-    parts_one, chip_two = lax.optimization_barrier((parts_one, chip_sum(keep, send)))
+        smem=1, flops=2 * ALL * 5 * D * D,
+    )
+    keep, returned = call(
+        leave_keep_kernel, "leave_keep", [((3 * D, D), BF16), ((GOT, D), BF16)],
+        (core, gm, gf, small, normed, filled, gout, cell),
+        smem=1, flops=2 * ALL * (2 * D * D + GOT * D),
+    )
+    other = lax.ppermute(send, "band", swap)
+    parts_one, returned, other = lax.optimization_barrier((parts_one, returned, other))
+    chip_two = chip_sum(keep, other)
     total_one = lax.all_gather(total(parts_one), both, axis=0).reshape(chips, 2, -1, D)
     mine = total(to_all(chip_two))
     mine = to_all(jnp.broadcast_to(mine[None], (chips,) + mine.shape)).reshape(-1, D)
@@ -656,6 +669,7 @@
     came = lax.all_to_all(
         returned.reshape(SRC, BLK, D), "clip", split_axis=0, concat_axis=0, tiled=True
     ).reshape(GOT, D)
+    came, small = lax.optimization_barrier((came, small))
     (grad_enc,) = call(
         return_kernel, "return", [((MICRO, vis, ENC), BF16)], (dest, came, embed_weight),
         flops=2 * MICRO * vis * D * (GOT + ENC),

time: 244 us -> 244 us (level)
  local copies, waits for them, and re-layouts: 10.8 us -> 32.5 us
  waiting for transfers between devices: 51.6 us -> 31 us
  blocking collectives: 70.7 us -> 61.8 us
  starting transfers between devices: 32.4 us -> 35.6 us
  Pallas kernels: 53.6 us -> 56.1 us
    all_to_all x1, waiting for transfers between devices: 26.3 us -> 0.01 us  [to_all(): lax.all_to_all(block, both, split_axis=0, concat_axis=0, tiled=True, axis...]
    unnamed x57 -> x131, local copies, waits for them, and re-layouts: 8.04 us -> 29 us
    all_to_all x1 -> x0, blocking collectives: 15.7 us -> none  [on_device(): lax.all_to_all(returned.reshape(SRC, BLK, D), 'clip', split_axis=0, conca...]
    all_to_all x0 -> x1, waiting for transfers between devices: none -> 10.1 us  [on_device(): lax.all_to_all(returned.reshape(SRC, BLK, D), 'clip', split_axis=0, conca...]
    all_to_all x2, blocking collectives: 54.9 us -> 61.8 us  [to_all(): lax.all_to_all(block, both, split_axis=0, concat_axis=0, tiled=True, axis...]
    all_to_all x0 -> x1, starting transfers between devices: none -> 3.73 us  [on_device(): lax.all_to_all(returned.reshape(SRC, BLK, D), 'clip', split_axis=0, conca...]
    all_to_all x1, waiting for transfers between devices: 11.1 us -> 7.46 us  [on_device(): lax.all_to_all(packed.reshape(SRC, BLK, ENC), 'clip', split_axis=0, conca...]
    pallas_call x10 -> x12, Pallas kernels: 49.9 us -> 50.3 us  [call(): pl.pallas_call(kernel, name=name, out_shape=outs, in_specs=specs, out_spe...]
  transfers between devices with their start and end apart: 10 -> 11, of which waited for: 6 -> 7; matrix products, arithmetic and copies ran while one was open for 4% -> 5% of each run, Pallas kernels for 3% -> 11%
where the time goes in v3:
time: 244 us; the launch traced here: 243 us
  blocking collectives  61.8 us (25%)
  Pallas kernels  56.1 us (23%)
  starting transfers between devices  35.6 us (15%)
  local copies, waits for them, and re-layouts  32.5 us (13%)
  waiting for transfers between devices  31 us (13%)
  between operations  14.9 us (6%)
  other arithmetic  10.6 us (4%)
    all_to_all x2, blocking collectives, to_all(): lax.all_to_all(block, both, split_axis=0, concat_axis=0, tiled=True, axis...  61.8 us
    pallas_call x12, Pallas kernels, call(): pl.pallas_call(kernel, name=name, out_shape=outs, in_specs=specs, out_spe...  50.3 us
    unnamed x131, local copies, waits for them, and re-layouts  29 us
    all_to_all x1, waiting for transfers between devices, on_device(): lax.all_to_all(returned.reshape(SRC, BLK, D), 'clip', split_axis=0, conca...  10.1 us
    ppermute x2, starting transfers between devices, on_device(): from_low = lax.ppermute(high, 'band', forward)  9.48 us
    all_to_all x1, starting transfers between devices, on_device(): lax.all_to_all(packed.reshape(SRC, BLK, ENC), 'clip', split_axis=0, conca...  8.6 us
    all_to_all x1, waiting for transfers between devices, on_device(): lax.all_to_all(packed.reshape(SRC, BLK, ENC), 'clip', split_axis=0, conca...  7.46 us
    ppermute x2, waiting for transfers between devices, on_device(): from_high = lax.ppermute(low, 'band', backward)  6.56 us
  transfers between devices with their start and end apart: 11, of which 7 were waited for; matrix products, arithmetic and copies ran while one was open for 5% of the time, Pallas kernels for 11%

profile of v3, /device:TPU:1, one launch (start us, length us, event | category | flops | bytes accessed | tf_op | source)
XLA Modules:
  0.0 242.6 jit_solution(16787823524458816550)
XLA Ops:
  9.1 2.5 %pack.1 = (bf16[640,768]{1,0:T(8,128)(2,1)}, s32[4,38,1]{2,1,0:T(8,128)S(1)}) custom-call(s32[1]{0:T(128)} %bitcast.1.band, s32[4,38]{1,0:T(4,128)S(1)} %copy-done.45, bf16[4,38,768]{2,1,0:T(8,128)(2,1)S(1)} %copy.47.enc), custom_call_target="tpu_custom_call" | custom-call | flops 149422080 | bytes 1217732 | tf_op jit(solution)/shard_map/pack/pallas_call | solution.py:52
  12.1 8.6 %all-to-all-start = ((bf16[16,40,768]{2,1,0:T(8,128)(2,1)}), bf16[16,40,768]{2,1,0:T(8,128)(2,1)S(1)}, u32[]{:S(2)}, u32[]{:S(2)}) async-start(bf16[16,40,768]{2,1,0:T(8,128)(2,1)} %bitcast.2), calls=%async_computation | async-start | bytes 1966080 | tf_op jit(solution)/shard_map/all_to_all | solution.py:564
  24.1 1.5 tile.10.mask
  26.1 1.3 pad_maximum_fusion
  28.1 7.5 %all-to-all-done = bf16[16,40,768]{2,1,0:T(8,128)(2,1)S(1)} async-done(((bf16[16,40,768]{2,1,0:T(8,128)(2,1)}), bf16[16,40,768]{2,1,0:T(8,128)(2,1)S(1)}, u32[]{:S(2)}, u32[]{:S(2)}) %all-to-all-start) | async-done | bytes 983072 | tf_op jit(solution)/shard_map/all_to_all | solution.py:564
  36.5 1.4 copy-done.13
  37.9 1.4 copy-done.14
  39.3 1.2 copy-done.19
  40.5 1.1 copy-done.20
  44.0 5.0 %enter.1 = (f32[768,512]{1,0:T(8,128)S(1)}, bf16[768,512]{1,0:T(8,128)(2,1)S(1)}, bf16[768,1536]{1,0:T(8,128)(2,1)S(1)}, bf16[768,768]{1,0:T(8,128)(2,1)S(1)}, f...) custom-call(s32[8,640]{1,0:T(8,128)S(1)} %copy-done.47, ...), custom_call_target="tpu_custom_call" | custom-call | flops 2566914048 | bytes 11144704 | tf_op jit(solution)/shard_map/enter/pallas_call | solution.py:52
  49.8 6.0 %collective-permute-start = (bf16[4,16,1024]{2,1,0:T(8,128)(2,1)S(1)}, bf16[4,16,1024]{2,1,0:T(8,128)(2,1)S(1)}, u32[]{:S(2)}, u32[]{:S(2)}) collective-permute-start(bf16[4,16,1024]{2,1,0:T(8,128)(2,1)S(1)} %get-tuple-element.68), channel_id=1, source_target_pairs={{0,1},{1,2},{2,3},{3,4},{4,5},{5,6},{6,7},{8,9},{9,10},{10,11},{11... | collective-permute-start | bytes 393224 | tf_op jit(solution)/shard_map/ppermute | solution.py:597
  55.8 2.1 collective-permute-start.1
  58.0 1.8 before.1.g_act
  59.9 2.2 collective-permute-done.1.high
  62.1 4.7 %attend.1 = (bf16[768,512]{1,0:T(8,128)(2,1)S(1)}, f32[28,32,512]{2,1,0:T(8,128)S(1)}) custom-call(bf16[768,1536]{1,0:T(8,128)(2,1)S(1)} %get-tuple-element.67.mixed, bf16[4,16,1024]{2,1,0:T(8,128)(2,1)S(1)} %collective-permute-done.low, bf16[4,16,1024]{2,1,0:T(8,128)(2,1)S(1)} %collective-permute-done.1.high, f32[28,32,128]{2,1,0:T(8,128)S(1)} %copy-done.12, ...), custom_call_target="tpu_custom_call" | custom-call | flops 117440512 | bytes 5705728 | tf_op jit(solution)/shard_map/attend/pallas_call | solution.py:52
  66.9 1.3 copy-done.10
  68.2 10.6 %mlp.1 = (f32[768,512]{1,0:T(8,128)S(1)}, bf16[768,2048]{1,0:T(8,128)(2,1)S(1)}, bf16[768,2048]{1,0:T(8,128)(2,1)S(1)}, bf16[512,768]{1,0:T(8,128)(2,1)S(1)}, bf16[2048,512]{1,0:T(8,128)(2,1)S(1)}) custom-call(s32[1]{0:T(128)} %bitcast.core, f32[768,512]{1,0:T(8,128)S(1)} %get-tuple-element.66.hidden, bf16[768,512]{1,0:T(8,128)(2,1)S(1)} %get-tuple-element.70.attended, ...), custom_call_target="tpu_custom_call" | custom-call | flops 3623878656 | bytes 22831108 | tf_op jit(solution)/shard_map/mlp/pallas_call | solution.py:52
  78.9 1.8 mlp_keep.1
  82.0 1.1 collective-permute-done.2
  83.0 1.9 add_convert_fusion
  84.9 6.4 %all-to-all-start.1 = ((bf16[64,32,512]{2,1,0:T(8,128)(2,1)}), bf16[64,32,512]{2,1,0:T(8,128)(2,1)}, u32[]{:S(2)}, u32[]{:S(2)}) async-start(bf16[64,32,512]{2,1,0:T(8,128)(2,1)} %bitcast.51), calls=%async_computation.1 | async-start | bytes 4194304 | tf_op jit(solution)/shard_map/all_to_all | solution.py:543
  91.6 1.9 copy-done.1
  93.5 1.9 copy-done.3
  95.4 1.1 copy-done.5
  96.5 1.6 copy-done.9
  98.8 1.6 copy-done.40
  100.4 1.1 copy-done.42
  101.6 1.0 copy-done.44
  102.6 1.4 copy-done.49
  104.0 6.3 %mlp_back.1 = (bf16[768,512]{1,0:T(8,128)(2,1)}, f32[768,512]{1,0:T(8,128)S(1)}, bf16[768,512]{1,0:T(8,128)(2,1)S(1)}, bf16[512,512]{1,0:T(8,128)(2,1)S(1)}, f32[8,512]{1,0:T(8,128)S(1)}) custom-call(f32[768,512]{1,0:T(8,128)S(1)} %copy-done.49, bf16[768,512]{1,0:T(8,128)(2,1)S(1)} %copy-done.42, bf16[768,512]{1,0:T(8,128)(2,1)S(1)} %bitcast.43, ...), custom_call_target="tpu_custom_call" | custom-call | flops 4026531840 | bytes 17858560 | tf_op jit(solution)/shard_map/mlp_back/pallas_call | solution.py:52
  110.4 5.8 %attend_back.1 = (bf16[768,1536]{1,0:T(8,128)(2,1)S(1)}, bf16[4,16,1024]{2,1,0:T(8,128)(2,1)S(1)}, bf16[4,16,1024]{2,1,0:T(8,128)(2,1)S(1)}, f32[4,2,16,1024]{3,2,1,0:T(8,128)S(1)}) custom-call(bf16[768,1536]{1,0:T(8,128)(2,1)S(1)} %get-tuple-element.67.mixed, bf16[4,16,1024]{2,1,0:T(8,128)(2,1)S(1)} %copy-done.24, bf16[4,16,1024]{2,1,0:T(8,128)(2,1)S(1)} %copy-done.26, ...), custom_call_target="tpu_custom_call" | custom-call | flops 469762048 | bytes 8392704 | tf_op jit(solution)/shard_map/attend_back/pallas_call | solution.py:52
  116.2 3.4 %collective-permute-start.3 = (bf16[4,16,1024]{2,1,0:T(8,128)(2,1)S(1)}, bf16[4,16,1024]{2,1,0:T(8,128)(2,1)S(1)}, u32[]{:S(2)}, u32[]{:S(2)}) collective-permute-start(bf16[4,16,1024]{2,1,0:T(8,128)(2,1)S(1)} %get-tuple-element.82), channel_id=1, source_target_pairs={{0,1},{1,2},{2,3},{3,4},{4,5},{5,6},{6,7},{8,9},{9,10},{10,11},{11... | collective-permute-start | bytes 393224 | tf_op jit(solution)/shard_map/ppermute | solution.py:640
  119.7 1.9 collective-permute-start.4
  121.6 4.3 %collective-permute-done.4.from_high = bf16[4,16,1024]{2,1,0:T(8,128)(2,1)S(1)} collective-permute-done((bf16[4,16,1024]{2,1,0:T(8,128)(2,1)S(1)}, bf16[4,16,1024]{2,1,0:T(8,128)(2,1)S(1)}, u32[]{:S(2)}, u32[]{:S(2)}) %collective-permute-start.4) | collective-permute-done | bytes 131104 | tf_op jit(solution)/shard_map/ppermute | solution.py:641
  126.0 4.3 %leave.1 = (bf16[768,1536]{1,0:T(8,128)(2,1)S(1)}, bf16[768,512]{1,0:T(8,128)(2,1)S(1)}, f32[16,512]{1,0:T(8,128)S(1)}, bf16[1536,512]{1,0:T(8,128)(2,1)S(1)}) custom-call(s32[1]{0:T(128)} %bitcast.core, bf16[768,1536]{1,0:T(8,128)(2,1)S(1)} %get-tuple-element.81.gmixed, bf16[4,16,1024]{2,1,0:T(8,128)(2,1)S(1)} %collective-permute-done.3.from_low, ...), custom_call_target="tpu_custom_call" | custom-call | flops 2013265920 | bytes 15141892 | tf_op jit(solution)/shard_map/leave/pallas_call | solution.py:52
  130.4 1.6 leave_keep.1
  132.8 1.1 collective-permute-done.5
  133.9 2.5 %reduce_sum.25 = bf16[32,512]{1,0:T(8,128)(2,1)} reduce(bf16[64,32,512]{2,1,0:T(8,128)(2,1)} %all-to-all-done.1, bf16[]{:T(256)} %constant.47.clone.1), dimensions={0}, to_apply=%region_1.2 | reduce | flops 1032192 | bytes 2129922 | tf_op jit(solution)/shard_map/reduce_sum | solution.py:552
  136.4 1.8 add_convert_fusion.1
  138.3 33.7 %all_to_all.25 = bf16[64,24,512]{2,1,0:T(8,128)(2,1)S(1)} all-to-all(bf16[64,24,512]{2,1,0:T(8,128)(2,1)S(1)} %bitcast.52), channel_id=1, replica_groups={{0,2,4,6,8,10,12,14,16,18,20,22,24,26,28,30,32,34,36,38,40,42,44,46,48,..., dimensions={0} | all-to-all | bytes 3145728 | tf_op jit(solution)/shard_map/all_to_all | solution.py:543
  172.3 28.2 %all_to_all.26 = bf16[64,24,512]{2,1,0:T(8,128)(2,1)S(1)} all-to-all(bf16[64,24,512]{2,1,0:T(8,128)(2,1)S(1)} %broadcast_in_dim.79), channel_id=1, replica_groups={{0,2,4,6,8,10,12,14,16,18,20,22,24,26,28,30,32,34,36,38,40,42,44,46,48,..., dimensions={0} | all-to-all | bytes 3145728 | tf_op jit(solution)/shard_map/all_to_all | solution.py:543
  200.5 3.0 %collective-permute-start.6 = (bf16[1536,512]{1,0:T(8,128)(2,1)S(1)}, bf16[1536,512]{1,0:T(8,128)(2,1)}, u32[]{:S(2)}, u32[]{:S(2)}) collective-permute-start(bf16[1536,512]{1,0:T(8,128)(2,1)S(1)} %bitcast.38), channel_id=1, source_target_pairs={{0,1},{1,0},{2,3},{3,2},{4,5},{5,4},{6,7},{7,6},{8,9},{9,8},{10,11... | collective-permute-start | bytes 4718600 | tf_op jit(solution)/shard_map/ppermute | solution.py:663
  203.5 3.7 %all-to-all-start.4 = ((bf16[16,40,512]{2,1,0:T(8,128)(2,1)}), bf16[16,40,512]{2,1,0:T(8,128)(2,1)S(1)}, u32[]{:S(2)}, u32[]{:S(2)}) async-start(bf16[16,40,512]{2,1,0:T(8,128)(2,1)} %bitcast.47), calls=%async_computation.4 | async-start | bytes 1310720 | tf_op jit(solution)/shard_map/all_to_all | solution.py:669
  207.2 4.3 %unpack_two.1 = (f32[512,1536]{1,0:T(8,128)}, f32[768,512]{1,0:T(8,128)}, f32[512,512]{1,0:T(8,128)}, f32[16,512]{1,0:T(8,128)S(1)}) custom-call(s32[1]{0:T(128)} %bitcast.core, bf16[1536,512]{1,0:T(8,128)(2,1)S(1)} %bitcast.39, bf16[1536,512]{1,0:T(8,128)(2,1)} %collective-permute-done.6.other), custom_call_target="tpu_custom_call" | custom-call | bytes 8945668 | tf_op jit(solution)/shard_map/unpack_two/pallas_call | solution.py:52
  211.5 10.1 %all-to-all-done.4 = bf16[16,40,512]{2,1,0:T(8,128)(2,1)S(1)} async-done(((bf16[16,40,512]{2,1,0:T(8,128)(2,1)}), bf16[16,40,512]{2,1,0:T(8,128)(2,1)S(1)}, u32[]{:S(2)}, u32[]{:S(2)}) %all-to-all-start.4) | async-done | bytes 655392 | tf_op jit(solution)/shard_map/all_to_all | solution.py:669
  221.7 1.5 return.1
  225.2 4.7 %all-gather.3.cloned.1.call-done = bf16[4096,512]{1,0:T(8,128)(2,1)} async-done(((bf16[32,512]{1,0:T(8,128)(2,1)}), bf16[4096,512]{1,0:T(8,128)(2,1)}) %all-gather.3.cloned.1.call-update) | async-done | bytes 4194320 | tf_op jit(solution)/shard_map/all_gather | solution.py:659
  229.9 5.8 %unpack_one.1 = (f32[2048,512]{1,0:T(8,128)}, f32[512,2048]{1,0:T(8,128)}) custom-call(bf16[64,2,32,512]{3,2,1,0:T(8,128)(2,1)} %bitcast.49, bf16[64,2,32,512]{3,2,1,0:T(8,128)(2,1)} %bitcast.50), custom_call_target="tpu_custom_call" | custom-call | bytes 12582912 | tf_op jit(solution)/shard_map/unpack_one/pallas_call | solution.py:458
  (174 shorter events, 16.3 us)
Async XLA Ops:
  7.2 16.2 %copy-start.50 = (pred[32,32]{1,0:T(32,128)(4,1)S(1)}, pred[32,32]{1,0:T(32,128)(4,1)}, u32[]{:S(2)}) copy-start(pred[32,32]{1,0:T(32,128)(4,1)} %constant.53.clone) | copy-start | bytes 3076
  7.2 13.7 %copy-start.52 = (s32[4,1,3]{0,1,2:T(1,128)S(1)}, s32[4,1,3]{0,1,2:T(1,128)}, u32[]{:S(2)}) copy-start(s32[4,1,3]{0,1,2:T(1,128)} %param.26) | copy-start | bytes 148
  7.2 14.5 %copy-start.53 = (bf16[512]{0:T(512)(128)(2,1)S(1)}, bf16[512]{0:T(512)(128)(2,1)}, u32[]{:S(2)}) copy-start(bf16[512]{0:T(512)(128)(2,1)} %param.29) | copy-start | bytes 3076
  7.2 14.5 %copy-start.54 = (bf16[512]{0:T(512)(128)(2,1)S(1)}, bf16[512]{0:T(512)(128)(2,1)}, u32[]{:S(2)}) copy-start(bf16[512]{0:T(512)(128)(2,1)} %param.30) | copy-start | bytes 3076
  7.2 14.5 %copy-start.55 = (bf16[512]{0:T(512)(128)(2,1)S(1)}, bf16[512]{0:T(512)(128)(2,1)}, u32[]{:S(2)}) copy-start(bf16[512]{0:T(512)(128)(2,1)} %param.31) | copy-start | bytes 3076
  7.2 14.5 %copy-start.56 = (bf16[512]{0:T(512)(128)(2,1)S(1)}, bf16[512]{0:T(512)(128)(2,1)}, u32[]{:S(2)}) copy-start(bf16[512]{0:T(512)(128)(2,1)} %param.32) | copy-start | bytes 3076
  7.3 14.5 %copy-start.57 = (bf16[512]{0:T(512)(128)(2,1)S(1)}, bf16[512]{0:T(512)(128)(2,1)}, u32[]{:S(2)}) copy-start(bf16[512]{0:T(512)(128)(2,1)} %param.34) | copy-start | bytes 3076
  7.3 14.5 %copy-start.58 = (bf16[512]{0:T(512)(128)(2,1)S(1)}, bf16[512]{0:T(512)(128)(2,1)}, u32[]{:S(2)}) copy-start(bf16[512]{0:T(512)(128)(2,1)} %param.35) | copy-start | bytes 3076
  7.3 14.5 %copy-start.59 = (bf16[512]{0:T(512)(128)(2,1)S(1)}, bf16[512]{0:T(512)(128)(2,1)}, u32[]{:S(2)}) copy-start(bf16[512]{0:T(512)(128)(2,1)} %param.37) | copy-start | bytes 3076
  7.3 14.5 %copy-start.60 = (bf16[512]{0:T(512)(128)(2,1)S(1)}, bf16[512]{0:T(512)(128)(2,1)}, u32[]{:S(2)}) copy-start(bf16[512]{0:T(512)(128)(2,1)} %param.38) | copy-start | bytes 3076
  7.3 14.6 %copy-start.61 = (bf16[512]{0:T(512)(128)(2,1)S(1)}, bf16[512]{0:T(512)(128)(2,1)}, u32[]{:S(2)}) copy-start(bf16[512]{0:T(512)(128)(2,1)} %param.39) | copy-start | bytes 3076
  7.3 14.6 %copy-start.62 = (bf16[512]{0:T(512)(128)(2,1)S(1)}, bf16[512]{0:T(512)(128)(2,1)}, u32[]{:S(2)}) copy-start(bf16[512]{0:T(512)(128)(2,1)} %param.43) | copy-start | bytes 3076
  7.3 15.4 %copy-start.51 = (bf16[2048]{0:T(1024)(128)(2,1)S(1)}, bf16[2048]{0:T(1024)(128)(2,1)}, u32[]{:S(2)}) copy-start(bf16[2048]{0:T(1024)(128)(2,1)} %param.41) | copy-start | bytes 12292
  12.1 23.4 %all-to-all-start = ((bf16[16,40,768]{2,1,0:T(8,128)(2,1)}), bf16[16,40,768]{2,1,0:T(8,128)(2,1)S(1)}, u32[]{:S(2)}, u32[]{:S(2)}) async-start(bf16[16,40,768]{2,1,0:T(8,128)(2,1)} %bitcast.2), calls=%async_computation | async-start | bytes 1966080 | tf_op jit(solution)/shard_map/all_to_all | solution.py:564
  44.0 13.9 %copy-start.4 = (bf16[4,1,24,8,512]{4,3,2,1,0:T(8,128)(2,1)S(1)}, bf16[4,1,24,8,512]{4,3,2,1,0:T(8,128)(2,1)}, u32[]{:S(2)}) copy-start(bf16[4,1,24,8,512]{4,3,2,1,0:T(8,128)(2,1)} %param.27) | copy-start | bytes 2359300
  44.0 13.9 %copy-start.8 = (bf16[2048,512]{1,0:T(8,128)(2,1)S(1)}, bf16[2048,512]{1,0:T(8,128)(2,1)}, u32[]{:S(2)}) copy-start(bf16[2048,512]{1,0:T(8,128)(2,1)} %down_w.3) | copy-start | bytes 6291460
  49.8 10.0 %copy-start.6 = (bf16[768,512]{1,0:T(8,128)(2,1)}, bf16[768,512]{1,0:T(8,128)(2,1)S(1)}, u32[]{:S(2)}) copy-start(bf16[768,512]{1,0:T(8,128)(2,1)S(1)} %get-tuple-element.85.normed) | copy-start | bytes 2359300
  49.8 10.0 %copy-start.27 = (f32[768,1]{1,0:T(8,128)}, f32[768,1]{1,0:T(8,128)S(1)}, u32[]{:S(2)}) copy-start(f32[768,1]{1,0:T(8,128)S(1)} %get-tuple-element.87.seen) | copy-start | bytes 9220
  49.8 18.3 %copy-start.16 = (f32[768,512]{1,0:T(8,128)}, f32[768,512]{1,0:T(8,128)S(1)}, u32[]{:S(2)}) copy-start(f32[768,512]{1,0:T(8,128)S(1)} %get-tuple-element.66.hidden) | copy-start | bytes 4718596
  49.8 10.1 %collective-permute-start = (bf16[4,16,1024]{2,1,0:T(8,128)(2,1)S(1)}, bf16[4,16,1024]{2,1,0:T(8,128)(2,1)S(1)}, u32[]{:S(2)}, u32[]{:S(2)}) collective-permute-start(bf16[4,16,1024]{2,1,0:T(8,128)(2,1)S(1)} %get-tuple-element.68), channel_id=1, source_target_pairs={{0,1},{1,2},{2,3},{3,4},{4,5},{5,6},{6,7},{8,9},{9,10},{10,11},{11... | collective-permute-start | bytes 393224 | tf_op jit(solution)/shard_map/ppermute | solution.py:597
  55.8 6.3 %collective-permute-start.1 = (bf16[4,16,1024]{2,1,0:T(8,128)(2,1)S(1)}, bf16[4,16,1024]{2,1,0:T(8,128)(2,1)S(1)}, u32[]{:S(2)}, u32[]{:S(2)}) collective-permute-start(bf16[4,16,1024]{2,1,0:T(8,128)(2,1)S(1)} %get-tuple-element.69), channel_id=1, source_target_pairs={{1,0},{2,1},{3,2},{4,3},{5,4},{6,5},{7,6},{9,8},{10,9},{11,10},{12... | collective-permute-start | bytes 393224 | tf_op jit(solution)/shard_map/ppermute | solution.py:598
  58.0 4.2 %copy-start.12 = (f32[28,32,128]{2,1,0:T(8,128)S(1)}, f32[28,32,128]{2,1,0:T(8,128)}, u32[]{:S(2)}) copy-start(f32[28,32,128]{2,1,0:T(8,128)} %tile.10.mask) | copy-start | bytes 1376260
  59.8 8.3 %copy-start.33 = (f32[8,512]{1,0:T(8,128)S(1)}, f32[8,512]{1,0:T(8,128)}, u32[]{:S(2)}) copy-start(f32[8,512]{1,0:T(8,128)} %convert_element_type.83.vecs) | copy-start | bytes 49156
  59.8 8.3 %copy-start.37 = (f32[2048]{0:T(1024)S(1)}, f32[2048]{0:T(1024)}, u32[]{:S(2)}) copy-start(f32[2048]{0:T(1024)} %broadcast_in_dim.80) | copy-start | bytes 24580
  59.9 8.3 %copy-start.39 = (bf16[512,2048]{1,0:T(8,128)(2,1)S(1)}, bf16[512,2048]{1,0:T(8,128)(2,1)}, u32[]{:S(2)}) copy-start(bf16[512,2048]{1,0:T(8,128)(2,1)} %up_w.3) | copy-start | bytes 6291460
  59.9 8.3 %copy-start.43 = (bf16[512,512]{1,0:T(8,128)(2,1)S(1)}, bf16[512,512]{1,0:T(8,128)(2,1)}, u32[]{:S(2)}) copy-start(bf16[512,512]{1,0:T(8,128)(2,1)} %out_w.3) | copy-start | bytes 1572868
  59.9 8.2 %copy-start.23 = (bf16[4,16,1024]{2,1,0:T(8,128)(2,1)}, bf16[4,16,1024]{2,1,0:T(8,128)(2,1)S(1)}, u32[]{:S(2)}) copy-start(bf16[4,16,1024]{2,1,0:T(8,128)(2,1)S(1)} %collective-permute-done.low) | copy-start | bytes 393220
  62.1 6.0 %copy-start.25 = (bf16[4,16,1024]{2,1,0:T(8,128)(2,1)}, bf16[4,16,1024]{2,1,0:T(8,128)(2,1)S(1)}, u32[]{:S(2)}) copy-start(bf16[4,16,1024]{2,1,0:T(8,128)(2,1)S(1)} %collective-permute-done.1.high) | copy-start | bytes 393220
  68.1 10.6 %copy-start.41 = (bf16[768,512]{1,0:T(8,128)(2,1)}, bf16[768,512]{1,0:T(8,128)(2,1)S(1)}, u32[]{:S(2)}) copy-start(bf16[768,512]{1,0:T(8,128)(2,1)S(1)} %get-tuple-element.70.attended) | copy-start | bytes 2359300
  78.8 4.2 %collective-permute-start.2 = (bf16[2048,512]{1,0:T(8,128)(2,1)S(1)}, bf16[2048,512]{1,0:T(8,128)(2,1)S(1)}, u32[]{:S(2)}, u32[]{:S(2)}) collective-permute-start(bf16[2048,512]{1,0:T(8,128)(2,1)S(1)} %get-tuple-element.75), channel_id=1, source_target_pairs={{0,1},{1,0},{2,3},{3,2},{4,5},{5,4},{6,7},{7,6},{8,9},{9,8},{10,11... | collective-permute-start | bytes 6291464 | tf_op jit(solution)/shard_map/ppermute | solution.py:619
  84.9 48.9 %all-to-all-start.1 = ((bf16[64,32,512]{2,1,0:T(8,128)(2,1)}), bf16[64,32,512]{2,1,0:T(8,128)(2,1)}, u32[]{:S(2)}, u32[]{:S(2)}) async-start(bf16[64,32,512]{2,1,0:T(8,128)(2,1)} %bitcast.51), calls=%async_computation.1 | async-start | bytes 4194304 | tf_op jit(solution)/shard_map/all_to_all | solution.py:543
  91.3 138.6 %all-gather.3.cloned.1.call-start = ((), (), s32[]{:S(2)}) async-start(), calls=%async_computation.5 | async-start | bytes 4227072 | tf_op jit(solution)/shard_map/all_gather | solution.py:659
  104.0 6.4 %copy-start.11 = (f32[28,32,512]{2,1,0:T(8,128)S(1)}, f32[28,32,512]{2,1,0:T(8,128)}, u32[]{:S(2)}) copy-start(f32[28,32,512]{2,1,0:T(8,128)} %copy-done.10) | copy-start | bytes 5505028
  104.0 6.4 %copy-start.24 = (bf16[4,16,1024]{2,1,0:T(8,128)(2,1)S(1)}, bf16[4,16,1024]{2,1,0:T(8,128)(2,1)}, u32[]{:S(2)}) copy-start(bf16[4,16,1024]{2,1,0:T(8,128)(2,1)} %copy-done.23) | copy-start | bytes 393220
  104.0 6.4 %copy-start.26 = (bf16[4,16,1024]{2,1,0:T(8,128)(2,1)S(1)}, bf16[4,16,1024]{2,1,0:T(8,128)(2,1)}, u32[]{:S(2)}) copy-start(bf16[4,16,1024]{2,1,0:T(8,128)(2,1)} %copy-done.25) | copy-start | bytes 393220
  104.0 6.4 %copy-start.36 = (bf16[16,128]{1,0:T(8,128)(2,1)S(1)}, bf16[16,128]{1,0:T(8,128)(2,1)}, u32[]{:S(2)}) copy-start(bf16[16,128]{1,0:T(8,128)(2,1)} %constant.52.clone.heads_i) | copy-start | bytes 12292
  110.4 15.6 %copy-start.7 = (bf16[768,512]{1,0:T(8,128)(2,1)S(1)}, bf16[768,512]{1,0:T(8,128)(2,1)}, u32[]{:S(2)}) copy-start(bf16[768,512]{1,0:T(8,128)(2,1)} %copy-done.6) | copy-start | bytes 2359300
  110.4 15.6 %copy-start.15 = (bf16[512,1536]{1,0:T(8,128)(2,1)S(1)}, bf16[512,1536]{1,0:T(8,128)(2,1)}, u32[]{:S(2)}) copy-start(bf16[512,1536]{1,0:T(8,128)(2,1)} %qkv_w.3) | copy-start | bytes 4718596
  110.4 15.6 %copy-start.17 = (f32[768,512]{1,0:T(8,128)S(1)}, f32[768,512]{1,0:T(8,128)}, u32[]{:S(2)}) copy-start(f32[768,512]{1,0:T(8,128)} %copy-done.16) | copy-start | bytes 4718596
  110.4 15.6 %copy-start.28 = (f32[768,1]{1,0:T(8,128)S(1)}, f32[768,1]{1,0:T(8,128)}, u32[]{:S(2)}) copy-start(f32[768,1]{1,0:T(8,128)} %copy-done.27) | copy-start | bytes 9220
  116.2 5.4 %collective-permute-start.3 = (bf16[4,16,1024]{2,1,0:T(8,128)(2,1)S(1)}, bf16[4,16,1024]{2,1,0:T(8,128)(2,1)S(1)}, u32[]{:S(2)}, u32[]{:S(2)}) collective-permute-start(bf16[4,16,1024]{2,1,0:T(8,128)(2,1)S(1)} %get-tuple-element.82), channel_id=1, source_target_pairs={{0,1},{1,2},{2,3},{3,4},{4,5},{5,6},{6,7},{8,9},{9,10},{10,11},{11... | collective-permute-start | bytes 393224 | tf_op jit(solution)/shard_map/ppermute | solution.py:640
  119.7 6.3 %collective-permute-start.4 = (bf16[4,16,1024]{2,1,0:T(8,128)(2,1)S(1)}, bf16[4,16,1024]{2,1,0:T(8,128)(2,1)S(1)}, u32[]{:S(2)}, u32[]{:S(2)}) collective-permute-start(bf16[4,16,1024]{2,1,0:T(8,128)(2,1)S(1)} %get-tuple-element.83), channel_id=1, source_target_pairs={{1,0},{2,1},{3,2},{4,3},{5,4},{6,5},{7,6},{9,8},{10,9},{11,10},{12... | collective-permute-start | bytes 393224 | tf_op jit(solution)/shard_map/ppermute | solution.py:641
  126.0 4.4 %copy-start.30 = (s32[640,1]{1,0:T(8,128)S(1)}, s32[640,1]{1,0:T(8,128)}, u32[]{:S(2)}) copy-start(s32[640,1]{1,0:T(8,128)} %copy-done.29) | copy-start | bytes 7684
  130.3 3.6 %collective-permute-start.5 = (bf16[1536,512]{1,0:T(8,128)(2,1)S(1)}, bf16[1536,512]{1,0:T(8,128)(2,1)}, u32[]{:S(2)}, u32[]{:S(2)}) collective-permute-start(bf16[1536,512]{1,0:T(8,128)(2,1)S(1)} %get-tuple-element.98), channel_id=1, source_target_pairs={{0,1},{1,0},{2,3},{3,2},{4,5},{5,4},{6,7},{7,6},{8,9},{9,8},{10,11... | collective-permute-start | bytes 4718600 | tf_op jit(solution)/shard_map/ppermute | solution.py:656
  200.5 6.7 %collective-permute-start.6 = (bf16[1536,512]{1,0:T(8,128)(2,1)S(1)}, bf16[1536,512]{1,0:T(8,128)(2,1)}, u32[]{:S(2)}, u32[]{:S(2)}) collective-permute-start(bf16[1536,512]{1,0:T(8,128)(2,1)S(1)} %bitcast.38), channel_id=1, source_target_pairs={{0,1},{1,0},{2,3},{3,2},{4,5},{5,4},{6,7},{7,6},{8,9},{9,8},{10,11... | collective-permute-start | bytes 4718600 | tf_op jit(solution)/shard_map/ppermute | solution.py:663
  203.5 18.2 %copy-start.21 = (bf16[768,512]{1,0:T(8,128)(2,1)S(1)}, bf16[768,512]{1,0:T(8,128)(2,1)}, u32[]{:S(2)}) copy-start(bf16[768,512]{1,0:T(8,128)(2,1)} %embed_w.3) | copy-start | bytes 2359300
  203.5 18.2 %copy-start.32 = (s32[4,38,1]{2,1,0:T(8,128)S(1)}, s32[4,38,1]{2,1,0:T(8,128)}, u32[]{:S(2)}) copy-start(s32[4,38,1]{2,1,0:T(8,128)} %copy-done.31) | copy-start | bytes 1828
  203.5 18.2 %all-to-all-start.4 = ((bf16[16,40,512]{2,1,0:T(8,128)(2,1)}), bf16[16,40,512]{2,1,0:T(8,128)(2,1)S(1)}, u32[]{:S(2)}, u32[]{:S(2)}) async-start(bf16[16,40,512]{2,1,0:T(8,128)(2,1)} %bitcast.47), calls=%async_computation.4 | async-start | bytes 1310720 | tf_op jit(solution)/shard_map/all_to_all | solution.py:669
  (26 other events, 37.1 us)
Sparse Core Ops, SparseCore 0:
  136.6 93.2 all-gather.2

commit v4 on v3

--- a/solution.py
+++ b/solution.py
@@ -42,9 +42,10 @@
     return jnp.where(hit, 1.0, 0.0).astype(BF16)
 
 
-def call(kernel, name, out_shape, args, scratch=(), smem=0, flops=0, vmem=16):
-    specs = [pl.BlockSpec(memory_space=pltpu.SMEM)] * smem
-    specs += [pl.BlockSpec(memory_space=pltpu.VMEM)] * (len(args) - smem)
+def call(kernel, name, out_shape, args, scratch=(), smem=0, flops=0, vmem=16, far=()):
+    spaces = [pltpu.SMEM] * smem + [pltpu.VMEM] * (len(args) - smem)
+    for i in far:
+        spaces[i] = pltpu.HBM
     outs = [jax.ShapeDtypeStruct(shape, dtype) for shape, dtype in out_shape]
     size = sum(a.size * a.dtype.itemsize for a in args) + sum(
         o.size * o.dtype.itemsize for o in outs
@@ -53,7 +54,7 @@
         kernel,
         name=name,
         out_shape=outs,
-        in_specs=specs,
+        in_specs=[pl.BlockSpec(memory_space=space) for space in spaces],
         out_specs=[pl.BlockSpec(memory_space=pltpu.VMEM)] * len(outs),
         scratch_shapes=list(scratch),
         compiler_params=pltpu.CompilerParams(vmem_limit_bytes=vmem * 2**20),
@@ -107,10 +108,20 @@
     )
 
 
+def fetch(pairs, sems):
+    copies = [pltpu.make_async_copy(far, near, sems.at[i]) for i, (far, near) in enumerate(pairs)]
+    for copy in copies:
+        copy.start()
+    return copies
+
+
 def enter_kernel(
-    idx_r, idx_c, got, table, embed_w, qkv_w, vecs, qkv_b,
+    idx_r, idx_c, got_i, row_table, freq_table, embed_i, qkv_i, vecs, qkv_b,
     hidden_o, normed_o, mixed_o, filled_o, seen_o, cell_o, low_o, high_o,
+    got, embed_w, qkv_w, sems,
 ):
+    copies = fetch([(got_i, got), (embed_i, embed_w), (qkv_i, qkv_w)], sems)
+    copies[0].wait()
     hit = one_hot(iota((SRC, GOT), 1) == iota((SRC, GOT), 0) * BLK + (BLK - 4))
     numbers = dot(hit, got[:, :128]).astype(BF16)
     spread_r = dot(numbers, one_hot(iota((SRC, GOT), 0) == idx_r[0:1, :]), TN)
@@ -134,8 +145,17 @@
         filled = dot(match.astype(BF16), got[...]).astype(BF16)
         filled_o[rows, :] = filled
         seen_o[rows, :] = seen
-        proj = (dot(filled, embed_w[...]) + vecs[0:1, :]).astype(BF16).astype(F32)
-        hidden = jnp.where(seen > 0.5, proj, vecs[1:2, :]) + table[rows, :]
+    copies[1].wait()
+    copies[2].wait()
+    freq = jnp.broadcast_to(freq_table[...][None], (ROWS, FREQ, D // 2)).reshape(CELLS, D // 2)
+    for m in range(MICRO):
+        rows = slice(m * CELLS, (m + 1) * CELLS)
+        seen = seen_o[rows, :]
+        proj = (dot(filled_o[rows, :], embed_w[...]) + vecs[0:1, :]).astype(BF16).astype(F32)
+        line = row_table[m * ROWS : (m + 1) * ROWS, :]
+        line = jnp.broadcast_to(line[:, None, :], (ROWS, FREQ, D // 2)).reshape(CELLS, D // 2)
+        table = jnp.concatenate([line, freq], axis=1)
+        hidden = jnp.where(seen > 0.5, proj, vecs[1:2, :]) + table
         hidden_o[rows, :] = hidden
         normal, unused = norm_parts(hidden)
         normed = (normal * vecs[2:3, :] + vecs[3:4, :]).astype(BF16)
@@ -448,29 +468,14 @@
         out[m] = dot(g_proj, embed_w[...], NT).astype(BF16)
 
 
-def unpack_one_kernel(down_i, up_i, down_o, up_o):
-    down_o[...] = down_i[...].reshape(512, D).astype(F32)
-    up_o[...] = up_i[...].reshape(512, D).astype(F32)
-
-
-def unpack_one(gathered):
-    block = (16, 1, 32, D)
-    return pl.pallas_call(
-        unpack_one_kernel,
-        name="unpack_one",
-        grid=(4,),
-        out_shape=[jax.ShapeDtypeStruct((FF, D), F32), jax.ShapeDtypeStruct((D, FF), F32)],
-        in_specs=[
-            pl.BlockSpec(block, lambda i: (i % 2, i // 2, 0, 0)),
-            pl.BlockSpec(block, lambda i: (2 + i % 2, i // 2, 0, 0)),
-        ],
-        out_specs=[
-            pl.BlockSpec((512, D), lambda i: (i, 0)),
-            pl.BlockSpec((512, D), lambda i: (0, i)),
-        ],
-        compiler_params=pltpu.CompilerParams(vmem_limit_bytes=58 * 2**20),
-        cost_estimate=pl.CostEstimate(flops=0, bytes_accessed=12 * 2**20, transcendentals=0),
-    )(gathered, gathered)
+def unpack_one_kernel(core, mine, other, down_o, up_o):
+    for half, source in ((core[0], mine), (1 - core[0], other)):
+        start = pl.multiple_of(half * 1024, 1024)
+        down_o[pl.ds(start, 1024), :] = source[0:1024, :].astype(F32)
+        for b in range(2):
+            up_o[:, pl.ds(start + 512 * b, 512)] = source[
+                1024 + 512 * b : 1536 + 512 * b, :
+            ].astype(F32)
 
 
 def unpack_two_kernel(core, mine, other, qkv_o, embed_o, out_o, small_o):
@@ -499,17 +504,14 @@
     return (jnp.where(inside[None, :], ident, -1), rows[None, :] - start)
 
 
-def position_table(row_in_clip, width):
+def position_tables(row_in_clip, width):
     quarter = width // 4
     omega = 1.0 / 10000.0 ** (jnp.arange(quarter, dtype=jnp.float32) / quarter)
     row_angle = row_in_clip.astype(jnp.float32)[..., None] * omega
     freq_angle = jnp.arange(FREQ, dtype=jnp.float32)[:, None] * omega
     row_part = jnp.concatenate([jnp.sin(row_angle), jnp.cos(row_angle)], -1)
     freq_part = jnp.concatenate([jnp.sin(freq_angle), jnp.cos(freq_angle)], -1)
-    shape = row_in_clip.shape + (FREQ, width // 2)
-    return jnp.concatenate(
-        [jnp.broadcast_to(row_part[..., None, :], shape), jnp.broadcast_to(freq_part, shape)], -1
-    )
+    return row_part.reshape(-1, width // 2), freq_part
 
 
 def window_mask(ident):
@@ -551,6 +553,9 @@
     def total(parts):
         return jnp.sum(parts.astype(F32), 0).astype(BF16)
 
+    def spread(chunk):
+        return jnp.broadcast_to(chunk[None], (chips,) + chunk.shape)
+
     vis = visible_pos.shape[1]
     packed, dest = call(
         pack_kernel, "pack", [((GOT, ENC), BF16), ((MICRO, vis, 1), jnp.int32)],
@@ -572,7 +577,7 @@
     heads = jnp.asarray(np.arange(128)[None, :] // 32 == np.arange(16)[:, None] % 4, BF16)
 
     unused, row_in_clip = clip_ident(clip_len[:, 0], band * ROWS + jnp.arange(ROWS))
-    table = position_table(row_in_clip, D).reshape(ALL, D)
+    row_table, freq_table = position_tables(row_in_clip, D)
     ident_ext, unused = clip_ident(clip_len[:, 0], band * ROWS - 2 + jnp.arange(ROWS + 4))
     mask = window_mask(ident_ext)
     zero = jnp.zeros((D,), BF16)
@@ -589,9 +594,14 @@
             ((MICRO, 16, 2 * D), BF16), ((MICRO, 16, 2 * D), BF16),
         ],
         (
-            jnp.asarray(index), jnp.asarray(np.ascontiguousarray(index.T)), got, table,
-            embed_weight, qkv_weight, vecs_one, qkv_b,
+            jnp.asarray(index), jnp.asarray(np.ascontiguousarray(index.T)), got, row_table,
+            freq_table, embed_weight, qkv_weight, vecs_one, qkv_b,
         ),
+        scratch=[
+            pltpu.VMEM((GOT, ENC), BF16), pltpu.VMEM((ENC, D), BF16), pltpu.VMEM((D, 3 * D), BF16),
+            pltpu.SemaphoreType.DMA((3,)),
+        ],
+        far=(2, 5, 6),
         flops=2 * ALL * (GOT * ENC + ENC * D + 3 * D * D),
     )
     from_low = lax.ppermute(high, "band", forward)
@@ -617,7 +627,6 @@
         smem=1, flops=2 * ALL * D * FF,
     )
     chip_one = chip_sum(keep, lax.ppermute(send, "band", swap))
-    act, chip_one = lax.optimization_barrier((act, chip_one))
     output, gmid, gatt, gout, sums = call(
         mlp_back_kernel, "mlp_back",
         [
@@ -627,7 +636,6 @@
         scratch=[pltpu.VMEM((ALL, D), BF16)],
         flops=2 * ALL * (2 * D * FF + 2 * D * D), vmem=24,
     )
-    parts_one = to_all(chip_one)
     gmixed, low, high, rim = call(
         attend_back_kernel, "attend_back",
         [
@@ -637,8 +645,12 @@
         (mixed, from_low, from_high, probs, gatt, heads),
         flops=MICRO * 7 * 4 * 2**22,
     )
+    chip_one, low, high = lax.optimization_barrier((chip_one, low, high))
     from_low = lax.ppermute(high, "band", forward)
     from_high = lax.ppermute(low, "band", backward)
+    total_one = total(to_all(chip_one))
+    total_one, from_low, from_high = lax.optimization_barrier((total_one, from_low, from_high))
+    mine_one = lax.all_gather(total_one, both, axis=0, axis_index_groups=halves).reshape(-1, D)
     gm, gf, small, send = call(
         leave_kernel, "leave",
         [((ALL, 3 * D), BF16), ((ALL, D), BF16), ((16, D), F32), ((3 * D, D), BF16)],
@@ -648,33 +660,32 @@
         ),
         smem=1, flops=2 * ALL * 5 * D * D,
     )
+    other = lax.ppermute(send, "band", swap)
     keep, returned = call(
         leave_keep_kernel, "leave_keep", [((3 * D, D), BF16), ((GOT, D), BF16)],
         (core, gm, gf, small, normed, filled, gout, cell),
         smem=1, flops=2 * ALL * (2 * D * D + GOT * D),
     )
-    other = lax.ppermute(send, "band", swap)
-    parts_one, returned, other = lax.optimization_barrier((parts_one, returned, other))
-    chip_two = chip_sum(keep, other)
-    total_one = lax.all_gather(total(parts_one), both, axis=0).reshape(chips, 2, -1, D)
-    mine = total(to_all(chip_two))
-    mine = to_all(jnp.broadcast_to(mine[None], (chips,) + mine.shape)).reshape(-1, D)
+    mine = to_all(spread(total(to_all(chip_sum(keep, other))))).reshape(-1, D)
     mine, returned = lax.optimization_barrier((mine, returned))
-    other = lax.ppermute(mine, "band", swap)
+    came = lax.all_to_all(
+        returned.reshape(SRC, BLK, D), "clip", split_axis=0, concat_axis=0, tiled=True
+    ).reshape(GOT, D)
     qkv, g_embed, g_out, small = call(
         unpack_two_kernel, "unpack_two",
         [((D, 3 * D), F32), ((ENC, D), F32), ((D, D), F32), ((16, D), F32)],
-        (core, mine, other), smem=1,
-    )
-    came = lax.all_to_all(
-        returned.reshape(SRC, BLK, D), "clip", split_axis=0, concat_axis=0, tiled=True
-    ).reshape(GOT, D)
+        (core, mine, lax.ppermute(mine, "band", swap)), smem=1,
+    )
     came, small = lax.optimization_barrier((came, small))
+    mine_one, came = lax.optimization_barrier((mine_one, came))
+    down, up = call(
+        unpack_one_kernel, "unpack_one", [((FF, D), F32), ((D, FF), F32)],
+        (core, mine_one, lax.ppermute(mine_one, "band", swap)), smem=1,
+    )
     (grad_enc,) = call(
         return_kernel, "return", [((MICRO, vis, ENC), BF16)], (dest, came, embed_weight),
         flops=2 * MICRO * vis * D * (GOT + ENC),
     )
-    down, up = unpack_one(total_one)
     return (
         output.reshape(cotangent.shape), grad_enc, g_embed, small[0], small[1], small[2],
         small[3], qkv, small[4], small[5], g_out, small[8], small[9], small[10], up,

time: 244 us -> 248 us (1.016)
  waiting for transfers between devices: 31 us -> 76.7 us
  blocking collectives: 61.8 us -> 27.9 us
  local copies, waits for them, and re-layouts: 32.5 us -> 20.2 us
  starting transfers between devices: 35.6 us -> 44.6 us
  other arithmetic: 10.6 us -> 7.76 us
    all_to_all x1 -> x2, waiting for transfers between devices: 0.01 us -> 45.6 us  [to_all(): lax.all_to_all(block, both, split_axis=0, concat_axis=0, tiled=True, axis...]
    all_to_all x2 -> x1, blocking collectives: 61.8 us -> 27.9 us  [to_all(): lax.all_to_all(block, both, split_axis=0, concat_axis=0, tiled=True, axis...]
    unnamed x131 -> x89, local copies, waits for them, and re-layouts: 29 us -> 17 us
    all_to_all x1 -> x2, starting transfers between devices: 6.38 us -> 11.3 us  [to_all(): lax.all_to_all(block, both, split_axis=0, concat_axis=0, tiled=True, axis...]
    ppermute x2, waiting for transfers between devices: 6.56 us -> 2.26 us  [on_device(): from_high = lax.ppermute(low, 'band', backward)]
    all_gather x1, waiting for transfers between devices: 4.68 us -> 8.68 us  [on_device(): lax.all_gather(total_one, both, axis=0, axis_index_groups=halves)]
    all_to_all x1, waiting for transfers between devices: 7.46 us -> 10.4 us  [on_device(): lax.all_to_all(packed.reshape(SRC, BLK, ENC), 'clip', split_axis=0, conca...]
  transfers between devices with their start and end apart: 11 -> 13, of which waited for: 7 -> 8; matrix products, arithmetic and copies ran while one was open for 5% -> 4% of each run, Pallas kernels for 11% -> 9%
where the time goes in v4:
time: 248 us; the launch traced here: 247 us
  waiting for transfers between devices  76.7 us (31%)
  Pallas kernels  55.4 us (22%)
  starting transfers between devices  44.6 us (18%)
  blocking collectives  27.9 us (11%)
  local copies, waits for them, and re-layouts  20.2 us (8%)
  between operations  14.8 us (6%)
  other arithmetic  7.76 us (3%)
    pallas_call x13, Pallas kernels, call(): pl.pallas_call(kernel, name=name, out_shape=outs, in_specs=[pl.BlockSpec(...  55.4 us
    all_to_all x2, waiting for transfers between devices, to_all(): lax.all_to_all(block, both, split_axis=0, concat_axis=0, tiled=True, axis...  45.6 us
    all_to_all x1, blocking collectives, to_all(): lax.all_to_all(block, both, split_axis=0, concat_axis=0, tiled=True, axis...  27.9 us
    unnamed x89, local copies, waits for them, and re-layouts  17 us
    all_to_all x2, starting transfers between devices, to_all(): lax.all_to_all(block, both, split_axis=0, concat_axis=0, tiled=True, axis...  11.3 us
    all_to_all x1, waiting for transfers between devices, on_device(): lax.all_to_all(packed.reshape(SRC, BLK, ENC), 'clip', split_axis=0, conca...  10.4 us
    ppermute x2, starting transfers between devices, on_device(): from_low = lax.ppermute(high, 'band', forward)  9.93 us
    all_gather x1, waiting for transfers between devices, on_device(): lax.all_gather(total_one, both, axis=0, axis_index_groups=halves)  8.68 us
  transfers between devices with their start and end apart: 13, of which 8 were waited for; matrix products, arithmetic and copies ran while one was open for 4% of the time, Pallas kernels for 9%

profile of v4, /device:TPU:1, one launch (start us, length us, event | category | flops | bytes accessed | tf_op | source)
XLA Modules:
  0.0 247.4 jit_solution(13096101102972991942)
XLA Ops:
  7.3 1.0 copy.47.enc
  9.1 2.5 pack.1
  12.2 8.6 %all-to-all-start = ((bf16[16,40,768]{2,1,0:T(8,128)(2,1)}), bf16[16,40,768]{2,1,0:T(8,128)(2,1)S(1)}, u32[]{:S(2)}, u32[]{:S(2)}) async-start(bf16[16,40,768]{2,1,0:T(8,128)(2,1)} %bitcast.2), calls=%async_computation | async-start | bytes 1966080 | tf_op jit(solution)/shard_map/all_to_all | solution.py:569
  23.5 0.8 tile.10.mask
  25.2 10.4 %all-to-all-done = bf16[16,40,768]{2,1,0:T(8,128)(2,1)S(1)} async-done(((bf16[16,40,768]{2,1,0:T(8,128)(2,1)}), bf16[16,40,768]{2,1,0:T(8,128)(2,1)S(1)}, u32[]{:S(2)}, u32[]{:S(2)}) %all-to-all-start) | async-done | bytes 983072 | tf_op jit(solution)/shard_map/all_to_all | solution.py:569
  35.5 1.4 copy-done.5
  36.9 1.1 copy-done.11
  38.1 0.7 copy-done.21
  38.8 1.0 copy-done.27
  39.7 0.7 copy-done.28
  40.5 5.5 %enter.1 = (f32[768,512]{1,0:T(8,128)S(1)}, bf16[768,512]{1,0:T(8,128)(2,1)S(1)}, bf16[768,1536]{1,0:T(8,128)(2,1)S(1)}, bf16[768,768]{1,0:T(8,128)(2,1)S(1)}, f...) custom-call(s32[8,640]{1,0:T(8,128)S(1)} %copy-done.28, ...), custom_call_target="tpu_custom_call" | custom-call | flops 2566914048 | bytes 9678336 | tf_op jit(solution)/shard_map/enter/pallas_call | solution.py:53
  46.0 6.0 %collective-permute-start = (bf16[4,16,1024]{2,1,0:T(8,128)(2,1)S(1)}, bf16[4,16,1024]{2,1,0:T(8,128)(2,1)S(1)}, u32[]{:S(2)}, u32[]{:S(2)}) collective-permute-start(bf16[4,16,1024]{2,1,0:T(8,128)(2,1)S(1)} %get-tuple-element.71), channel_id=1, source_target_pairs={{0,1},{1,2},{2,3},{3,4},{4,5},{5,6},{6,7},{8,9},{9,10},{10,11},{11... | collective-permute-start | bytes 393224 | tf_op jit(solution)/shard_map/ppermute | solution.py:607
  52.0 2.1 collective-permute-start.1
  54.2 1.8 before.1.g_act
  56.1 2.3 collective-permute-done.1.high
  58.3 4.7 %attend.1 = (bf16[768,512]{1,0:T(8,128)(2,1)S(1)}, f32[28,32,512]{2,1,0:T(8,128)S(1)}) custom-call(bf16[768,1536]{1,0:T(8,128)(2,1)S(1)} %get-tuple-element.70.mixed, bf16[4,16,1024]{2,1,0:T(8,128)(2,1)S(1)} %collective-permute-done.low, bf16[4,16,1024]{2,1,0:T(8,128)(2,1)S(1)} %collective-permute-done.1.high, f32[28,32,128]{2,1,0:T(8,128)S(1)} %tile.10.mask, ...), custom_call_target="tpu_custom_call" | custom-call | flops 117440512 | bytes 5705728 | tf_op jit(solution)/shard_map/attend/pallas_call | solution.py:53
  63.1 10.6 %mlp.1 = (f32[768,512]{1,0:T(8,128)S(1)}, bf16[768,2048]{1,0:T(8,128)(2,1)S(1)}, bf16[768,2048]{1,0:T(8,128)(2,1)S(1)}, bf16[512,768]{1,0:T(8,128)(2,1)S(1)}, bf16[2048,512]{1,0:T(8,128)(2,1)S(1)}) custom-call(s32[1]{0:T(128)} %bitcast.core, f32[768,512]{1,0:T(8,128)S(1)} %get-tuple-element.69.hidden, bf16[768,512]{1,0:T(8,128)(2,1)S(1)} %get-tuple-element.73.attended, ...), custom_call_target="tpu_custom_call" | custom-call | flops 3623878656 | bytes 22831108 | tf_op jit(solution)/shard_map/mlp/pallas_call | solution.py:53
  73.7 6.1 %mlp_back.1 = (bf16[768,512]{1,0:T(8,128)(2,1)}, f32[768,512]{1,0:T(8,128)S(1)}, bf16[768,512]{1,0:T(8,128)(2,1)S(1)}, bf16[512,512]{1,0:T(8,128)(2,1)S(1)}, f32[8,512]{1,0:T(8,128)S(1)}) custom-call(f32[768,512]{1,0:T(8,128)S(1)} %get-tuple-element.74.middle_i, bf16[768,512]{1,0:T(8,128)(2,1)S(1)} %get-tuple-element.73.attended, ...), custom_call_target="tpu_custom_call" | custom-call | flops 4026531840 | bytes 17858560 | tf_op jit(solution)/shard_map/mlp_back/pallas_call | solution.py:53
  79.8 5.8 %attend_back.1 = (bf16[768,1536]{1,0:T(8,128)(2,1)S(1)}, bf16[4,16,1024]{2,1,0:T(8,128)(2,1)S(1)}, bf16[4,16,1024]{2,1,0:T(8,128)(2,1)S(1)}, f32[4,2,16,1024]{3,2,1,0:T(8,128)S(1)}) custom-call(bf16[768,1536]{1,0:T(8,128)(2,1)S(1)} %get-tuple-element.70.mixed, bf16[4,16,1024]{2,1,0:T(8,128)(2,1)S(1)} %collective-permute-done.low, ...), custom_call_target="tpu_custom_call" | custom-call | flops 469762048 | bytes 8392704 | tf_op jit(solution)/shard_map/attend_back/pallas_call | solution.py:53
  85.7 1.4 copy-done.1
  87.1 1.8 mlp_keep.1
  88.9 1.9 add_convert_fusion
  90.9 6.6 %all-to-all-start.1 = ((bf16[64,32,512]{2,1,0:T(8,128)(2,1)}), bf16[64,32,512]{2,1,0:T(8,128)(2,1)}, u32[]{:S(2)}, u32[]{:S(2)}) async-start(bf16[64,32,512]{2,1,0:T(8,128)(2,1)} %bitcast.48), calls=%async_computation.1 | async-start | bytes 4194304 | tf_op jit(solution)/shard_map/all_to_all | solution.py:545
  97.5 3.9 %collective-permute-start.3 = (bf16[4,16,1024]{2,1,0:T(8,128)(2,1)}, bf16[4,16,1024]{2,1,0:T(8,128)(2,1)}, u32[]{:S(2)}, u32[]{:S(2)}) collective-permute-start(bf16[4,16,1024]{2,1,0:T(8,128)(2,1)} %copy-done.25), channel_id=1, source_target_pairs={{0,1},{1,2},{2,3},{3,4},{4,5},{5,6},{6,7},{8,9},{9,10},{10,11},{11... | collective-permute-start | bytes 393224 | tf_op jit(solution)/shard_map/ppermute | solution.py:649
  101.4 1.9 collective-permute-start.4
  103.3 22.7 %all-to-all-done.1 = bf16[64,32,512]{2,1,0:T(8,128)(2,1)} async-done(((bf16[64,32,512]{2,1,0:T(8,128)(2,1)}), bf16[64,32,512]{2,1,0:T(8,128)(2,1)}, u32[]{:S(2)}, u32[]{:S(2)}) %all-to-all-start.1) | async-done | bytes 2097184 | tf_op jit(solution)/shard_map/all_to_all | solution.py:545
  126.0 2.5 %reduce_sum.24 = bf16[32,512]{1,0:T(8,128)(2,1)} reduce(bf16[64,32,512]{2,1,0:T(8,128)(2,1)} %all-to-all-done.1, bf16[]{:T(256)} %constant.47.clone.1), dimensions={0}, to_apply=%region_0.1 | reduce | flops 1032192 | bytes 2129922 | tf_op jit(solution)/shard_map/reduce_sum | solution.py:554
  128.6 1.7 copy-done.2
  130.2 1.4 copy-done.6
  131.7 1.4 copy-done.8
  133.1 1.4 copy-done.10
  134.5 5.3 %leave.1 = (bf16[768,1536]{1,0:T(8,128)(2,1)S(1)}, bf16[768,512]{1,0:T(8,128)(2,1)S(1)}, f32[16,512]{1,0:T(8,128)S(1)}, bf16[1536,512]{1,0:T(8,128)(2,1)S(1)}) custom-call(s32[1]{0:T(128)} %bitcast.core, bf16[768,1536]{1,0:T(8,128)(2,1)S(1)} %copy-done.2, bf16[4,16,1024]{2,1,0:T(8,128)(2,1)} %collective-permute-done.3.from_low, ...), custom_call_target="tpu_custom_call" | custom-call | flops 2013265920 | bytes 15141892 | tf_op jit(solution)/shard_map/leave/pallas_call | solution.py:53
  139.8 2.5 %collective-permute-start.5 = (bf16[1536,512]{1,0:T(8,128)(2,1)S(1)}, bf16[1536,512]{1,0:T(8,128)(2,1)S(1)}, u32[]{:S(2)}, u32[]{:S(2)}) collective-permute-start(bf16[1536,512]{1,0:T(8,128)(2,1)S(1)} %get-tuple-element.104), channel_id=1, source_target_pairs={{0,1},{1,0},{2,3},{3,2},{4,5},{5,4},{6,7},{7,6},{8,9},{9,8},{10,11... | collective-permute-start | bytes 4718600 | tf_op jit(solution)/shard_map/ppermute | solution.py:663
  142.3 1.6 leave_keep.1
  143.9 0.8 copy-done.13
  145.3 1.6 add_convert_fusion.1
  146.9 4.7 %all-to-all-start.2 = ((bf16[64,24,512]{2,1,0:T(8,128)(2,1)}), bf16[64,24,512]{2,1,0:T(8,128)(2,1)S(1)}, u32[]{:S(2)}, u32[]{:S(2)}) async-start(bf16[64,24,512]{2,1,0:T(8,128)(2,1)} %bitcast.11), calls=%async_computation.2 | async-start | bytes 3145728 | tf_op jit(solution)/shard_map/all_to_all | solution.py:545
  152.4 22.8 %all-to-all-done.2 = bf16[64,24,512]{2,1,0:T(8,128)(2,1)S(1)} async-done(((bf16[64,24,512]{2,1,0:T(8,128)(2,1)}), bf16[64,24,512]{2,1,0:T(8,128)(2,1)S(1)}, u32[]{:S(2)}, u32[]{:S(2)}) %all-to-all-start.2) | async-done | bytes 1572896 | tf_op jit(solution)/shard_map/all_to_all | solution.py:545
  175.6 27.9 %all_to_all.25 = bf16[64,24,512]{2,1,0:T(8,128)(2,1)S(1)} all-to-all(bf16[64,24,512]{2,1,0:T(8,128)(2,1)S(1)} %broadcast_in_dim.74), channel_id=1, replica_groups={{0,2,4,6,8,10,12,14,16,18,20,22,24,26,28,30,32,34,36,38,40,42,44,46,48,..., dimensions={0} | all-to-all | bytes 3145728 | tf_op jit(solution)/shard_map/all_to_all | solution.py:545
  203.5 3.3 %collective-permute-start.6 = (bf16[1536,512]{1,0:T(8,128)(2,1)S(1)}, bf16[1536,512]{1,0:T(8,128)(2,1)}, u32[]{:S(2)}, u32[]{:S(2)}) collective-permute-start(bf16[1536,512]{1,0:T(8,128)(2,1)S(1)} %bitcast.38), channel_id=1, source_target_pairs={{0,1},{1,0},{2,3},{3,2},{4,5},{5,4},{6,7},{7,6},{8,9},{9,8},{10,11... | collective-permute-start | bytes 4718600 | tf_op jit(solution)/shard_map/ppermute | solution.py:677
  206.8 3.7 %all-to-all-start.4 = ((bf16[16,40,512]{2,1,0:T(8,128)(2,1)}), bf16[16,40,512]{2,1,0:T(8,128)(2,1)S(1)}, u32[]{:S(2)}, u32[]{:S(2)}) async-start(bf16[16,40,512]{2,1,0:T(8,128)(2,1)} %bitcast.46), calls=%async_computation.4 | async-start | bytes 1310720 | tf_op jit(solution)/shard_map/all_to_all | solution.py:671
  210.5 4.3 %unpack_two.1 = (f32[512,1536]{1,0:T(8,128)}, f32[768,512]{1,0:T(8,128)}, f32[512,512]{1,0:T(8,128)}, f32[16,512]{1,0:T(8,128)S(1)}) custom-call(s32[1]{0:T(128)} %bitcast.core, bf16[1536,512]{1,0:T(8,128)(2,1)S(1)} %bitcast.39, bf16[1536,512]{1,0:T(8,128)(2,1)} %collective-permute-done.6.other), custom_call_target="tpu_custom_call" | custom-call | bytes 8945668 | tf_op jit(solution)/shard_map/unpack_two/pallas_call | solution.py:53
  214.9 8.1 %all-to-all-done.4 = bf16[16,40,512]{2,1,0:T(8,128)(2,1)S(1)} async-done(((bf16[16,40,512]{2,1,0:T(8,128)(2,1)}), bf16[16,40,512]{2,1,0:T(8,128)(2,1)S(1)}, u32[]{:S(2)}, u32[]{:S(2)}) %all-to-all-start.4) | async-done | bytes 655392 | tf_op jit(solution)/shard_map/all_to_all | solution.py:671
  223.0 8.7 %all-gather.3.cloned.1.call-done.mine = bf16[2048,512]{1,0:T(8,128)(2,1)} async-done(((bf16[32,512]{1,0:T(8,128)(2,1)}), bf16[2048,512]{1,0:T(8,128)(2,1)}) %all-gather.3.cloned.1.call-update) | async-done | bytes 2097168 | tf_op jit(solution)/shard_map/all_gather | solution.py:653
  231.6 1.0 collective-permute-start.7
  232.7 1.5 return.1
  234.2 0.8 copy.53
  236.7 3.9 %unpack_one.1 = (f32[2048,512]{1,0:T(8,128)}, f32[512,2048]{1,0:T(8,128)}) custom-call(s32[1]{0:T(128)} %bitcast.core, bf16[2048,512]{1,0:T(8,128)(2,1)S(1)} %copy-done.3, bf16[2048,512]{1,0:T(8,128)(2,1)S(1)} %collective-permute-done.7.other), custom_call_target="tpu_custom_call" | custom-call | bytes 12582916 | tf_op jit(solution)/shard_map/unpack_one/pallas_call | solution.py:53
  (140 shorter events, 8.2 us)
Async XLA Ops:
  7.2 14.7 %copy-start.29 = (pred[32,32]{1,0:T(32,128)(4,1)S(1)}, pred[32,32]{1,0:T(32,128)(4,1)}, u32[]{:S(2)}) copy-start(pred[32,32]{1,0:T(32,128)(4,1)} %constant.53.clone) | copy-start | bytes 3076
  7.2 13.7 %copy-start.31 = (s32[4,1,3]{0,1,2:T(1,128)S(1)}, s32[4,1,3]{0,1,2:T(1,128)}, u32[]{:S(2)}) copy-start(s32[4,1,3]{0,1,2:T(1,128)} %param.26) | copy-start | bytes 148
  7.2 15.6 %copy-start.32 = (bf16[512]{0:T(512)(128)(2,1)S(1)}, bf16[512]{0:T(512)(128)(2,1)}, u32[]{:S(2)}) copy-start(bf16[512]{0:T(512)(128)(2,1)} %param.29) | copy-start | bytes 3076
  7.2 15.6 %copy-start.33 = (bf16[512]{0:T(512)(128)(2,1)S(1)}, bf16[512]{0:T(512)(128)(2,1)}, u32[]{:S(2)}) copy-start(bf16[512]{0:T(512)(128)(2,1)} %param.30) | copy-start | bytes 3076
  7.2 15.6 %copy-start.34 = (bf16[512]{0:T(512)(128)(2,1)S(1)}, bf16[512]{0:T(512)(128)(2,1)}, u32[]{:S(2)}) copy-start(bf16[512]{0:T(512)(128)(2,1)} %param.31) | copy-start | bytes 3076
  7.2 15.6 %copy-start.35 = (bf16[512]{0:T(512)(128)(2,1)S(1)}, bf16[512]{0:T(512)(128)(2,1)}, u32[]{:S(2)}) copy-start(bf16[512]{0:T(512)(128)(2,1)} %param.32) | copy-start | bytes 3076
  7.3 15.6 %copy-start.36 = (bf16[512]{0:T(512)(128)(2,1)S(1)}, bf16[512]{0:T(512)(128)(2,1)}, u32[]{:S(2)}) copy-start(bf16[512]{0:T(512)(128)(2,1)} %param.34) | copy-start | bytes 3076
  7.3 15.6 %copy-start.37 = (bf16[512]{0:T(512)(128)(2,1)S(1)}, bf16[512]{0:T(512)(128)(2,1)}, u32[]{:S(2)}) copy-start(bf16[512]{0:T(512)(128)(2,1)} %param.35) | copy-start | bytes 3076
  7.3 15.6 %copy-start.38 = (bf16[512]{0:T(512)(128)(2,1)S(1)}, bf16[512]{0:T(512)(128)(2,1)}, u32[]{:S(2)}) copy-start(bf16[512]{0:T(512)(128)(2,1)} %param.37) | copy-start | bytes 3076
  7.3 15.6 %copy-start.39 = (bf16[512]{0:T(512)(128)(2,1)S(1)}, bf16[512]{0:T(512)(128)(2,1)}, u32[]{:S(2)}) copy-start(bf16[512]{0:T(512)(128)(2,1)} %param.38) | copy-start | bytes 3076
  7.3 15.7 %copy-start.40 = (bf16[512]{0:T(512)(128)(2,1)S(1)}, bf16[512]{0:T(512)(128)(2,1)}, u32[]{:S(2)}) copy-start(bf16[512]{0:T(512)(128)(2,1)} %param.39) | copy-start | bytes 3076
  7.3 15.7 %copy-start.41 = (bf16[512]{0:T(512)(128)(2,1)S(1)}, bf16[512]{0:T(512)(128)(2,1)}, u32[]{:S(2)}) copy-start(bf16[512]{0:T(512)(128)(2,1)} %param.43) | copy-start | bytes 3076
  7.3 15.8 %copy-start.30 = (bf16[2048]{0:T(1024)(128)(2,1)S(1)}, bf16[2048]{0:T(1024)(128)(2,1)}, u32[]{:S(2)}) copy-start(bf16[2048]{0:T(1024)(128)(2,1)} %param.41) | copy-start | bytes 12292
  12.2 23.4 %all-to-all-start = ((bf16[16,40,768]{2,1,0:T(8,128)(2,1)}), bf16[16,40,768]{2,1,0:T(8,128)(2,1)S(1)}, u32[]{:S(2)}, u32[]{:S(2)}) async-start(bf16[16,40,768]{2,1,0:T(8,128)(2,1)} %bitcast.2), calls=%async_computation | async-start | bytes 1966080 | tf_op jit(solution)/shard_map/all_to_all | solution.py:569
  35.5 1.4 copy-start.5
  40.5 13.7 %copy-start = (bf16[4,1,24,8,512]{4,3,2,1,0:T(8,128)(2,1)S(1)}, bf16[4,1,24,8,512]{4,3,2,1,0:T(8,128)(2,1)}, u32[]{:S(2)}) copy-start(bf16[4,1,24,8,512]{4,3,2,1,0:T(8,128)(2,1)} %param.27) | copy-start | bytes 2359300
  40.5 13.7 %copy-start.4 = (bf16[2048,512]{1,0:T(8,128)(2,1)S(1)}, bf16[2048,512]{1,0:T(8,128)(2,1)}, u32[]{:S(2)}) copy-start(bf16[2048,512]{1,0:T(8,128)(2,1)} %down_w.3) | copy-start | bytes 6291460
  45.9 10.1 %copy-start.14 = (f32[768,1]{1,0:T(8,128)}, f32[768,1]{1,0:T(8,128)S(1)}, u32[]{:S(2)}) copy-start(f32[768,1]{1,0:T(8,128)S(1)} %get-tuple-element.95.seen) | copy-start | bytes 9220
  46.0 10.1 %copy-start.16 = (s32[640,1]{1,0:T(8,128)}, s32[640,1]{1,0:T(8,128)S(1)}, u32[]{:S(2)}) copy-start(s32[640,1]{1,0:T(8,128)S(1)} %get-tuple-element.102.cell) | copy-start | bytes 7684
  46.0 17.1 %copy-start.7 = (f32[768,512]{1,0:T(8,128)}, f32[768,512]{1,0:T(8,128)S(1)}, u32[]{:S(2)}) copy-start(f32[768,512]{1,0:T(8,128)S(1)} %get-tuple-element.69.hidden) | copy-start | bytes 4718596
  46.0 10.1 %collective-permute-start = (bf16[4,16,1024]{2,1,0:T(8,128)(2,1)S(1)}, bf16[4,16,1024]{2,1,0:T(8,128)(2,1)S(1)}, u32[]{:S(2)}, u32[]{:S(2)}) collective-permute-start(bf16[4,16,1024]{2,1,0:T(8,128)(2,1)S(1)} %get-tuple-element.71), channel_id=1, source_target_pairs={{0,1},{1,2},{2,3},{3,4},{4,5},{5,6},{6,7},{8,9},{9,10},{10,11},{11... | collective-permute-start | bytes 393224 | tf_op jit(solution)/shard_map/ppermute | solution.py:607
  52.0 6.3 %collective-permute-start.1 = (bf16[4,16,1024]{2,1,0:T(8,128)(2,1)S(1)}, bf16[4,16,1024]{2,1,0:T(8,128)(2,1)S(1)}, u32[]{:S(2)}, u32[]{:S(2)}) collective-permute-start(bf16[4,16,1024]{2,1,0:T(8,128)(2,1)S(1)} %get-tuple-element.72), channel_id=1, source_target_pairs={{1,0},{2,1},{3,2},{4,3},{5,4},{6,5},{7,6},{9,8},{10,9},{11,10},{12... | collective-permute-start | bytes 393224 | tf_op jit(solution)/shard_map/ppermute | solution.py:608
  54.2 4.2 %copy-start.20 = (bf16[16,128]{1,0:T(8,128)(2,1)S(1)}, bf16[16,128]{1,0:T(8,128)(2,1)}, u32[]{:S(2)}) copy-start(bf16[16,128]{1,0:T(8,128)(2,1)} %constant.52.clone.heads_i) | copy-start | bytes 12292
  56.0 7.0 %copy-start.22 = (bf16[512,2048]{1,0:T(8,128)(2,1)S(1)}, bf16[512,2048]{1,0:T(8,128)(2,1)}, u32[]{:S(2)}) copy-start(bf16[512,2048]{1,0:T(8,128)(2,1)} %up_w.3) | copy-start | bytes 6291460
  56.0 7.0 %copy-start.23 = (bf16[512,512]{1,0:T(8,128)(2,1)S(1)}, bf16[512,512]{1,0:T(8,128)(2,1)}, u32[]{:S(2)}) copy-start(bf16[512,512]{1,0:T(8,128)(2,1)} %out_w.3) | copy-start | bytes 1572868
  73.6 15.3 %collective-permute-start.2 = (bf16[2048,512]{1,0:T(8,128)(2,1)S(1)}, bf16[2048,512]{1,0:T(8,128)(2,1)S(1)}, u32[]{:S(2)}, u32[]{:S(2)}) collective-permute-start(bf16[2048,512]{1,0:T(8,128)(2,1)S(1)} %get-tuple-element.80), channel_id=1, source_target_pairs={{0,1},{1,0},{2,3},{3,2},{4,5},{5,4},{6,7},{7,6},{8,9},{9,8},{10,11... | collective-permute-start | bytes 6291464 | tf_op jit(solution)/shard_map/ppermute | solution.py:629
  79.8 5.8 %copy-start.9 = (f32[768,512]{1,0:T(8,128)}, f32[768,512]{1,0:T(8,128)S(1)}, u32[]{:S(2)}) copy-start(f32[768,512]{1,0:T(8,128)S(1)} %get-tuple-element.96.gmid) | copy-start | bytes 4718596
  85.7 1.4 copy-start.1
  87.1 1.8 copy-start.24
  87.1 1.9 copy-start.25
  90.9 35.2 %all-to-all-start.1 = ((bf16[64,32,512]{2,1,0:T(8,128)(2,1)}), bf16[64,32,512]{2,1,0:T(8,128)(2,1)}, u32[]{:S(2)}, u32[]{:S(2)}) async-start(bf16[64,32,512]{2,1,0:T(8,128)(2,1)} %bitcast.48), calls=%async_computation.1 | async-start | bytes 4194304 | tf_op jit(solution)/shard_map/all_to_all | solution.py:545
  97.5 31.1 %copy-start.15 = (f32[768,1]{1,0:T(8,128)S(1)}, f32[768,1]{1,0:T(8,128)}, u32[]{:S(2)}) copy-start(f32[768,1]{1,0:T(8,128)} %copy-done.14) | copy-start | bytes 9220
  97.5 31.1 %collective-permute-start.3 = (bf16[4,16,1024]{2,1,0:T(8,128)(2,1)}, bf16[4,16,1024]{2,1,0:T(8,128)(2,1)}, u32[]{:S(2)}, u32[]{:S(2)}) collective-permute-start(bf16[4,16,1024]{2,1,0:T(8,128)(2,1)} %copy-done.25), channel_id=1, source_target_pairs={{0,1},{1,2},{2,3},{3,4},{4,5},{5,6},{6,7},{8,9},{9,10},{10,11},{11... | collective-permute-start | bytes 393224 | tf_op jit(solution)/shard_map/ppermute | solution.py:649
  101.4 27.2 %collective-permute-start.4 = (bf16[4,16,1024]{2,1,0:T(8,128)(2,1)}, bf16[4,16,1024]{2,1,0:T(8,128)(2,1)}, u32[]{:S(2)}, u32[]{:S(2)}) collective-permute-start(bf16[4,16,1024]{2,1,0:T(8,128)(2,1)} %copy-done.24), channel_id=1, source_target_pairs={{1,0},{2,1},{3,2},{4,3},{5,4},{6,5},{7,6},{9,8},{10,9},{11,10},{12... | collective-permute-start | bytes 393224 | tf_op jit(solution)/shard_map/ppermute | solution.py:650
  128.6 1.7 copy-start.2
  130.2 1.4 copy-start.6
  131.6 1.4 copy-start.8
  133.1 1.4 copy-start.10
  134.5 7.8 %copy-start.17 = (s32[640,1]{1,0:T(8,128)S(1)}, s32[640,1]{1,0:T(8,128)}, u32[]{:S(2)}) copy-start(s32[640,1]{1,0:T(8,128)} %copy-done.16) | copy-start | bytes 7684
  139.8 5.6 %collective-permute-start.5 = (bf16[1536,512]{1,0:T(8,128)(2,1)S(1)}, bf16[1536,512]{1,0:T(8,128)(2,1)S(1)}, u32[]{:S(2)}, u32[]{:S(2)}) collective-permute-start(bf16[1536,512]{1,0:T(8,128)(2,1)S(1)} %get-tuple-element.104), channel_id=1, source_target_pairs={{0,1},{1,0},{2,3},{3,2},{4,5},{5,4},{6,7},{7,6},{8,9},{9,8},{10,11... | collective-permute-start | bytes 4718600 | tf_op jit(solution)/shard_map/ppermute | solution.py:663
  146.9 28.3 %all-to-all-start.2 = ((bf16[64,24,512]{2,1,0:T(8,128)(2,1)}), bf16[64,24,512]{2,1,0:T(8,128)(2,1)S(1)}, u32[]{:S(2)}, u32[]{:S(2)}) async-start(bf16[64,24,512]{2,1,0:T(8,128)(2,1)} %bitcast.11), calls=%async_computation.2 | async-start | bytes 3145728 | tf_op jit(solution)/shard_map/all_to_all | solution.py:545
  151.7 80.0 %all-gather.3.cloned.1.call-start = ((), (), s32[]{:S(2)}) async-start(), calls=%async_computation.5 | async-start | bytes 2129920 | tf_op jit(solution)/shard_map/all_gather | solution.py:653
  203.5 7.1 %collective-permute-start.6 = (bf16[1536,512]{1,0:T(8,128)(2,1)S(1)}, bf16[1536,512]{1,0:T(8,128)(2,1)}, u32[]{:S(2)}, u32[]{:S(2)}) collective-permute-start(bf16[1536,512]{1,0:T(8,128)(2,1)S(1)} %bitcast.38), channel_id=1, source_target_pairs={{0,1},{1,0},{2,3},{3,2},{4,5},{5,4},{6,7},{7,6},{8,9},{9,8},{10,11... | collective-permute-start | bytes 4718600 | tf_op jit(solution)/shard_map/ppermute | solution.py:677
  206.8 25.9 %copy-start.12 = (bf16[768,512]{1,0:T(8,128)(2,1)S(1)}, bf16[768,512]{1,0:T(8,128)(2,1)}, u32[]{:S(2)}) copy-start(bf16[768,512]{1,0:T(8,128)(2,1)} %embed_w.1) | copy-start | bytes 2359300
  206.8 25.9 %copy-start.19 = (s32[4,38,1]{2,1,0:T(8,128)S(1)}, s32[4,38,1]{2,1,0:T(8,128)}, u32[]{:S(2)}) copy-start(s32[4,38,1]{2,1,0:T(8,128)} %copy-done.18) | copy-start | bytes 1828
  206.8 16.2 %all-to-all-start.4 = ((bf16[16,40,512]{2,1,0:T(8,128)(2,1)}), bf16[16,40,512]{2,1,0:T(8,128)(2,1)S(1)}, u32[]{:S(2)}, u32[]{:S(2)}) async-start(bf16[16,40,512]{2,1,0:T(8,128)(2,1)} %bitcast.46), calls=%async_computation.4 | async-start | bytes 1310720 | tf_op jit(solution)/shard_map/all_to_all | solution.py:671
  231.6 5.0 %copy-start.3 = (bf16[2048,512]{1,0:T(8,128)(2,1)S(1)}, bf16[2048,512]{1,0:T(8,128)(2,1)}, u32[]{:S(2)}) copy-start(bf16[2048,512]{1,0:T(8,128)(2,1)} %all-gather.3.cloned.1.call-done.mine) | copy-start | bytes 6291460
  231.6 5.0 %collective-permute-start.7 = (bf16[2048,512]{1,0:T(8,128)(2,1)}, bf16[2048,512]{1,0:T(8,128)(2,1)S(1)}, u32[]{:S(2)}, u32[]{:S(2)}) collective-permute-start(bf16[2048,512]{1,0:T(8,128)(2,1)} %all-gather.3.cloned.1.call-done.mine), channel_id=1, source_target_pairs={{0,1},{1,0},{2,3},{3,2},{4,5},{5,4},{6,7},{7,6},{8,9},{9,8},{10,11... | collective-permute-start | bytes 6291464 | tf_op jit(solution)/shard_map/ppermute | solution.py:683
  (7 other events, 5.7 us)
Sparse Core Ops, SparseCore 0:
  155.4 76.2 all-gather.2

commit v5 on v4

--- a/solution.py
+++ b/solution.py
@@ -648,9 +648,7 @@
     chip_one, low, high = lax.optimization_barrier((chip_one, low, high))
     from_low = lax.ppermute(high, "band", forward)
     from_high = lax.ppermute(low, "band", backward)
-    total_one = total(to_all(chip_one))
-    total_one, from_low, from_high = lax.optimization_barrier((total_one, from_low, from_high))
-    mine_one = lax.all_gather(total_one, both, axis=0, axis_index_groups=halves).reshape(-1, D)
+    parts_one = to_all(chip_one)
     gm, gf, small, send = call(
         leave_kernel, "leave",
         [((ALL, 3 * D), BF16), ((ALL, D), BF16), ((16, D), F32), ((3 * D, D), BF16)],
@@ -666,6 +664,9 @@
         (core, gm, gf, small, normed, filled, gout, cell),
         smem=1, flops=2 * ALL * (2 * D * D + GOT * D),
     )
+    parts_one, returned, other = lax.optimization_barrier((parts_one, returned, other))
+    mine_one = lax.all_gather(total(parts_one), both, axis=0, axis_index_groups=halves)
+    mine_one = mine_one.reshape(-1, D)
     mine = to_all(spread(total(to_all(chip_sum(keep, other))))).reshape(-1, D)
     mine, returned = lax.optimization_barrier((mine, returned))
     came = lax.all_to_all(

time: 248 us -> 246 us (level)
  waiting for transfers between devices: 76.7 us -> 70.1 us
  starting transfers between devices: 44.6 us -> 47.4 us
    all_to_all x2, waiting for transfers between devices: 45.6 us -> 19.9 us  [to_all(): lax.all_to_all(block, both, split_axis=0, concat_axis=0, tiled=True, axis...]
    ppermute x2, waiting for transfers between devices: 0.01 us -> 18.3 us  [on_device(): from_low = lax.ppermute(high, 'band', forward)]
    all_to_all x2, starting transfers between devices: 11.3 us -> 16.2 us  [to_all(): lax.all_to_all(block, both, split_axis=0, concat_axis=0, tiled=True, axis...]
    unnamed x89 -> x91, local copies, waits for them, and re-layouts: 17 us -> 18.2 us
  transfers between devices with their start and end apart: 13 -> 13, of which waited for: 8 -> 8; matrix products, arithmetic and copies ran while one was open for 4% -> 4% of each run, Pallas kernels for 9% -> 11%
where the time goes in v5:
time: 246 us; the launch traced here: 245 us
  waiting for transfers between devices  70.1 us (28%)
  Pallas kernels  54.4 us (22%)
  starting transfers between devices  47.4 us (19%)
  blocking collectives  27.3 us (11%)
  local copies, waits for them, and re-layouts  21.3 us (9%)
  between operations  14.8 us (6%)
  other arithmetic  9.65 us (4%)
    pallas_call x13, Pallas kernels, call(): pl.pallas_call(kernel, name=name, out_shape=outs, in_specs=[pl.BlockSpec(...  54.4 us
    all_to_all x1, blocking collectives, to_all(): lax.all_to_all(block, both, split_axis=0, concat_axis=0, tiled=True, axis...  27.3 us
    all_to_all x2, waiting for transfers between devices, to_all(): lax.all_to_all(block, both, split_axis=0, concat_axis=0, tiled=True, axis...  19.9 us
    ppermute x2, waiting for transfers between devices, on_device(): from_low = lax.ppermute(high, 'band', forward)  18.3 us
    unnamed x91, local copies, waits for them, and re-layouts  18.2 us
    all_to_all x2, starting transfers between devices, to_all(): lax.all_to_all(block, both, split_axis=0, concat_axis=0, tiled=True, axis...  16.2 us
    all_to_all x1, waiting for transfers between devices, on_device(): lax.all_to_all(packed.reshape(SRC, BLK, ENC), 'clip', split_axis=0, conca...  10.4 us
    ppermute x2, starting transfers between devices, on_device(): from_low = lax.ppermute(high, 'band', forward)  9.81 us
  transfers between devices with their start and end apart: 13, of which 8 were waited for; matrix products, arithmetic and copies ran while one was open for 4% of the time, Pallas kernels for 11%

profile of v5, /device:TPU:1, one launch (start us, length us, event | category | flops | bytes accessed | tf_op | source)
XLA Modules:
  0.0 244.9 jit_solution(12471327065179284696)
XLA Ops:
  7.3 1.0 copy.47.enc
  9.1 2.5 %pack.1 = (bf16[640,768]{1,0:T(8,128)(2,1)}, s32[4,38,1]{2,1,0:T(8,128)S(1)}) custom-call(s32[1]{0:T(128)} %bitcast.1.band, s32[4,38]{1,0:T(4,128)S(1)} %copy-done.27, bf16[4,38,768]{2,1,0:T(8,128)(2,1)S(1)} %copy.47.enc), custom_call_target="tpu_custom_call" | custom-call | flops 149422080 | bytes 1217732 | tf_op jit(solution)/shard_map/pack/pallas_call | solution.py:53
  12.2 8.6 %all-to-all-start = ((bf16[16,40,768]{2,1,0:T(8,128)(2,1)}), bf16[16,40,768]{2,1,0:T(8,128)(2,1)S(1)}, u32[]{:S(2)}, u32[]{:S(2)}) async-start(bf16[16,40,768]{2,1,0:T(8,128)(2,1)} %bitcast.2), calls=%async_computation | async-start | bytes 1966080 | tf_op jit(solution)/shard_map/all_to_all | solution.py:569
  23.5 0.8 tile.10.mask
  25.2 10.4 %all-to-all-done = bf16[16,40,768]{2,1,0:T(8,128)(2,1)S(1)} async-done(((bf16[16,40,768]{2,1,0:T(8,128)(2,1)}), bf16[16,40,768]{2,1,0:T(8,128)(2,1)S(1)}, u32[]{:S(2)}, u32[]{:S(2)}) %all-to-all-start) | async-done | bytes 983072 | tf_op jit(solution)/shard_map/all_to_all | solution.py:569
  35.5 1.4 copy-done.6
  36.9 1.1 copy-done.12
  38.8 1.0 copy-done.28
  39.7 0.7 copy-done.29
  40.5 5.5 %enter.1 = (f32[768,512]{1,0:T(8,128)S(1)}, bf16[768,512]{1,0:T(8,128)(2,1)S(1)}, bf16[768,1536]{1,0:T(8,128)(2,1)S(1)}, bf16[768,768]{1,0:T(8,128)(2,1)S(1)}, f...) custom-call(s32[8,640]{1,0:T(8,128)S(1)} %copy-done.29, ...), custom_call_target="tpu_custom_call" | custom-call | flops 2566914048 | bytes 9678336 | tf_op jit(solution)/shard_map/enter/pallas_call | solution.py:53
  46.0 6.1 %collective-permute-start = (bf16[4,16,1024]{2,1,0:T(8,128)(2,1)S(1)}, bf16[4,16,1024]{2,1,0:T(8,128)(2,1)S(1)}, u32[]{:S(2)}, u32[]{:S(2)}) collective-permute-start(bf16[4,16,1024]{2,1,0:T(8,128)(2,1)S(1)} %get-tuple-element.71), channel_id=1, source_target_pairs={{0,1},{1,2},{2,3},{3,4},{4,5},{5,6},{6,7},{8,9},{9,10},{10,11},{11... | collective-permute-start | bytes 393224 | tf_op jit(solution)/shard_map/ppermute | solution.py:607
  52.0 2.1 collective-permute-start.1
  54.2 1.8 before.1.g_act
  56.1 2.3 collective-permute-done.1.high
  58.3 4.7 %attend.1 = (bf16[768,512]{1,0:T(8,128)(2,1)S(1)}, f32[28,32,512]{2,1,0:T(8,128)S(1)}) custom-call(bf16[768,1536]{1,0:T(8,128)(2,1)S(1)} %get-tuple-element.70.mixed, bf16[4,16,1024]{2,1,0:T(8,128)(2,1)S(1)} %collective-permute-done.low, bf16[4,16,1024]{2,1,0:T(8,128)(2,1)S(1)} %collective-permute-done.1.high, f32[28,32,128]{2,1,0:T(8,128)S(1)} %tile.10.mask, ...), custom_call_target="tpu_custom_call" | custom-call | flops 117440512 | bytes 5705728 | tf_op jit(solution)/shard_map/attend/pallas_call | solution.py:53
  63.1 10.6 %mlp.1 = (f32[768,512]{1,0:T(8,128)S(1)}, bf16[768,2048]{1,0:T(8,128)(2,1)S(1)}, bf16[768,2048]{1,0:T(8,128)(2,1)S(1)}, bf16[512,768]{1,0:T(8,128)(2,1)S(1)}, bf16[2048,512]{1,0:T(8,128)(2,1)S(1)}) custom-call(s32[1]{0:T(128)} %bitcast.core, f32[768,512]{1,0:T(8,128)S(1)} %get-tuple-element.69.hidden, bf16[768,512]{1,0:T(8,128)(2,1)S(1)} %get-tuple-element.73.attended, ...), custom_call_target="tpu_custom_call" | custom-call | flops 3623878656 | bytes 22831108 | tf_op jit(solution)/shard_map/mlp/pallas_call | solution.py:53
  73.7 6.1 %mlp_back.1 = (bf16[768,512]{1,0:T(8,128)(2,1)}, f32[768,512]{1,0:T(8,128)S(1)}, bf16[768,512]{1,0:T(8,128)(2,1)S(1)}, bf16[512,512]{1,0:T(8,128)(2,1)S(1)}, f32[8,512]{1,0:T(8,128)S(1)}) custom-call(f32[768,512]{1,0:T(8,128)S(1)} %get-tuple-element.74.middle_i, bf16[768,512]{1,0:T(8,128)(2,1)S(1)} %get-tuple-element.73.attended, ...), custom_call_target="tpu_custom_call" | custom-call | flops 4026531840 | bytes 17858560 | tf_op jit(solution)/shard_map/mlp_back/pallas_call | solution.py:53
  79.9 5.8 %attend_back.1 = (bf16[768,1536]{1,0:T(8,128)(2,1)S(1)}, bf16[4,16,1024]{2,1,0:T(8,128)(2,1)S(1)}, bf16[4,16,1024]{2,1,0:T(8,128)(2,1)S(1)}, f32[4,2,16,1024]{3,2,1,0:T(8,128)S(1)}) custom-call(bf16[768,1536]{1,0:T(8,128)(2,1)S(1)} %get-tuple-element.70.mixed, bf16[4,16,1024]{2,1,0:T(8,128)(2,1)S(1)} %collective-permute-done.low, ...), custom_call_target="tpu_custom_call" | custom-call | flops 469762048 | bytes 8392704 | tf_op jit(solution)/shard_map/attend_back/pallas_call | solution.py:53
  85.7 1.4 copy-done.1
  87.1 1.8 mlp_keep.1
  89.0 1.9 add_convert_fusion
  90.9 6.7 %all-to-all-start.1 = ((bf16[64,32,512]{2,1,0:T(8,128)(2,1)}), bf16[64,32,512]{2,1,0:T(8,128)(2,1)}, u32[]{:S(2)}, u32[]{:S(2)}) async-start(bf16[64,32,512]{2,1,0:T(8,128)(2,1)} %bitcast.48), calls=%async_computation.1 | async-start | bytes 4194304 | tf_op jit(solution)/shard_map/all_to_all | solution.py:545
  97.6 3.8 %collective-permute-start.3 = (bf16[4,16,1024]{2,1,0:T(8,128)(2,1)}, bf16[4,16,1024]{2,1,0:T(8,128)(2,1)S(1)}, u32[]{:S(2)}, u32[]{:S(2)}) collective-permute-start(bf16[4,16,1024]{2,1,0:T(8,128)(2,1)} %copy-done.26), channel_id=1, source_target_pairs={{0,1},{1,2},{2,3},{3,4},{4,5},{5,6},{6,7},{8,9},{9,10},{10,11},{11... | collective-permute-start | bytes 393224 | tf_op jit(solution)/shard_map/ppermute | solution.py:649
  101.4 1.9 collective-permute-start.4
  103.3 18.3 %collective-permute-done.3.from_low = bf16[4,16,1024]{2,1,0:T(8,128)(2,1)S(1)} collective-permute-done((bf16[4,16,1024]{2,1,0:T(8,128)(2,1)}, bf16[4,16,1024]{2,1,0:T(8,128)(2,1)S(1)}, u32[]{:S(2)}, u32[]{:S(2)}) %collective-permute-start.3) | collective-permute-done | bytes 131104 | tf_op jit(solution)/shard_map/ppermute | solution.py:649
  121.5 1.9 collective-permute-done.4.from_high
  123.4 1.7 copy-done.2
  125.1 1.4 copy-done.7
  126.5 1.4 copy-done.9
  127.9 1.4 copy-done.11
  129.3 4.2 %leave.1 = (bf16[768,1536]{1,0:T(8,128)(2,1)S(1)}, bf16[768,512]{1,0:T(8,128)(2,1)S(1)}, f32[16,512]{1,0:T(8,128)S(1)}, bf16[1536,512]{1,0:T(8,128)(2,1)S(1)}) custom-call(s32[1]{0:T(128)} %bitcast.core, bf16[768,1536]{1,0:T(8,128)(2,1)S(1)} %copy-done.2, bf16[4,16,1024]{2,1,0:T(8,128)(2,1)S(1)} %collective-permute-done.3.from_low, ...), custom_call_target="tpu_custom_call" | custom-call | flops 2013265920 | bytes 15141892 | tf_op jit(solution)/shard_map/leave/pallas_call | solution.py:53
  133.7 1.6 leave_keep.1
  135.3 1.1 copy-done.5
  136.4 0.8 copy-done.14
  137.3 3.5 %add_convert_fusion.1 = bf16[1536,512]{1,0:T(8,128)(2,1)} fusion(bf16[1536,512]{1,0:T(8,128)(2,1)} %collective-permute-done.5, bf16[1536,512]{1,0:T(8,128)(2,1)} %copy-done.5), kind=kLoop, calls=%fused_computation.1 | loop fusion | flops 3145728 | bytes 4718592 | tf_op jit(solution)/shard_map/convert_element_type | solution.py:550
  140.7 9.5 %all-to-all-start.2 = ((bf16[64,24,512]{2,1,0:T(8,128)(2,1)}), bf16[64,24,512]{2,1,0:T(8,128)(2,1)S(1)}, u32[]{:S(2)}, u32[]{:S(2)}) async-start(bf16[64,24,512]{2,1,0:T(8,128)(2,1)} %bitcast.11), calls=%async_computation.2 | async-start | bytes 3145728 | tf_op jit(solution)/shard_map/all_to_all | solution.py:545
  150.3 2.5 %reduce_sum.24 = bf16[32,512]{1,0:T(8,128)(2,1)} reduce(bf16[64,32,512]{2,1,0:T(8,128)(2,1)} %all-to-all-done.1, bf16[]{:T(256)} %constant.47.clone.1), dimensions={0}, to_apply=%region_0.1 | reduce | flops 1032192 | bytes 2129922 | tf_op jit(solution)/shard_map/reduce_sum | solution.py:554
  152.8 19.9 %all-to-all-done.2 = bf16[64,24,512]{2,1,0:T(8,128)(2,1)S(1)} async-done(((bf16[64,24,512]{2,1,0:T(8,128)(2,1)}), bf16[64,24,512]{2,1,0:T(8,128)(2,1)S(1)}, u32[]{:S(2)}, u32[]{:S(2)}) %all-to-all-start.2) | async-done | bytes 1572896 | tf_op jit(solution)/shard_map/all_to_all | solution.py:545
  173.1 27.3 %all_to_all.25 = bf16[64,24,512]{2,1,0:T(8,128)(2,1)S(1)} all-to-all(bf16[64,24,512]{2,1,0:T(8,128)(2,1)S(1)} %broadcast_in_dim.74), channel_id=1, replica_groups={{0,2,4,6,8,10,12,14,16,18,20,22,24,26,28,30,32,34,36,38,40,42,44,46,48,..., dimensions={0} | all-to-all | bytes 3145728 | tf_op jit(solution)/shard_map/all_to_all | solution.py:545
  200.4 3.8 %collective-permute-start.6 = (bf16[1536,512]{1,0:T(8,128)(2,1)S(1)}, bf16[1536,512]{1,0:T(8,128)(2,1)}, u32[]{:S(2)}, u32[]{:S(2)}) collective-permute-start(bf16[1536,512]{1,0:T(8,128)(2,1)S(1)} %bitcast.38), channel_id=1, source_target_pairs={{0,1},{1,0},{2,3},{3,2},{4,5},{5,4},{6,7},{7,6},{8,9},{9,8},{10,11... | collective-permute-start | bytes 4718600 | tf_op jit(solution)/shard_map/ppermute | solution.py:678
  204.2 3.7 %all-to-all-start.4 = ((bf16[16,40,512]{2,1,0:T(8,128)(2,1)}), bf16[16,40,512]{2,1,0:T(8,128)(2,1)S(1)}, u32[]{:S(2)}, u32[]{:S(2)}) async-start(bf16[16,40,512]{2,1,0:T(8,128)(2,1)} %bitcast.46), calls=%async_computation.4 | async-start | bytes 1310720 | tf_op jit(solution)/shard_map/all_to_all | solution.py:672
  207.9 4.3 %unpack_two.1 = (f32[512,1536]{1,0:T(8,128)}, f32[768,512]{1,0:T(8,128)}, f32[512,512]{1,0:T(8,128)}, f32[16,512]{1,0:T(8,128)S(1)}) custom-call(s32[1]{0:T(128)} %bitcast.core, bf16[1536,512]{1,0:T(8,128)(2,1)S(1)} %bitcast.39, bf16[1536,512]{1,0:T(8,128)(2,1)} %collective-permute-done.6.other), custom_call_target="tpu_custom_call" | custom-call | bytes 8945668 | tf_op jit(solution)/shard_map/unpack_two/pallas_call | solution.py:53
  212.2 8.2 %all-to-all-done.4 = bf16[16,40,512]{2,1,0:T(8,128)(2,1)S(1)} async-done(((bf16[16,40,512]{2,1,0:T(8,128)(2,1)}), bf16[16,40,512]{2,1,0:T(8,128)(2,1)S(1)}, u32[]{:S(2)}, u32[]{:S(2)}) %all-to-all-start.4) | async-done | bytes 655392 | tf_op jit(solution)/shard_map/all_to_all | solution.py:672
  220.4 8.8 %all-gather.3.cloned.1.call-done.mine = bf16[2048,512]{1,0:T(8,128)(2,1)} async-done(((bf16[32,512]{1,0:T(8,128)(2,1)}), bf16[2048,512]{1,0:T(8,128)(2,1)}) %all-gather.3.cloned.1.call-update) | async-done | bytes 2097168 | tf_op jit(solution)/shard_map/all_gather | solution.py:668
  229.2 1.0 collective-permute-start.7
  230.2 1.5 return.1
  231.8 0.8 copy.53
  234.2 3.9 %unpack_one.1 = (f32[2048,512]{1,0:T(8,128)}, f32[512,2048]{1,0:T(8,128)}) custom-call(s32[1]{0:T(128)} %bitcast.core, bf16[2048,512]{1,0:T(8,128)(2,1)S(1)} %copy-done.3, bf16[2048,512]{1,0:T(8,128)(2,1)S(1)} %collective-permute-done.7.other), custom_call_target="tpu_custom_call" | custom-call | bytes 12582916 | tf_op jit(solution)/shard_map/unpack_one/pallas_call | solution.py:53
  (142 shorter events, 7.7 us)
Async XLA Ops:
  7.2 14.7 %copy-start.30 = (pred[32,32]{1,0:T(32,128)(4,1)S(1)}, pred[32,32]{1,0:T(32,128)(4,1)}, u32[]{:S(2)}) copy-start(pred[32,32]{1,0:T(32,128)(4,1)} %constant.53.clone) | copy-start | bytes 3076
  7.2 13.7 %copy-start.32 = (s32[4,1,3]{0,1,2:T(1,128)S(1)}, s32[4,1,3]{0,1,2:T(1,128)}, u32[]{:S(2)}) copy-start(s32[4,1,3]{0,1,2:T(1,128)} %param.26) | copy-start | bytes 148
  7.2 15.6 %copy-start.33 = (bf16[512]{0:T(512)(128)(2,1)S(1)}, bf16[512]{0:T(512)(128)(2,1)}, u32[]{:S(2)}) copy-start(bf16[512]{0:T(512)(128)(2,1)} %param.29) | copy-start | bytes 3076
  7.2 15.6 %copy-start.34 = (bf16[512]{0:T(512)(128)(2,1)S(1)}, bf16[512]{0:T(512)(128)(2,1)}, u32[]{:S(2)}) copy-start(bf16[512]{0:T(512)(128)(2,1)} %param.30) | copy-start | bytes 3076
  7.2 15.6 %copy-start.35 = (bf16[512]{0:T(512)(128)(2,1)S(1)}, bf16[512]{0:T(512)(128)(2,1)}, u32[]{:S(2)}) copy-start(bf16[512]{0:T(512)(128)(2,1)} %param.31) | copy-start | bytes 3076
  7.2 15.6 %copy-start.36 = (bf16[512]{0:T(512)(128)(2,1)S(1)}, bf16[512]{0:T(512)(128)(2,1)}, u32[]{:S(2)}) copy-start(bf16[512]{0:T(512)(128)(2,1)} %param.32) | copy-start | bytes 3076
  7.3 15.6 %copy-start.37 = (bf16[512]{0:T(512)(128)(2,1)S(1)}, bf16[512]{0:T(512)(128)(2,1)}, u32[]{:S(2)}) copy-start(bf16[512]{0:T(512)(128)(2,1)} %param.34) | copy-start | bytes 3076
  7.3 15.6 %copy-start.38 = (bf16[512]{0:T(512)(128)(2,1)S(1)}, bf16[512]{0:T(512)(128)(2,1)}, u32[]{:S(2)}) copy-start(bf16[512]{0:T(512)(128)(2,1)} %param.35) | copy-start | bytes 3076
  7.3 15.6 %copy-start.39 = (bf16[512]{0:T(512)(128)(2,1)S(1)}, bf16[512]{0:T(512)(128)(2,1)}, u32[]{:S(2)}) copy-start(bf16[512]{0:T(512)(128)(2,1)} %param.37) | copy-start | bytes 3076
  7.3 15.7 %copy-start.40 = (bf16[512]{0:T(512)(128)(2,1)S(1)}, bf16[512]{0:T(512)(128)(2,1)}, u32[]{:S(2)}) copy-start(bf16[512]{0:T(512)(128)(2,1)} %param.38) | copy-start | bytes 3076
  7.3 15.7 %copy-start.41 = (bf16[512]{0:T(512)(128)(2,1)S(1)}, bf16[512]{0:T(512)(128)(2,1)}, u32[]{:S(2)}) copy-start(bf16[512]{0:T(512)(128)(2,1)} %param.39) | copy-start | bytes 3076
  7.3 15.7 %copy-start.42 = (bf16[512]{0:T(512)(128)(2,1)S(1)}, bf16[512]{0:T(512)(128)(2,1)}, u32[]{:S(2)}) copy-start(bf16[512]{0:T(512)(128)(2,1)} %param.43) | copy-start | bytes 3076
  7.3 15.8 %copy-start.31 = (bf16[2048]{0:T(1024)(128)(2,1)S(1)}, bf16[2048]{0:T(1024)(128)(2,1)}, u32[]{:S(2)}) copy-start(bf16[2048]{0:T(1024)(128)(2,1)} %param.41) | copy-start | bytes 12292
  12.2 23.4 %all-to-all-start = ((bf16[16,40,768]{2,1,0:T(8,128)(2,1)}), bf16[16,40,768]{2,1,0:T(8,128)(2,1)S(1)}, u32[]{:S(2)}, u32[]{:S(2)}) async-start(bf16[16,40,768]{2,1,0:T(8,128)(2,1)} %bitcast.2), calls=%async_computation | async-start | bytes 1966080 | tf_op jit(solution)/shard_map/all_to_all | solution.py:569
  35.5 1.4 copy-start.6
  40.5 13.7 %copy-start = (bf16[4,1,24,8,512]{4,3,2,1,0:T(8,128)(2,1)S(1)}, bf16[4,1,24,8,512]{4,3,2,1,0:T(8,128)(2,1)}, u32[]{:S(2)}) copy-start(bf16[4,1,24,8,512]{4,3,2,1,0:T(8,128)(2,1)} %param.27) | copy-start | bytes 2359300
  40.5 13.7 %copy-start.4 = (bf16[2048,512]{1,0:T(8,128)(2,1)S(1)}, bf16[2048,512]{1,0:T(8,128)(2,1)}, u32[]{:S(2)}) copy-start(bf16[2048,512]{1,0:T(8,128)(2,1)} %down_w.3) | copy-start | bytes 6291460
  45.9 10.1 %copy-start.15 = (f32[768,1]{1,0:T(8,128)}, f32[768,1]{1,0:T(8,128)S(1)}, u32[]{:S(2)}) copy-start(f32[768,1]{1,0:T(8,128)S(1)} %get-tuple-element.92.seen) | copy-start | bytes 9220
  46.0 10.1 %copy-start.17 = (s32[640,1]{1,0:T(8,128)}, s32[640,1]{1,0:T(8,128)S(1)}, u32[]{:S(2)}) copy-start(s32[640,1]{1,0:T(8,128)S(1)} %get-tuple-element.99.cell) | copy-start | bytes 7684
  46.0 17.1 %copy-start.8 = (f32[768,512]{1,0:T(8,128)}, f32[768,512]{1,0:T(8,128)S(1)}, u32[]{:S(2)}) copy-start(f32[768,512]{1,0:T(8,128)S(1)} %get-tuple-element.69.hidden) | copy-start | bytes 4718596
  46.0 10.1 %collective-permute-start = (bf16[4,16,1024]{2,1,0:T(8,128)(2,1)S(1)}, bf16[4,16,1024]{2,1,0:T(8,128)(2,1)S(1)}, u32[]{:S(2)}, u32[]{:S(2)}) collective-permute-start(bf16[4,16,1024]{2,1,0:T(8,128)(2,1)S(1)} %get-tuple-element.71), channel_id=1, source_target_pairs={{0,1},{1,2},{2,3},{3,4},{4,5},{5,6},{6,7},{8,9},{9,10},{10,11},{11... | collective-permute-start | bytes 393224 | tf_op jit(solution)/shard_map/ppermute | solution.py:607
  52.0 6.3 %collective-permute-start.1 = (bf16[4,16,1024]{2,1,0:T(8,128)(2,1)S(1)}, bf16[4,16,1024]{2,1,0:T(8,128)(2,1)S(1)}, u32[]{:S(2)}, u32[]{:S(2)}) collective-permute-start(bf16[4,16,1024]{2,1,0:T(8,128)(2,1)S(1)} %get-tuple-element.72), channel_id=1, source_target_pairs={{1,0},{2,1},{3,2},{4,3},{5,4},{6,5},{7,6},{9,8},{10,9},{11,10},{12... | collective-permute-start | bytes 393224 | tf_op jit(solution)/shard_map/ppermute | solution.py:608
  54.2 4.2 %copy-start.21 = (bf16[16,128]{1,0:T(8,128)(2,1)S(1)}, bf16[16,128]{1,0:T(8,128)(2,1)}, u32[]{:S(2)}) copy-start(bf16[16,128]{1,0:T(8,128)(2,1)} %constant.52.clone.heads_i) | copy-start | bytes 12292
  56.0 7.1 %copy-start.23 = (bf16[512,2048]{1,0:T(8,128)(2,1)S(1)}, bf16[512,2048]{1,0:T(8,128)(2,1)}, u32[]{:S(2)}) copy-start(bf16[512,2048]{1,0:T(8,128)(2,1)} %up_w.3) | copy-start | bytes 6291460
  56.0 7.1 %copy-start.24 = (bf16[512,512]{1,0:T(8,128)(2,1)S(1)}, bf16[512,512]{1,0:T(8,128)(2,1)}, u32[]{:S(2)}) copy-start(bf16[512,512]{1,0:T(8,128)(2,1)} %out_w.3) | copy-start | bytes 1572868
  73.7 15.3 %collective-permute-start.2 = (bf16[2048,512]{1,0:T(8,128)(2,1)S(1)}, bf16[2048,512]{1,0:T(8,128)(2,1)S(1)}, u32[]{:S(2)}, u32[]{:S(2)}) collective-permute-start(bf16[2048,512]{1,0:T(8,128)(2,1)S(1)} %get-tuple-element.80), channel_id=1, source_target_pairs={{0,1},{1,0},{2,3},{3,2},{4,5},{5,4},{6,7},{7,6},{8,9},{9,8},{10,11... | collective-permute-start | bytes 6291464 | tf_op jit(solution)/shard_map/ppermute | solution.py:629
  79.9 5.8 %copy-start.10 = (f32[768,512]{1,0:T(8,128)}, f32[768,512]{1,0:T(8,128)S(1)}, u32[]{:S(2)}) copy-start(f32[768,512]{1,0:T(8,128)S(1)} %get-tuple-element.93.gmid) | copy-start | bytes 4718596
  85.7 1.4 copy-start.1
  87.1 1.8 copy-start.25
  87.1 1.9 copy-start.26
  90.9 32.5 %copy-start.16 = (f32[768,1]{1,0:T(8,128)S(1)}, f32[768,1]{1,0:T(8,128)}, u32[]{:S(2)}) copy-start(f32[768,1]{1,0:T(8,128)} %copy-done.15) | copy-start | bytes 9220
  90.9 46.4 %all-to-all-start.1 = ((bf16[64,32,512]{2,1,0:T(8,128)(2,1)}), bf16[64,32,512]{2,1,0:T(8,128)(2,1)}, u32[]{:S(2)}, u32[]{:S(2)}) async-start(bf16[64,32,512]{2,1,0:T(8,128)(2,1)} %bitcast.48), calls=%async_computation.1 | async-start | bytes 4194304 | tf_op jit(solution)/shard_map/all_to_all | solution.py:545
  97.6 24.0 %collective-permute-start.3 = (bf16[4,16,1024]{2,1,0:T(8,128)(2,1)}, bf16[4,16,1024]{2,1,0:T(8,128)(2,1)S(1)}, u32[]{:S(2)}, u32[]{:S(2)}) collective-permute-start(bf16[4,16,1024]{2,1,0:T(8,128)(2,1)} %copy-done.26), channel_id=1, source_target_pairs={{0,1},{1,2},{2,3},{3,4},{4,5},{5,6},{6,7},{8,9},{9,10},{10,11},{11... | collective-permute-start | bytes 393224 | tf_op jit(solution)/shard_map/ppermute | solution.py:649
  101.4 22.0 %collective-permute-start.4 = (bf16[4,16,1024]{2,1,0:T(8,128)(2,1)}, bf16[4,16,1024]{2,1,0:T(8,128)(2,1)S(1)}, u32[]{:S(2)}, u32[]{:S(2)}) collective-permute-start(bf16[4,16,1024]{2,1,0:T(8,128)(2,1)} %copy-done.25), channel_id=1, source_target_pairs={{1,0},{2,1},{3,2},{4,3},{5,4},{6,5},{7,6},{9,8},{10,9},{11,10},{12... | collective-permute-start | bytes 393224 | tf_op jit(solution)/shard_map/ppermute | solution.py:650
  123.4 1.7 copy-start.2
  125.1 1.4 copy-start.7
  126.5 1.4 copy-start.9
  127.9 1.4 copy-start.11
  129.3 4.4 %copy-start.18 = (s32[640,1]{1,0:T(8,128)S(1)}, s32[640,1]{1,0:T(8,128)}, u32[]{:S(2)}) copy-start(s32[640,1]{1,0:T(8,128)} %copy-done.17) | copy-start | bytes 7684
  133.6 3.7 %collective-permute-start.5 = (bf16[1536,512]{1,0:T(8,128)(2,1)S(1)}, bf16[1536,512]{1,0:T(8,128)(2,1)}, u32[]{:S(2)}, u32[]{:S(2)}) collective-permute-start(bf16[1536,512]{1,0:T(8,128)(2,1)S(1)} %get-tuple-element.101), channel_id=1, source_target_pairs={{0,1},{1,0},{2,3},{3,2},{4,5},{5,4},{6,7},{7,6},{8,9},{9,8},{10,11... | collective-permute-start | bytes 4718600 | tf_op jit(solution)/shard_map/ppermute | solution.py:661
  140.7 32.0 %all-to-all-start.2 = ((bf16[64,24,512]{2,1,0:T(8,128)(2,1)}), bf16[64,24,512]{2,1,0:T(8,128)(2,1)S(1)}, u32[]{:S(2)}, u32[]{:S(2)}) async-start(bf16[64,24,512]{2,1,0:T(8,128)(2,1)} %bitcast.11), calls=%async_computation.2 | async-start | bytes 3145728 | tf_op jit(solution)/shard_map/all_to_all | solution.py:545
  150.2 79.0 %all-gather.3.cloned.1.call-start = ((), (), s32[]{:S(2)}) async-start(), calls=%async_computation.5 | async-start | bytes 2129920 | tf_op jit(solution)/shard_map/all_gather | solution.py:668
  200.4 7.5 %collective-permute-start.6 = (bf16[1536,512]{1,0:T(8,128)(2,1)S(1)}, bf16[1536,512]{1,0:T(8,128)(2,1)}, u32[]{:S(2)}, u32[]{:S(2)}) collective-permute-start(bf16[1536,512]{1,0:T(8,128)(2,1)S(1)} %bitcast.38), channel_id=1, source_target_pairs={{0,1},{1,0},{2,3},{3,2},{4,5},{5,4},{6,7},{7,6},{8,9},{9,8},{10,11... | collective-permute-start | bytes 4718600 | tf_op jit(solution)/shard_map/ppermute | solution.py:678
  204.2 26.1 %copy-start.13 = (bf16[768,512]{1,0:T(8,128)(2,1)S(1)}, bf16[768,512]{1,0:T(8,128)(2,1)}, u32[]{:S(2)}) copy-start(bf16[768,512]{1,0:T(8,128)(2,1)} %embed_w.1) | copy-start | bytes 2359300
  204.2 26.1 %copy-start.20 = (s32[4,38,1]{2,1,0:T(8,128)S(1)}, s32[4,38,1]{2,1,0:T(8,128)}, u32[]{:S(2)}) copy-start(s32[4,38,1]{2,1,0:T(8,128)} %copy-done.19) | copy-start | bytes 1828
  204.2 16.2 %all-to-all-start.4 = ((bf16[16,40,512]{2,1,0:T(8,128)(2,1)}), bf16[16,40,512]{2,1,0:T(8,128)(2,1)S(1)}, u32[]{:S(2)}, u32[]{:S(2)}) async-start(bf16[16,40,512]{2,1,0:T(8,128)(2,1)} %bitcast.46), calls=%async_computation.4 | async-start | bytes 1310720 | tf_op jit(solution)/shard_map/all_to_all | solution.py:672
  229.2 5.0 %copy-start.3 = (bf16[2048,512]{1,0:T(8,128)(2,1)S(1)}, bf16[2048,512]{1,0:T(8,128)(2,1)}, u32[]{:S(2)}) copy-start(bf16[2048,512]{1,0:T(8,128)(2,1)} %all-gather.3.cloned.1.call-done.mine) | copy-start | bytes 6291460
  229.2 5.0 %collective-permute-start.7 = (bf16[2048,512]{1,0:T(8,128)(2,1)}, bf16[2048,512]{1,0:T(8,128)(2,1)S(1)}, u32[]{:S(2)}, u32[]{:S(2)}) collective-permute-start(bf16[2048,512]{1,0:T(8,128)(2,1)} %all-gather.3.cloned.1.call-done.mine), channel_id=1, source_target_pairs={{0,1},{1,0},{2,3},{3,2},{4,5},{5,4},{6,7},{7,6},{8,9},{9,8},{10,11... | collective-permute-start | bytes 6291464 | tf_op jit(solution)/shard_map/ppermute | solution.py:684
  (8 other events, 6.8 us)
Sparse Core Ops, SparseCore 0:
  154.5 74.6 all-gather.2
